TPU v7x, 128 devices: a whole 4x4x4 slice. The times are simulated.
128 devices in a mesh: dp: 8 (over x, core), tensor: 16 (over z, y).
Axes of the slice: x: 4, y: 4, z: 4, core: 2. Of those that a mesh axis runs over, the one named last changes fastest.
Arguments:
- hidden: bfloat16 [1024, 53248], P('dp', 'tensor'), may hold values from -6 to 6
- out_grad: bfloat16 [1024, 8192], P('dp'), may hold values from -4 to 4
- weight: bfloat16 [53248, 8192], P('tensor', 'dp'), may hold values from -0.02734375 to 0.02734375
- inv_scale: float32 [8192], P('dp'), may hold values from 392.28397 to 1199.9275
Outputs:
- hidden_grad: bfloat16 [1024, 53248], P('dp', 'tensor')
- weight_grad: bfloat16 [53248, 8192], P('tensor', 'dp')
All inputs are finite; a program needn't handle non-finite values.
Results may differ from a plain program's by a relative error of at most 0.02.
Values may be sent and summed in bfloat16 or wider, within the bound.
No kernel may reach another device: no remote copies, remote signals or barrier semaphores. Data moves between devices by JAX's collectives and lax.ppermute only.
A program may use at most 128 MiB of HBM per device.

v0:
```python
import math

import jax
import jax.numpy as jnp
from jax import lax
from jax.sharding import PartitionSpec as P

HB = 256


def from_partner(block, axis, distance):
    count = lax.axis_size(axis)
    route = []
    for low in range(count):
        high = low | 1 << distance
        if high != low and high < count:
            route += [(low, high), (high, low)]
    return lax.ppermute(block, axis, route)


def hadamard(order_size):
    indices = jnp.arange(order_size, dtype=jnp.int32)
    parity = jnp.zeros((order_size, order_size), jnp.int32)
    bit_pos = 0
    while 1 << bit_pos < order_size:
        parity = parity + jnp.bitwise_and(
            jnp.right_shift(indices[:, None], bit_pos), 1
        ) * jnp.bitwise_and(jnp.right_shift(indices[None, :], bit_pos), 1)
        bit_pos = bit_pos + 1
    return (1 - 2 * (parity % 2)).astype(jnp.float32)


def block_rotate(values, block_table):
    dim_list = values.shape
    blocks = values.reshape(
        dim_list[:-1] + (dim_list[-1] // block_table.shape[0], block_table.shape[0])
    )
    blocks = jnp.einsum("...bk,kl->...bl", blocks, block_table, precision=lax.Precision.HIGHEST)
    return blocks.reshape(dim_list)


def butterfly(values, trade, position, bit_count):
    for bit_pos in range(bit_count):
        partner = trade(values, bit_pos)
        lower_half = jnp.bitwise_and(jnp.right_shift(position, bit_pos), 1) == 0
        values = jnp.where(lower_half, values + partner, partner - values)
    return values


def on_device(hidden, out_grad, weight, inv_scale):
    tensor_count = lax.axis_size("tensor")
    bit_count = tensor_count.bit_length() - 1
    position = lax.axis_index("tensor")
    block_table = hadamard(HB)
    scaling = 1.0 / math.sqrt(tensor_count * HB)

    def finish(mixed):
        return (block_rotate(mixed, block_table) * scaling).astype(jnp.bfloat16)

    mixed_hidden = finish(
        butterfly(
            hidden.astype(jnp.float32),
            lambda values, bit_pos: from_partner(
                values.astype(jnp.bfloat16), "tensor", bit_pos
            ).astype(values.dtype),
            position,
            bit_count,
        )
    )
    raw_code = jnp.floor(weight.astype(jnp.float32) * inv_scale[None, :] + 0.5)
    keep_mask = jnp.logical_and(raw_code >= -8.0, raw_code <= 7.0)
    quant_weight = (jnp.clip(raw_code, -8.0, 7.0) / inv_scale[None, :]).astype(jnp.bfloat16)
    grad_cols = lax.all_to_all(out_grad, "dp", split_axis=1, concat_axis=0, tiled=True)
    selected = grad_cols
    grad_mixed = lax.psum_scatter(
        lax.dot_general(
            selected, quant_weight, (((1,), (1,)), ((), ())), preferred_element_type=jnp.float32
        ).astype(jnp.bfloat16),
        "dp",
        scatter_dimension=0,
        tiled=True,
    ).astype(jnp.float32)
    selected = grad_cols
    weight_sum = lax.dot_general(
        lax.all_gather(mixed_hidden, "dp", axis=0, tiled=True),
        selected,
        (((0,), (0,)), ((), ())),
        preferred_element_type=jnp.float32,
    )
    weight_grad = jnp.where(keep_mask, weight_sum, 0.0).astype(jnp.bfloat16)
    hidden_grad = finish(
        butterfly(
            grad_mixed,
            lambda values, bit_pos: from_partner(
                values.astype(jnp.bfloat16), "tensor", bit_pos
            ).astype(values.dtype),
            position,
            bit_count,
        )
    )
    return (hidden_grad, weight_grad)


def solution(mesh):
    in_specs = (P("dp", "tensor"), P("dp", None), P("tensor", "dp"), P("dp"))
    out_specs = (P("dp", "tensor"), P("tensor", "dp"))
    return jax.shard_map(
        on_device, mesh=mesh, in_specs=in_specs, out_specs=out_specs, check_vma=False
    )
```

profile of v0, /device:TPU:0, one launch (start us, length us, event | category | flops | bytes accessed | tf_op | source)
XLA Modules:
  0.0 251.4 jit_solution(14921240197523584723)
XLA Ops:
  7.2 0.0 reduce-scatter.4.cloned.1.call-start
  7.2 4.1 %copy.26 = bf16[128,8192]{0,1:T(8,128)(2,1)} copy(bf16[128,8192]{1,0:T(8,128)(2,1)} %param.5) | data formatting | bytes 4194304 | tf_op args[1]
  11.3 31.9 %all_to_all.19 = bf16[128,8,1024]{0,2,1:T(8,128)(2,1)S(1)} all-to-all(bf16[128,8,1024]{0,2,1:T(8,128)(2,1)} %bitcast.20), channel_id=1, replica_groups=mesh['dp'=8,'tensor'=16] {'dp'}, dimensions={1} | all-to-all | bytes 4194304 | tf_op jit(solution)/shard_map/all_to_all | solution.py:73
  43.2 0.0 copy-start.1
  43.2 2.6 %copy.27 = bf16[8,128,1024]{2,1,0:T(8,128)(2,1)} copy(bf16[8,128,1024]{1,2,0:T(8,128)(2,1)S(1)} %bitcast.19) | data formatting | bytes 4194304 | tf_op jit(solution)/shard_map/all_to_all | solution.py:73
  45.8 0.0 copy-done.1
  45.8 11.9 %fusion.7 = bf16[1024,3328]{0,1:T(8,128)(2,1)} fusion(bf16[1024,1024]{1,0:T(8,128)(2,1)} %bitcast.23, bf16[3328,1024]{1,0:T(8,128)(2,1)} %param.6, f32[1024]{0:T(1024)S(1)} %copy-done.1), kind=kOutput, calls=%fused_computation.11 | convolution fusion | flops 7006584832 | bytes 15732736 | tf_op jit(solution)/shard_map/dot_general | solution.py:76
  57.8 9.7 %copy.37 = bf16[1024,3328]{1,0:T(8,128)(2,1)} copy(bf16[1024,3328]{0,1:T(8,128)(2,1)} %fusion.7) | data formatting | bytes 13631488
  67.5 0.0 copy-start
  67.5 0.0 reduce-scatter.4.cloned.1.call-update
  67.5 0.0 all-gather.2.cloned.1.call-start
  67.5 1.1 copy-done
  68.6 0.6 copy.30
  69.2 1.7 collective-permute-start.4
  70.9 18.7 %collective-permute-done.4 = bf16[128,3328]{0,1:T(8,128)(2,1)S(1)} collective-permute-done((bf16[128,3328]{0,1:T(8,128)(2,1)S(1)}, bf16[128,3328]{0,1:T(8,128)(2,1)S(1)}, u32[]{:S(2)}, u32[]{:S(2)}) %collective-permute-start.4) | collective-permute-done | bytes 852000 | tf_op jit(solution)/shard_map/ppermute | solution.py:18
  89.6 0.3 fusion.16
  90.0 3.3 %collective-permute-start.5 = (bf16[128,3328]{0,1:T(8,128)(2,1)S(1)}, bf16[128,3328]{0,1:T(8,128)(2,1)S(1)}, u32[]{:S(2)}, u32[]{:S(2)}) collective-permute-start(bf16[128,3328]{0,1:T(8,128)(2,1)S(1)} %fusion.16), channel_id=1, source_target_pairs={{0,2},{2,0},{1,3},{3,1},{4,6},{6,4},{5,7},{7,5},{8,10},{10,8},{9,1... | collective-permute-start | bytes 2555912 | tf_op jit(solution)/shard_map/ppermute | solution.py:18
  93.2 17.8 %collective-permute-done.5 = bf16[128,3328]{0,1:T(8,128)(2,1)S(1)} collective-permute-done((bf16[128,3328]{0,1:T(8,128)(2,1)S(1)}, bf16[128,3328]{0,1:T(8,128)(2,1)S(1)}, u32[]{:S(2)}, u32[]{:S(2)}) %collective-permute-start.5) | collective-permute-done | bytes 852000 | tf_op jit(solution)/shard_map/ppermute | solution.py:18
  111.1 1.5 fusion.62
  112.5 1.9 collective-permute-start.6
  114.4 17.0 %collective-permute-done.6 = bf16[128,3328]{0,1:T(8,128)(2,1)S(1)} collective-permute-done((bf16[128,3328]{0,1:T(8,128)(2,1)}, bf16[128,3328]{0,1:T(8,128)(2,1)S(1)}, u32[]{:S(2)}, u32[]{:S(2)}) %collective-permute-start.6) | collective-permute-done | bytes 852000 | tf_op jit(solution)/shard_map/ppermute | solution.py:18
  131.5 1.7 fusion.18
  133.1 3.7 %collective-permute-start.7 = (bf16[128,3328]{0,1:T(8,128)(2,1)}, bf16[128,3328]{0,1:T(8,128)(2,1)}, u32[]{:S(2)}, u32[]{:S(2)}) collective-permute-start(bf16[128,3328]{0,1:T(8,128)(2,1)} %fusion.18), channel_id=1, source_target_pairs={{0,8},{8,0},{1,9},{9,1},{2,10},{10,2},{3,11},{11,3},{4,12},{12,4},... | collective-permute-start | bytes 2555912 | tf_op jit(solution)/shard_map/ppermute | solution.py:18
  136.9 16.3 %collective-permute-done.7 = bf16[128,3328]{0,1:T(8,128)(2,1)} collective-permute-done((bf16[128,3328]{0,1:T(8,128)(2,1)}, bf16[128,3328]{0,1:T(8,128)(2,1)}, u32[]{:S(2)}, u32[]{:S(2)}) %collective-permute-start.7) | collective-permute-done | bytes 852000 | tf_op jit(solution)/shard_map/ppermute | solution.py:18
  153.1 2.1 fusion.15
  155.2 3.2 %multiply_convert_fusion = bf16[128,13,256]{2,0,1:T(8,128)(2,1)S(1)} fusion(f32[128,13,256]{0,2,1:T(8,128)S(1)} %bitcast.26, s32[256]{0:T(256)S(1)} %get-tuple-element.8, s32[256]{0:T(256)S(1)} %get-tuple-element.9, s32[256]{0:T(256)S(1)} %get-tuple-element.10, s32[256]{0:T(256)S(1)} %get-tuple-element.11, s32[256]{0:T(256)S(1)} %get-tuple-element.12, ...), kind=kOutput, calls=%fused_computation.36 | convolution fusion | flops 1311375360 | bytes 2564096 | tf_op jit(solution)/shard_map/...bk,kl->...bl/dot_general | solution.py:38
  158.5 1.3 copy.33
  159.8 0.0 all-gather.2.cloned.1.call-update
  159.8 0.0 reduce-scatter.4.cloned.1.call-done
  159.9 1.5 copy.38
  161.4 1.8 collective-permute-start
  163.2 15.4 %collective-permute-done = bf16[128,3328]{0,1:T(8,128)(2,1)S(1)} collective-permute-done((bf16[128,3328]{0,1:T(8,128)(2,1)S(1)}, bf16[128,3328]{0,1:T(8,128)(2,1)S(1)}, u32[]{:S(2)}, u32[]{:S(2)}) %collective-permute-start) | collective-permute-done | bytes 852000 | tf_op jit(solution)/shard_map/ppermute | solution.py:18
  178.6 0.3 fusion.17
  178.9 4.5 %collective-permute-start.1 = (bf16[128,3328]{0,1:T(8,128)(2,1)S(1)}, bf16[128,3328]{0,1:T(8,128)(2,1)S(1)}, u32[]{:S(2)}, u32[]{:S(2)}) collective-permute-start(bf16[128,3328]{0,1:T(8,128)(2,1)S(1)} %fusion.17), channel_id=1, source_target_pairs={{0,2},{2,0},{1,3},{3,1},{4,6},{6,4},{5,7},{7,5},{8,10},{10,8},{9,1... | collective-permute-start | bytes 2555912 | tf_op jit(solution)/shard_map/ppermute | solution.py:18
  183.4 15.9 %collective-permute-done.1 = bf16[128,3328]{0,1:T(8,128)(2,1)S(1)} collective-permute-done((bf16[128,3328]{0,1:T(8,128)(2,1)S(1)}, bf16[128,3328]{0,1:T(8,128)(2,1)S(1)}, u32[]{:S(2)}, u32[]{:S(2)}) %collective-permute-start.1) | collective-permute-done | bytes 852000 | tf_op jit(solution)/shard_map/ppermute | solution.py:18
  199.3 0.6 fusion.63
  199.9 0.9 collective-permute-start.2
  200.8 16.1 %collective-permute-done.2 = bf16[128,3328]{0,1:T(8,128)(2,1)S(1)} collective-permute-done((bf16[128,3328]{0,1:T(8,128)(2,1)S(1)}, bf16[128,3328]{0,1:T(8,128)(2,1)S(1)}, u32[]{:S(2)}, u32[]{:S(2)}) %collective-permute-start.2) | collective-permute-done | bytes 852000 | tf_op jit(solution)/shard_map/ppermute | solution.py:18
  216.9 1.7 fusion.19
  218.6 2.9 %collective-permute-start.3 = (bf16[128,3328]{0,1:T(8,128)(2,1)}, bf16[128,3328]{0,1:T(8,128)(2,1)}, u32[]{:S(2)}, u32[]{:S(2)}) collective-permute-start(bf16[128,3328]{0,1:T(8,128)(2,1)} %fusion.19), channel_id=1, source_target_pairs={{0,8},{8,0},{1,9},{9,1},{2,10},{10,2},{3,11},{11,3},{4,12},{12,4},... | collective-permute-start | bytes 2555912 | tf_op jit(solution)/shard_map/ppermute | solution.py:18
  221.5 0.0 all-gather.2.cloned.1.call-done
  221.5 14.9 %select_convert_fusion = bf16[3328,1024]{1,0:T(8,128)(2,1)} fusion(bf16[3328,1024]{1,0:T(8,128)(2,1)} %param.6, bf16[1024,3328]{0,1:T(8,128)(2,1)} %all-gather.2.cloned.1.call-done, bf16[1024,1024]{1,0:T(8,128)(2,1)} %bitcast.24, f32[1024]{0:T(1024)S(1)} %copy-done.1), kind=kOutput, calls=%fused_computation | convolution fusion | flops 7009992704 | bytes 22548480 | tf_op jit(solution)/shard_map/dot_general | solution.py:84
  236.3 0.9 collective-permute-done.3
  237.2 2.1 fusion.11
  239.3 3.2 %multiply_convert_fusion.1 = bf16[128,13,256]{2,0,1:T(8,128)(2,1)S(1)} fusion(f32[128,13,256]{0,2,1:T(8,128)S(1)} %bitcast.25, s32[256]{0:T(256)S(1)} %get-tuple-element.8, s32[256]{0:T(256)S(1)} %get-tuple-element.9, s32[256]{0:T(256)S(1)} %get-tuple-element.10, s32[256]{0:T(256)S(1)} %get-tuple-element.11, s32[256]{0:T(256)S(1)} %get-tuple-element.12, ...), kind=kOutput, calls=%fused_computation.37 | convolution fusion | flops 1311375360 | bytes 2564096 | tf_op jit(solution)/shard_map/...bk,kl->...bl/dot_general | solution.py:38
  242.6 0.7 copy.29
  243.3 1.3 copy.34
  (4 shorter events, 0.0 us)
Async XLA Ops:
  7.2 152.7 %reduce-scatter.4.cloned.1.call-start = ((), (), s32[]{:S(2)}) async-start(), calls=%async_computation.3 | async-start | bytes 7667712
  43.2 2.6 %copy-start.1 = (f32[1024]{0:T(1024)S(1)}, f32[1024]{0:T(1024)}, u32[]{:S(2)}) copy-start(f32[1024]{0:T(1024)} %param.7) | copy-start | bytes 12292
  67.5 1.2 copy-start
  67.5 154.0 %all-gather.2.cloned.1.call-start = ((), (), s32[]{:S(2)}) async-start(), calls=%async_computation.2 | async-start | bytes 7667712 | tf_op jit(solution)/shard_map/all_gather | solution.py:85
  69.2 20.4 %collective-permute-start.4 = (bf16[128,3328]{0,1:T(8,128)(2,1)S(1)}, bf16[128,3328]{0,1:T(8,128)(2,1)S(1)}, u32[]{:S(2)}, u32[]{:S(2)}) collective-permute-start(bf16[128,3328]{0,1:T(8,128)(2,1)S(1)} %copy.30), channel_id=1, source_target_pairs={{0,1},{1,0},{2,3},{3,2},{4,5},{5,4},{6,7},{7,6},{8,9},{9,8},{10,11... | collective-permute-start | bytes 2555912 | tf_op jit(solution)/shard_map/ppermute | solution.py:18
  90.0 21.1 %collective-permute-start.5 = (bf16[128,3328]{0,1:T(8,128)(2,1)S(1)}, bf16[128,3328]{0,1:T(8,128)(2,1)S(1)}, u32[]{:S(2)}, u32[]{:S(2)}) collective-permute-start(bf16[128,3328]{0,1:T(8,128)(2,1)S(1)} %fusion.16), channel_id=1, source_target_pairs={{0,2},{2,0},{1,3},{3,1},{4,6},{6,4},{5,7},{7,5},{8,10},{10,8},{9,1... | collective-permute-start | bytes 2555912 | tf_op jit(solution)/shard_map/ppermute | solution.py:18
  112.5 19.0 %collective-permute-start.6 = (bf16[128,3328]{0,1:T(8,128)(2,1)}, bf16[128,3328]{0,1:T(8,128)(2,1)S(1)}, u32[]{:S(2)}, u32[]{:S(2)}) collective-permute-start(bf16[128,3328]{0,1:T(8,128)(2,1)} %fusion.62), channel_id=1, source_target_pairs={{0,4},{4,0},{1,5},{5,1},{2,6},{6,2},{3,7},{7,3},{8,12},{12,8},{9,1... | collective-permute-start | bytes 2555912 | tf_op jit(solution)/shard_map/ppermute | solution.py:18
  133.1 20.0 %collective-permute-start.7 = (bf16[128,3328]{0,1:T(8,128)(2,1)}, bf16[128,3328]{0,1:T(8,128)(2,1)}, u32[]{:S(2)}, u32[]{:S(2)}) collective-permute-start(bf16[128,3328]{0,1:T(8,128)(2,1)} %fusion.18), channel_id=1, source_target_pairs={{0,8},{8,0},{1,9},{9,1},{2,10},{10,2},{3,11},{11,3},{4,12},{12,4},... | collective-permute-start | bytes 2555912 | tf_op jit(solution)/shard_map/ppermute | solution.py:18
  161.4 17.2 %collective-permute-start = (bf16[128,3328]{0,1:T(8,128)(2,1)S(1)}, bf16[128,3328]{0,1:T(8,128)(2,1)S(1)}, u32[]{:S(2)}, u32[]{:S(2)}) collective-permute-start(bf16[128,3328]{0,1:T(8,128)(2,1)S(1)} %copy.38), channel_id=1, source_target_pairs={{0,1},{1,0},{2,3},{3,2},{4,5},{5,4},{6,7},{7,6},{8,9},{9,8},{10,11... | collective-permute-start | bytes 2555912 | tf_op jit(solution)/shard_map/ppermute | solution.py:18
  178.9 20.4 %collective-permute-start.1 = (bf16[128,3328]{0,1:T(8,128)(2,1)S(1)}, bf16[128,3328]{0,1:T(8,128)(2,1)S(1)}, u32[]{:S(2)}, u32[]{:S(2)}) collective-permute-start(bf16[128,3328]{0,1:T(8,128)(2,1)S(1)} %fusion.17), channel_id=1, source_target_pairs={{0,2},{2,0},{1,3},{3,1},{4,6},{6,4},{5,7},{7,5},{8,10},{10,8},{9,1... | collective-permute-start | bytes 2555912 | tf_op jit(solution)/shard_map/ppermute | solution.py:18
  199.9 17.0 %collective-permute-start.2 = (bf16[128,3328]{0,1:T(8,128)(2,1)S(1)}, bf16[128,3328]{0,1:T(8,128)(2,1)S(1)}, u32[]{:S(2)}, u32[]{:S(2)}) collective-permute-start(bf16[128,3328]{0,1:T(8,128)(2,1)S(1)} %fusion.63), channel_id=1, source_target_pairs={{0,4},{4,0},{1,5},{5,1},{2,6},{6,2},{3,7},{7,3},{8,12},{12,8},{9,1... | collective-permute-start | bytes 2555912 | tf_op jit(solution)/shard_map/ppermute | solution.py:18
  218.6 18.6 %collective-permute-start.3 = (bf16[128,3328]{0,1:T(8,128)(2,1)}, bf16[128,3328]{0,1:T(8,128)(2,1)}, u32[]{:S(2)}, u32[]{:S(2)}) collective-permute-start(bf16[128,3328]{0,1:T(8,128)(2,1)} %fusion.19), channel_id=1, source_target_pairs={{0,8},{8,0},{1,9},{9,1},{2,10},{10,2},{3,11},{11,3},{4,12},{12,4},... | collective-permute-start | bytes 2555912 | tf_op jit(solution)/shard_map/ppermute | solution.py:18
Sparse Core Ops, SparseCore 0:
  67.6 45.3 reduce-scatter.3
  160.0 48.1 all-gather.1
where the time goes:
time: 252 us; the launch traced here: 251 us
  waiting for transfers between devices  118 us (47%)
  matrix products  33.3 us (13%)
  blocking collectives  31.9 us (13%)
  local copies, waits for them, and re-layouts  22.9 us (9%)
  starting transfers between devices  20.8 us (8%)
  between operations  14.1 us (6%)
  other arithmetic  10.2 us (4%)
    ppermute x8, waiting for transfers between devices, from_partner(): return lax.ppermute(block, axis, route)  118 us
    all_to_all x1, blocking collectives, on_device(): lax.all_to_all(out_grad, 'dp', split_axis=1, concat_axis=0, tiled=True)  31.9 us
    ppermute x8, starting transfers between devices, from_partner(): return lax.ppermute(block, axis, route)  20.7 us
    unnamed x9, local copies, waits for them, and re-layouts  18.2 us
    dot_general x1, matrix products, on_device(): lax.dot_general(lax.all_gather(mixed_hidden, 'dp', axis=0, tiled=True), s...  14.9 us
    dot_general x1, matrix products, on_device(): lax.dot_general(selected, quant_weight, (((1,), (1,)), ((), ())), preferr...  11.9 us
    dot_general x2, matrix products, block_rotate(): jnp.einsum('...bk,kl->...bl', blocks, block_table, precision=lax.Precisio...  6.5 us
    convert_element_type x6, other arithmetic, on_device(): values.astype(jnp.bfloat16)  6.02 us
  transfers between devices with their start and end apart: 10, of which 8 were waited for; matrix products, arithmetic and copies ran while one was open for 12% of the time, Pallas kernels for 0%

commit v1 on v0

v1 whole, which is shorter than its diff:
```python
import jax
import jax.numpy as jnp
from jax import lax
from jax.sharding import PartitionSpec as P

HB = 256
AXES = ("x", "core", "z", "y")
BF16 = jnp.bfloat16
F32 = jnp.float32


def move(value, route):
    nx, nc, nz, ny = (lax.axis_size(axis) for axis in AXES)

    def flat(x, c, z, y):
        return ((x % nx * nc + c) * nz + z) * ny + y

    pairs = [
        (flat(x, c, z, y), flat(*route(x, c, z, y)))
        for x in range(nx)
        for c in range(nc)
        for z in range(nz)
        for y in range(ny)
    ]
    return lax.ppermute(value, AXES, pairs)


def swap(value):
    return move(value, lambda x, c, z, y: (x, 1 - c, z, y))


def forward(value):
    return move(value, lambda x, c, z, y: (x + 1 - 2 * c, c, z, y))


def backward(value):
    return move(value, lambda x, c, z, y: (x - 1 + 2 * c, c, z, y))


def across(value):
    return move(value, lambda x, c, z, y: (x + 2, c, z, y))


def hadamard(order):
    i = jnp.arange(order, dtype=jnp.int32)
    both = jnp.bitwise_and(i[:, None], i[None, :])
    return (1 - 2 * (lax.population_count(both) % 2)).astype(BF16)


def mix_blocks(value):
    core, z, y = (lax.axis_index(axis) for axis in ("core", "z", "y"))
    for step in range(4):
        bit = 1 << (step % 2)
        y_first = step < 2

        def route(x, c, zz, yy, bit=bit, y_first=y_first):
            return (x, c, zz, yy ^ bit) if (c == 0) == y_first else (x, c, zz ^ bit, yy)

        partner = move(value, route)
        place = jnp.where((core == 0) == y_first, y, z)
        sign = jnp.where(jnp.bitwise_and(place, bit) == 0, 1.0, -1.0).astype(F32)
        total = value.astype(F32) * sign + partner.astype(F32)
        value = total.astype(BF16) if step < 3 else total
    return value


def on_device(hidden, out_grad, weight, inv_scale):
    x, core = lax.axis_index("x"), lax.axis_index("core")
    table = hadamard(HB)
    scaling = 1.0 / 64.0
    tokens, ff = hidden.shape
    cols = weight.shape[1]

    def columns(distance):
        chip = lax.rem(x + distance + 4, 4)
        return lax.dynamic_slice(out_grad, (0, chip * 2 * cols), (tokens, 2 * cols))

    def halves(value):
        mine = lax.dynamic_slice(value, (0, core * cols), (tokens, cols))
        other = lax.dynamic_slice(value, (0, (1 - core) * cols), (tokens, cols))
        return mine, other

    ahead = 1 - 2 * core
    from_across = across(columns(2))
    from_fwd = backward(columns(-ahead))
    from_bwd = forward(columns(ahead))
    own_mine, own_send = halves(columns(0))
    across_mine, across_send = halves(from_across)
    fwd_mine, fwd_send = halves(from_fwd)
    bwd_mine, bwd_send = halves(from_bwd)
    own_other, across_other = swap(own_send), swap(across_send)
    fwd_other, bwd_other = swap(bwd_send), swap(fwd_send)

    raw_code = jnp.floor(weight.astype(F32) * inv_scale[None, :] + 0.5)
    code = jnp.clip(raw_code, -8.0, 7.0).astype(BF16)
    turned = jnp.einsum(
        "kl,bkd->bld", table, code.reshape(ff // HB, HB, cols), preferred_element_type=F32
    ).reshape(ff, cols)
    turned = (turned * (scaling / inv_scale)[None, :]).astype(BF16)

    def product(mine, other):
        both = lax.dot_general(
            jnp.concatenate([mine, other]),
            turned,
            (((1,), (1,)), ((), ())),
            preferred_element_type=F32,
        ).astype(BF16)
        return both[:tokens], both[tokens:]

    def add(*terms):
        return sum(term.astype(F32) for term in terms).astype(BF16)

    p_across = product(across_mine, across_other)
    first = forward(add(p_across[0], swap(p_across[1])))
    p_fwd = product(fwd_mine, fwd_other)
    p_bwd = product(bwd_mine, bwd_other)
    second = forward(add(p_fwd[1], swap(p_bwd[0])))
    third = forward(add(p_fwd[0], swap(p_bwd[1]), first))
    p_own = product(own_mine, own_other)
    grad = add(p_own[0], swap(p_own[1]), swap(second), third)
    hidden_grad = mix_blocks(grad).astype(BF16)

    mixed = mix_blocks(hidden).astype(BF16)
    rotated = lax.dot_general(
        mixed.reshape(tokens * ff // HB, HB), table, (((1,), (0,)), ((), ())), preferred_element_type=F32
    )
    rotated = (rotated * scaling).astype(BF16).reshape(tokens, ff)
    other = swap(rotated)
    bwd_a = forward(rotated)
    bwd_b = forward(other)
    opp_a = forward(bwd_a)
    every = [rotated, other, bwd_a, bwd_b, swap(bwd_b), swap(bwd_a), opp_a, swap(opp_a)]
    grads = [own_mine, own_other, bwd_mine, bwd_other, fwd_mine, fwd_other, across_mine, across_other]
    weight_sum = lax.dot_general(
        jnp.concatenate(every),
        jnp.concatenate(grads),
        (((0,), (0,)), ((), ())),
        preferred_element_type=F32,
    )
    keep = jnp.logical_and(raw_code >= -8.0, raw_code <= 7.0)
    weight_grad = jnp.where(keep, weight_sum, 0.0).astype(BF16)
    return hidden_grad, weight_grad


def solution(mesh):
    grid = jax.sharding.Mesh(mesh.devices.reshape(4, 2, 4, 4), AXES)
    dp, tensor = ("x", "core"), ("z", "y")
    in_specs = (P(dp, tensor), P(dp, None), P(tensor, dp), P(dp))
    out_specs = (P(dp, tensor), P(tensor, dp))
    return jax.shard_map(
        on_device, mesh=grid, in_specs=in_specs, out_specs=out_specs, check_vma=False
    )
```

time: 252 us -> 182 us (0.72)
  waiting for transfers between devices: 118 us -> 75 us
  blocking collectives: 31.9 us -> 0 us
  starting transfers between devices: 20.8 us -> 36.3 us
  between operations: 14.1 us -> 1.03 us
  other arithmetic: 10.2 us -> 19.4 us
  local copies, waits for them, and re-layouts: 22.9 us -> 16.2 us
    ppermute x8 -> x30, waiting for transfers between devices: 118 us -> 75 us  [move(): return lax.ppermute(value, AXES, pairs)]
    all_to_all x1 -> x0, blocking collectives: 31.9 us -> none  [on_device(): lax.all_to_all(out_grad, 'dp', split_axis=1, concat_axis=0, tiled=True)]
    ppermute x8 -> x30, starting transfers between devices: 20.7 us -> 36.3 us  [move(): return lax.ppermute(value, AXES, pairs)]
    convert_element_type x6 -> x13, other arithmetic: 6.02 us -> 19.4 us  [the longest x1 9.88 us: on_device(): turned = (turned * (scaling / inv_scale)[None, :]).astype(BF16)]
    unnamed x9 -> x38, local copies, waits for them, and re-layouts: 18.2 us -> 10.3 us
    select_n x2 -> x0, other arithmetic: 4.18 us -> none  [butterfly(): values = jnp.where(lower_half, values + partner, partner - values)]
    reshape x0 -> x2, local copies, waits for them, and re-layouts: none -> 3.07 us  [the longest x1 2.06 us: on_device(): rotated = (rotated * scaling).astype(BF16).reshape(tokens, ff)]
    all_to_all x1 -> x0, local copies, waits for them, and re-layouts: 2.63 us -> none  [on_device(): lax.all_to_all(out_grad, 'dp', split_axis=1, concat_axis=0, tiled=True)]
  transfers between devices with their start and end apart: 10 -> 30, of which waited for: 8 -> 9; matrix products, arithmetic and copies ran while one was open for 12% -> 37% of each run, Pallas kernels for 0% -> 0%
where the time goes in v1:
time: 182 us
  waiting for transfers between devices  75 us (41%)
  starting transfers between devices  36.3 us (20%)
  matrix products  34.2 us (19%)
  other arithmetic  19.4 us (11%)
  local copies, waits for them, and re-layouts  16.2 us (9%)
    ppermute x30, waiting for transfers between devices, move(): return lax.ppermute(value, AXES, pairs)  75 us
    ppermute x30, starting transfers between devices, move(): return lax.ppermute(value, AXES, pairs)  36.3 us
    dot_general x4, matrix products, product(): lax.dot_general(jnp.concatenate([mine, other]), turned, (((1,), (1,)), ((...  14.1 us
    dot_general x1, matrix products, on_device(): lax.dot_general(jnp.concatenate(every), jnp.concatenate(grads), (((0,), (...  11.8 us
    unnamed x38, local copies, waits for them, and re-layouts  10.3 us
    convert_element_type x1, other arithmetic, on_device(): turned = (turned * (scaling / inv_scale)[None, :]).astype(BF16)  9.88 us
    dot_general x1, matrix products, on_device(): jnp.einsum('kl,bkd->bld', table, code.reshape(ff // HB, HB, cols), prefer...  6.93 us
    convert_element_type x1, other arithmetic, on_device(): code = jnp.clip(raw_code, -8.0, 7.0).astype(BF16)  5.42 us
  transfers between devices with their start and end apart: 30, of which 9 were waited for; matrix products, arithmetic and copies ran while one was open for 37% of the time, Pallas kernels for 0%

profile of v1, /device:TPU:0, one launch (start us, length us, event | category | flops | bytes accessed | tf_op | source)
XLA Modules:
  0.0 182.1 jit_solution(2687324387478338074)
XLA Ops:
  0.7 1.5 constant_dynamic-slice_fusion.8
  2.2 2.9 %collective-permute-start.2 = (bf16[128,2048]{1,0:T(8,128)(2,1)S(1)}, bf16[128,2048]{1,0:T(8,128)(2,1)}, u32[]{:S(2)}, u32[]{:S(2)}) collective-permute-start(bf16[128,2048]{1,0:T(8,128)(2,1)S(1)} %get-tuple-element.10), channel_id=1, source_target_pairs={{0,96},{1,97},{2,98},{3,99},{4,100},{5,101},{6,102},{7,103},{8,104... | collective-permute-start | bytes 1572872 | tf_op jit(solution)/shard_map/ppermute | solution.py:25
  5.1 2.2 %constant_dynamic-update-slice_fusion.15 = (bf16[1024,1024]{1,0:T(8,128)(2,1)}, bf16[128,1024]{1,0:T(8,128)(2,1)}, bf16[128,1024]{1,0:T(8,128)(2,1)}) fusion(bf16[128,8192]{1,0:T(8,128)(2,1)} %param.5, s32[]{:T(128)S(6)} %dynamic_slice.40, s32[]{:T(128)S(6)} %dynamic_slice.42), kind=kLoop, calls=%fused_computation.62 | loop fusion | bytes 1310728
  7.3 2.3 %collective-permute-start.10 = (bf16[128,2048]{1,0:T(8,128)(2,1)S(1)}, bf16[128,2048]{1,0:T(8,128)(2,1)}, u32[]{:S(2)}, u32[]{:S(2)}) collective-permute-start(bf16[128,2048]{1,0:T(8,128)(2,1)S(1)} %get-tuple-element.11), channel_id=1, source_target_pairs={{0,64},{1,65},{2,66},{3,67},{4,68},{5,69},{6,70},{7,71},{8,72},{9,... | collective-permute-start | bytes 1572872 | tf_op jit(solution)/shard_map/ppermute | solution.py:25
  9.6 1.6 collective-permute-start.19
  11.2 5.4 %clamp_convert_fusion = bf16[3328,1024]{1,0:T(8,128)(2,1)S(1)} fusion(bf16[3328,1024]{1,0:T(8,128)(2,1)} %param.6, f32[1024]{0:T(1024)S(1)} %copy-done.7), kind=kLoop, calls=%fused_computation.3 | loop fusion | flops 20447232 | bytes 13635584 | tf_op jit(solution)/shard_map/convert_element_type | solution.py:95
  16.6 6.9 %fusion.21 = f32[13,1024,256]{1,2,0:T(8,128)} fusion(bf16[13,256,1024]{2,1,0:T(8,128)(2,1)S(1)} %bitcast.18), kind=kOutput, calls=%fused_computation.45 | convolution fusion | flops 1745879040 | bytes 20447232 | tf_op jit(solution)/shard_map/kl,bkd->bld/dot_general | solution.py:96
  23.5 1.0 constant_dynamic-slice_fusion.3
  24.5 0.1 collective-permute-start.5
  24.6 9.9 %fusion = bf16[3328,1024]{1,0:T(8,128)(2,1)} fusion(f32[13,1024,256]{1,2,0:T(8,128)} %fusion.21, f32[1024]{0:T(1024)S(1)} %broadcast_divide_fusion), kind=kLoop, calls=%fused_computation.1 | loop fusion | flops 6815744 | bytes 20451328 | tf_op jit(solution)/shard_map/convert_element_type | solution.py:99
  34.5 0.8 constant_dynamic-update-slice_fusion.14
  35.3 2.0 %constant_dynamic-update-slice_fusion.13 = (bf16[1024,1024]{1,0:T(8,128)(2,1)}, bf16[128,1024]{1,0:T(8,128)(2,1)S(1)}, bf16[128,1024]{1,0:T(8,128)(2,1)S(1)}) fusion(bf16[1024,1024]{1,0:T(8,128)(2,1)} %constant_dynamic-update-slice_fusion.14, bf16[128,2048]{1,0:T(8,128)(2,1)} %collective-permute-done.3, s32[]{:T(128)S(6)} %select_n.72, s32[]{:T(128)S(6)} %select_n.76), kind=kLoop, calls=%fused_computation.60 | loop fusion | bytes 1310728
  37.3 0.5 collective-permute-start.4
  37.8 5.1 %convolution_convert_fusion.1 = bf16[256,3328]{1,0:T(8,128)(2,1)S(1)} fusion(bf16[3328,1024]{1,0:T(8,128)(2,1)} %fusion, bf16[128,1024]{1,0:T(8,128)(2,1)S(1)} %collective-permute-done.5, bf16[128,1024]{1,0:T(8,128)(2,1)S(1)} %get-tuple-element.7), kind=kOutput, calls=%fused_computation.9 | convolution fusion | flops 1746731008 | bytes 9043968 | tf_op jit(solution)/shard_map/dot_general | solution.py:102
  42.8 0.1 fusion.35
  43.0 0.1 collective-permute-start.6
  43.1 0.7 constant_dynamic-update-slice_fusion.12
  43.8 1.7 constant_dynamic-update-slice_fusion.11
  45.5 0.7 constant_dynamic-update-slice_fusion.10
  46.2 1.8 constant_dynamic-update-slice_fusion.9
  48.0 0.5 collective-permute-start.11
  48.5 0.2 add_convert_fusion.3
  48.7 3.0 %collective-permute-start.20 = (bf16[128,3328]{1,0:T(8,128)(2,1)S(1)}, bf16[128,3328]{1,0:T(8,128)(2,1)S(1)}, u32[]{:S(2)}, u32[]{:S(2)}) collective-permute-start(bf16[128,3328]{1,0:T(8,128)(2,1)S(1)} %add_convert_fusion.3), channel_id=1, source_target_pairs={{0,2},{1,3},{2,0},{3,1},{4,6},{5,7},{6,4},{7,5},{8,10},{9,11},{10,... | collective-permute-start | bytes 2555912 | tf_op jit(solution)/shard_map/ppermute | solution.py:25
  51.7 2.0 %convolution_convert_fusion.2 = bf16[256,3328]{1,0:T(8,128)(2,1)S(1)} fusion(bf16[3328,1024]{1,0:T(8,128)(2,1)S(1)} %bitcast.22, bf16[128,1024]{1,0:T(8,128)(2,1)S(1)} %collective-permute-done.4, bf16[128,1024]{1,0:T(8,128)(2,1)S(1)} %get-tuple-element.5), kind=kOutput, calls=%fused_computation.10 | convolution fusion | flops 1746731008 | bytes 9043968 | tf_op jit(solution)/shard_map/dot_general | solution.py:102
  53.7 2.0 %convolution_convert_fusion = bf16[256,3328]{1,0:T(8,128)(2,1)S(1)} fusion(bf16[3328,1024]{1,0:T(8,128)(2,1)S(1)} %bitcast.22, bf16[128,1024]{1,0:T(8,128)(2,1)S(1)} %collective-permute-done.11, bf16[128,1024]{1,0:T(8,128)(2,1)S(1)} %get-tuple-element.3), kind=kOutput, calls=%fused_computation.8 | convolution fusion | flops 1746731008 | bytes 9043968 | tf_op jit(solution)/shard_map/dot_general | solution.py:102
  55.8 1.3 collective-permute-start.12
  57.1 5.9 %collective-permute-done.20 = bf16[128,3328]{1,0:T(8,128)(2,1)S(1)} collective-permute-done((bf16[128,3328]{1,0:T(8,128)(2,1)S(1)}, bf16[128,3328]{1,0:T(8,128)(2,1)S(1)}, u32[]{:S(2)}, u32[]{:S(2)}) %collective-permute-start.20) | collective-permute-done | bytes 852000 | tf_op jit(solution)/shard_map/ppermute | solution.py:25
  63.0 0.2 add_convert_fusion.2
  63.3 2.0 %collective-permute-start.21 = (bf16[128,3328]{1,0:T(8,128)(2,1)S(1)}, bf16[128,3328]{1,0:T(8,128)(2,1)S(1)}, u32[]{:S(2)}, u32[]{:S(2)}) collective-permute-start(bf16[128,3328]{1,0:T(8,128)(2,1)S(1)} %add_convert_fusion.2), channel_id=1, source_target_pairs={{0,4},{1,5},{2,6},{3,7},{4,0},{5,1},{6,2},{7,3},{8,12},{9,13},{10,... | collective-permute-start | bytes 2555912 | tf_op jit(solution)/shard_map/ppermute | solution.py:25
  65.3 0.2 add_convert_fusion.10
  65.5 1.9 %collective-permute-start.13 = (bf16[128,3328]{1,0:T(8,128)(2,1)S(1)}, bf16[128,3328]{1,0:T(8,128)(2,1)S(1)}, u32[]{:S(2)}, u32[]{:S(2)}) collective-permute-start(bf16[128,3328]{1,0:T(8,128)(2,1)S(1)} %add_convert_fusion.10), channel_id=1, source_target_pairs={{0,32},{1,33},{2,34},{3,35},{4,36},{5,37},{6,38},{7,39},{8,40},{9,... | collective-permute-start | bytes 2555912 | tf_op jit(solution)/shard_map/ppermute | solution.py:25
  67.4 8.7 %collective-permute-done.21 = bf16[128,3328]{1,0:T(8,128)(2,1)S(1)} collective-permute-done((bf16[128,3328]{1,0:T(8,128)(2,1)S(1)}, bf16[128,3328]{1,0:T(8,128)(2,1)S(1)}, u32[]{:S(2)}, u32[]{:S(2)}) %collective-permute-start.21) | collective-permute-done | bytes 852000 | tf_op jit(solution)/shard_map/ppermute | solution.py:25
  76.1 0.2 add_convert_fusion.1
  76.3 4.0 %collective-permute-start.22 = (bf16[128,3328]{1,0:T(8,128)(2,1)S(1)}, bf16[128,3328]{1,0:T(8,128)(2,1)S(1)}, u32[]{:S(2)}, u32[]{:S(2)}) collective-permute-start(bf16[128,3328]{1,0:T(8,128)(2,1)S(1)} %add_convert_fusion.1), channel_id=1, source_target_pairs={{0,8},{1,9},{2,10},{3,11},{4,12},{5,13},{6,14},{7,15},{8,0},{9,1},... | collective-permute-start | bytes 2555912 | tf_op jit(solution)/shard_map/ppermute | solution.py:25
  80.3 0.5 add_convert_fusion.11
  80.8 1.9 %collective-permute-start.7 = (bf16[128,3328]{1,0:T(8,128)(2,1)S(1)}, bf16[128,3328]{1,0:T(8,128)(2,1)}, u32[]{:S(2)}, u32[]{:S(2)}) collective-permute-start(bf16[128,3328]{1,0:T(8,128)(2,1)S(1)} %get-tuple-element.14), channel_id=1, source_target_pairs={{0,32},{1,33},{2,34},{3,35},{4,36},{5,37},{6,38},{7,39},{8,40},{9,... | collective-permute-start | bytes 2555912 | tf_op jit(solution)/shard_map/ppermute | solution.py:25
  82.7 8.2 %collective-permute-done.22 = bf16[128,3328]{1,0:T(8,128)(2,1)S(1)} collective-permute-done((bf16[128,3328]{1,0:T(8,128)(2,1)S(1)}, bf16[128,3328]{1,0:T(8,128)(2,1)S(1)}, u32[]{:S(2)}, u32[]{:S(2)}) %collective-permute-start.22) | collective-permute-done | bytes 852000 | tf_op jit(solution)/shard_map/ppermute | solution.py:25
  90.9 0.2 add_convert_fusion
  91.2 1.0 reshape.20
  92.2 1.4 fusion.4
  93.6 2.1 %reshape.21 = bf16[128,3328]{1,0:T(8,128)(2,1)S(1)} reshape(bf16[1664,256]{1,0:T(8,128)(2,1)} %fusion.4) | data formatting | bytes 1703936 | tf_op jit(solution)/shard_map/reshape | solution.py:127
  95.7 0.1 collective-permute-start.23
  95.8 2.1 %collective-permute-start.24 = (bf16[128,3328]{1,0:T(8,128)(2,1)S(1)}, bf16[128,3328]{1,0:T(8,128)(2,1)S(1)}, u32[]{:S(2)}, u32[]{:S(2)}) collective-permute-start(bf16[128,3328]{1,0:T(8,128)(2,1)S(1)} %reshape.21), channel_id=1, source_target_pairs={{0,32},{1,33},{2,34},{3,35},{4,36},{5,37},{6,38},{7,39},{8,40},{9,... | collective-permute-start | bytes 2555912 | tf_op jit(solution)/shard_map/ppermute | solution.py:25
  97.9 5.1 %convolution_convert_fusion.3 = bf16[256,3328]{1,0:T(8,128)(2,1)S(1)} fusion(bf16[3328,1024]{1,0:T(8,128)(2,1)} %fusion, bf16[128,1024]{1,0:T(8,128)(2,1)S(1)} %copy-done.2, bf16[128,1024]{1,0:T(8,128)(2,1)S(1)} %copy-done.5), kind=kOutput, calls=%fused_computation.11 | convolution fusion | flops 1746731008 | bytes 9043968 | tf_op jit(solution)/shard_map/dot_general | solution.py:102
  103.0 0.3 collective-permute-start.1
  103.5 1.4 collective-permute-start.8
  104.9 0.7 collective-permute-start.25
  105.6 4.4 %collective-permute-done.24 = bf16[128,3328]{1,0:T(8,128)(2,1)S(1)} collective-permute-done((bf16[128,3328]{1,0:T(8,128)(2,1)S(1)}, bf16[128,3328]{1,0:T(8,128)(2,1)S(1)}, u32[]{:S(2)}, u32[]{:S(2)}) %collective-permute-start.24) | collective-permute-done | bytes 852000 | tf_op jit(solution)/shard_map/ppermute | solution.py:25
  110.1 0.7 collective-permute-start.28
  110.7 8.4 %collective-permute-done.14 = bf16[128,3328]{1,0:T(8,128)(2,1)S(1)} collective-permute-done((bf16[128,3328]{1,0:T(8,128)(2,1)S(1)}, bf16[128,3328]{1,0:T(8,128)(2,1)S(1)}, u32[]{:S(2)}, u32[]{:S(2)}) %collective-permute-start.14) | collective-permute-done | bytes 852000 | tf_op jit(solution)/shard_map/ppermute | solution.py:25
  119.1 0.5 add_convert_fusion.8
  119.6 0.6 collective-permute-start.15
  120.2 8.1 %collective-permute-done.25 = bf16[128,3328]{1,0:T(8,128)(2,1)S(1)} collective-permute-done((bf16[128,3328]{1,0:T(8,128)(2,1)S(1)}, bf16[128,3328]{1,0:T(8,128)(2,1)S(1)}, u32[]{:S(2)}, u32[]{:S(2)}) %collective-permute-start.25) | collective-permute-done | bytes 852000 | tf_op jit(solution)/shard_map/ppermute | solution.py:25
  128.2 9.1 %collective-permute-done.28 = bf16[128,3328]{1,0:T(8,128)(2,1)S(1)} collective-permute-done((bf16[128,3328]{1,0:T(8,128)(2,1)S(1)}, bf16[128,3328]{1,0:T(8,128)(2,1)S(1)}, u32[]{:S(2)}, u32[]{:S(2)}) %collective-permute-start.28) | collective-permute-done | bytes 852000 | tf_op jit(solution)/shard_map/ppermute | solution.py:25
  137.5 0.3 add_convert_fusion.7
  137.7 3.0 %collective-permute-start.16 = (bf16[128,3328]{1,0:T(8,128)(2,1)S(1)}, bf16[128,3328]{1,0:T(8,128)(2,1)S(1)}, u32[]{:S(2)}, u32[]{:S(2)}) collective-permute-start(bf16[128,3328]{1,0:T(8,128)(2,1)S(1)} %add_convert_fusion.7), channel_id=1, source_target_pairs={{0,2},{1,3},{2,0},{3,1},{4,6},{5,7},{6,4},{7,5},{8,10},{9,11},{10,... | collective-permute-start | bytes 2555912 | tf_op jit(solution)/shard_map/ppermute | solution.py:25
  140.9 11.1 %collective-permute-done.16 = bf16[128,3328]{1,0:T(8,128)(2,1)S(1)} collective-permute-done((bf16[128,3328]{1,0:T(8,128)(2,1)S(1)}, bf16[128,3328]{1,0:T(8,128)(2,1)S(1)}, u32[]{:S(2)}, u32[]{:S(2)}) %collective-permute-start.16) | collective-permute-done | bytes 852000 | tf_op jit(solution)/shard_map/ppermute | solution.py:25
  152.0 0.2 add_convert_fusion.6
  152.3 1.6 collective-permute-start.17
  154.0 11.0 %collective-permute-done.17 = bf16[128,3328]{1,0:T(8,128)(2,1)S(1)} collective-permute-done((bf16[128,3328]{1,0:T(8,128)(2,1)S(1)}, bf16[128,3328]{1,0:T(8,128)(2,1)S(1)}, u32[]{:S(2)}, u32[]{:S(2)}) %collective-permute-start.17) | collective-permute-done | bytes 852000 | tf_op jit(solution)/shard_map/ppermute | solution.py:25
  165.0 0.3 add_convert_fusion.5
  165.3 3.9 %collective-permute-start.18 = (bf16[128,3328]{1,0:T(8,128)(2,1)S(1)}, bf16[128,3328]{1,0:T(8,128)(2,1)S(1)}, u32[]{:S(2)}, u32[]{:S(2)}) collective-permute-start(bf16[128,3328]{1,0:T(8,128)(2,1)S(1)} %add_convert_fusion.5), channel_id=1, source_target_pairs={{0,8},{1,9},{2,10},{3,11},{4,12},{5,13},{6,14},{7,15},{8,0},{9,1},... | collective-permute-start | bytes 2555912 | tf_op jit(solution)/shard_map/ppermute | solution.py:25
  169.2 11.8 %select_convert_fusion = bf16[3328,1024]{1,0:T(8,128)(2,1)} fusion(bf16[3328,1024]{1,0:T(8,128)(2,1)S(1)} %bitcast.20, bf16[1024,3328]{1,0:T(8,128)(2,1)S(1)} %constant_dynamic-update-slice_fusion, bf16[1024,1024]{1,0:T(8,128)(2,1)S(1)} %constant_dynamic-update-slice_fusion.8, f32[1024]{0:T(1024)S(1)} %copy-done.7), kind=kOutput, calls=%fused_computation.2 | convolution fusion | flops 7009992704 | bytes 22548480 | tf_op jit(solution)/shard_map/dot_general | solution.py:134
  181.0 1.2 add_convert_fusion.4
  (66 shorter events, 0.8 us)
Async XLA Ops:
  0.7 8.9 %copy-start = (bf16[128,3328]{1,0:T(8,128)(2,1)S(1)}, bf16[128,3328]{1,0:T(8,128)(2,1)}, u32[]{:S(2)}) copy-start(bf16[128,3328]{1,0:T(8,128)(2,1)} %param.4) | copy-start | bytes 2555908
  0.7 10.5 %copy-start.7 = (f32[1024]{0:T(1024)S(1)}, f32[1024]{0:T(1024)}, u32[]{:S(2)}) copy-start(f32[1024]{0:T(1024)} %param.7) | copy-start | bytes 12292
  2.2 21.3 %collective-permute-start.2 = (bf16[128,2048]{1,0:T(8,128)(2,1)S(1)}, bf16[128,2048]{1,0:T(8,128)(2,1)}, u32[]{:S(2)}, u32[]{:S(2)}) collective-permute-start(bf16[128,2048]{1,0:T(8,128)(2,1)S(1)} %get-tuple-element.10), channel_id=1, source_target_pairs={{0,96},{1,97},{2,98},{3,99},{4,100},{5,101},{6,102},{7,103},{8,104... | collective-permute-start | bytes 1572872 | tf_op jit(solution)/shard_map/ppermute | solution.py:25
  7.3 27.2 %collective-permute-start = (bf16[128,1024]{1,0:T(8,128)(2,1)}, bf16[128,1024]{1,0:T(8,128)(2,1)S(1)}, u32[]{:S(2)}, u32[]{:S(2)}) collective-permute-start(bf16[128,1024]{1,0:T(8,128)(2,1)} %get-tuple-element.13), channel_id=1, source_target_pairs={{0,16},{1,17},{2,18},{3,19},{4,20},{5,21},{6,22},{7,23},{8,24},{9,... | collective-permute-start | bytes 786440 | tf_op jit(solution)/shard_map/ppermute | solution.py:25
  7.3 28.0 %collective-permute-start.3 = (bf16[128,2048]{1,0:T(8,128)(2,1)S(1)}, bf16[128,2048]{1,0:T(8,128)(2,1)}, u32[]{:S(2)}, u32[]{:S(2)}) collective-permute-start(bf16[128,2048]{1,0:T(8,128)(2,1)S(1)} %get-tuple-element.12), channel_id=1, source_target_pairs={{0,32},{1,33},{2,34},{3,35},{4,36},{5,37},{6,38},{7,39},{8,40},{9,... | collective-permute-start | bytes 1572872 | tf_op jit(solution)/shard_map/ppermute | solution.py:25
  7.3 38.9 %collective-permute-start.10 = (bf16[128,2048]{1,0:T(8,128)(2,1)S(1)}, bf16[128,2048]{1,0:T(8,128)(2,1)}, u32[]{:S(2)}, u32[]{:S(2)}) collective-permute-start(bf16[128,2048]{1,0:T(8,128)(2,1)S(1)} %get-tuple-element.11), channel_id=1, source_target_pairs={{0,64},{1,65},{2,66},{3,67},{4,68},{5,69},{6,70},{7,71},{8,72},{9,... | collective-permute-start | bytes 1572872 | tf_op jit(solution)/shard_map/ppermute | solution.py:25
  9.6 38.9 %collective-permute-start.19 = (bf16[128,3328]{1,0:T(8,128)(2,1)S(1)}, bf16[128,3328]{1,0:T(8,128)(2,1)S(1)}, u32[]{:S(2)}, u32[]{:S(2)}) collective-permute-start(bf16[128,3328]{1,0:T(8,128)(2,1)S(1)} %copy-done), channel_id=1, source_target_pairs={{0,1},{1,0},{2,3},{3,2},{4,5},{5,4},{6,7},{7,6},{8,9},{9,8},{10,11... | collective-permute-start | bytes 2555912 | tf_op jit(solution)/shard_map/ppermute | solution.py:25
  24.5 13.3 %collective-permute-start.5 = (bf16[128,1024]{1,0:T(8,128)(2,1)S(1)}, bf16[128,1024]{1,0:T(8,128)(2,1)S(1)}, u32[]{:S(2)}, u32[]{:S(2)}) collective-permute-start(bf16[128,1024]{1,0:T(8,128)(2,1)S(1)} %constant_dynamic-slice_fusion.3), channel_id=1, source_target_pairs={{0,16},{1,17},{2,18},{3,19},{4,20},{5,21},{6,22},{7,23},{8,24},{9,... | collective-permute-start | bytes 786440 | tf_op jit(solution)/shard_map/ppermute | solution.py:25
  34.5 8.4 %copy-start.1 = (bf16[128,1024]{1,0:T(8,128)(2,1)}, bf16[128,1024]{1,0:T(8,128)(2,1)S(1)}, u32[]{:S(2)}) copy-start(bf16[128,1024]{1,0:T(8,128)(2,1)S(1)} %collective-permute-done) | copy-start | bytes 786436
  35.3 16.4 %slice-start.2 = ((s8[6815744]{0:T(1024)(128)(4,1)}), s8[4194304]{0:T(1024)(128)(4,1)S(1)}, s32[]{:S(2)}) async-start(s8[6815744]{0:T(1024)(128)(4,1)} %bitcast.21), calls=%async_computation.2 | async-start | bytes 8388608
  37.3 8.2 %collective-permute-start.4 = (bf16[128,1024]{1,0:T(8,128)(2,1)S(1)}, bf16[128,1024]{1,0:T(8,128)(2,1)S(1)}, u32[]{:S(2)}, u32[]{:S(2)}) collective-permute-start(bf16[128,1024]{1,0:T(8,128)(2,1)S(1)} %get-tuple-element.19), channel_id=1, source_target_pairs={{0,16},{1,17},{2,18},{3,19},{4,20},{5,21},{6,22},{7,23},{8,24},{9,... | collective-permute-start | bytes 786440 | tf_op jit(solution)/shard_map/ppermute | solution.py:25
  37.8 14.0 %slice-start.3 = ((s8[6815744]{0:T(1024)(128)(4,1)}), s8[2621440]{0:T(1024)(128)(4,1)S(1)}, s32[]{:S(2)}) async-start(s8[6815744]{0:T(1024)(128)(4,1)} %bitcast.21), calls=%async_computation.3 | async-start | bytes 5242880
  43.0 37.3 %collective-permute-start.6 = (bf16[128,3328]{1,0:T(8,128)(2,1)S(1)}, bf16[128,3328]{1,0:T(8,128)(2,1)S(1)}, u32[]{:S(2)}, u32[]{:S(2)}) collective-permute-start(bf16[128,3328]{1,0:T(8,128)(2,1)S(1)} %get-tuple-element.16), channel_id=1, source_target_pairs={{0,16},{1,17},{2,18},{3,19},{4,20},{5,21},{6,22},{7,23},{8,24},{9,... | collective-permute-start | bytes 2555912 | tf_op jit(solution)/shard_map/ppermute | solution.py:25
  48.0 5.8 %collective-permute-start.11 = (bf16[128,1024]{1,0:T(8,128)(2,1)S(1)}, bf16[128,1024]{1,0:T(8,128)(2,1)S(1)}, u32[]{:S(2)}, u32[]{:S(2)}) collective-permute-start(bf16[128,1024]{1,0:T(8,128)(2,1)S(1)} %get-tuple-element.18), channel_id=1, source_target_pairs={{0,16},{1,17},{2,18},{3,19},{4,20},{5,21},{6,22},{7,23},{8,24},{9,... | collective-permute-start | bytes 786440 | tf_op jit(solution)/shard_map/ppermute | solution.py:25
  48.5 31.8 %collective-permute-start.9 = (bf16[128,3328]{1,0:T(8,128)(2,1)S(1)}, bf16[128,3328]{1,0:T(8,128)(2,1)S(1)}, u32[]{:S(2)}, u32[]{:S(2)}) collective-permute-start(bf16[128,3328]{1,0:T(8,128)(2,1)S(1)} %get-tuple-element.17), channel_id=1, source_target_pairs={{0,16},{1,17},{2,18},{3,19},{4,20},{5,21},{6,22},{7,23},{8,24},{9,... | collective-permute-start | bytes 2555912 | tf_op jit(solution)/shard_map/ppermute | solution.py:25
  48.7 14.3 %collective-permute-start.20 = (bf16[128,3328]{1,0:T(8,128)(2,1)S(1)}, bf16[128,3328]{1,0:T(8,128)(2,1)S(1)}, u32[]{:S(2)}, u32[]{:S(2)}) collective-permute-start(bf16[128,3328]{1,0:T(8,128)(2,1)S(1)} %add_convert_fusion.3), channel_id=1, source_target_pairs={{0,2},{1,3},{2,0},{3,1},{4,6},{5,7},{6,4},{7,5},{8,10},{9,11},{10,... | collective-permute-start | bytes 2555912 | tf_op jit(solution)/shard_map/ppermute | solution.py:25
  53.7 2.0 %copy-start.3 = (bf16[128,1024]{1,0:T(8,128)(2,1)}, bf16[128,1024]{1,0:T(8,128)(2,1)S(1)}, u32[]{:S(2)}) copy-start(bf16[128,1024]{1,0:T(8,128)(2,1)S(1)} %collective-permute-done.11) | copy-start | bytes 786436
  55.8 9.5 %collective-permute-start.12 = (bf16[128,3328]{1,0:T(8,128)(2,1)S(1)}, bf16[128,3328]{1,0:T(8,128)(2,1)S(1)}, u32[]{:S(2)}, u32[]{:S(2)}) collective-permute-start(bf16[128,3328]{1,0:T(8,128)(2,1)S(1)} %slice.39), channel_id=1, source_target_pairs={{0,16},{1,17},{2,18},{3,19},{4,20},{5,21},{6,22},{7,23},{8,24},{9,... | collective-permute-start | bytes 2555912 | tf_op jit(solution)/shard_map/ppermute | solution.py:25
  63.3 12.8 %collective-permute-start.21 = (bf16[128,3328]{1,0:T(8,128)(2,1)S(1)}, bf16[128,3328]{1,0:T(8,128)(2,1)S(1)}, u32[]{:S(2)}, u32[]{:S(2)}) collective-permute-start(bf16[128,3328]{1,0:T(8,128)(2,1)S(1)} %add_convert_fusion.2), channel_id=1, source_target_pairs={{0,4},{1,5},{2,6},{3,7},{4,0},{5,1},{6,2},{7,3},{8,12},{9,13},{10,... | collective-permute-start | bytes 2555912 | tf_op jit(solution)/shard_map/ppermute | solution.py:25
  65.5 14.8 %collective-permute-start.13 = (bf16[128,3328]{1,0:T(8,128)(2,1)S(1)}, bf16[128,3328]{1,0:T(8,128)(2,1)S(1)}, u32[]{:S(2)}, u32[]{:S(2)}) collective-permute-start(bf16[128,3328]{1,0:T(8,128)(2,1)S(1)} %add_convert_fusion.10), channel_id=1, source_target_pairs={{0,32},{1,33},{2,34},{3,35},{4,36},{5,37},{6,38},{7,39},{8,40},{9,... | collective-permute-start | bytes 2555912 | tf_op jit(solution)/shard_map/ppermute | solution.py:25
  76.3 14.6 %collective-permute-start.22 = (bf16[128,3328]{1,0:T(8,128)(2,1)S(1)}, bf16[128,3328]{1,0:T(8,128)(2,1)S(1)}, u32[]{:S(2)}, u32[]{:S(2)}) collective-permute-start(bf16[128,3328]{1,0:T(8,128)(2,1)S(1)} %add_convert_fusion.1), channel_id=1, source_target_pairs={{0,8},{1,9},{2,10},{3,11},{4,12},{5,13},{6,14},{7,15},{8,0},{9,1},... | collective-permute-start | bytes 2555912 | tf_op jit(solution)/shard_map/ppermute | solution.py:25
  80.8 22.7 %collective-permute-start.7 = (bf16[128,3328]{1,0:T(8,128)(2,1)S(1)}, bf16[128,3328]{1,0:T(8,128)(2,1)}, u32[]{:S(2)}, u32[]{:S(2)}) collective-permute-start(bf16[128,3328]{1,0:T(8,128)(2,1)S(1)} %get-tuple-element.14), channel_id=1, source_target_pairs={{0,32},{1,33},{2,34},{3,35},{4,36},{5,37},{6,38},{7,39},{8,40},{9,... | collective-permute-start | bytes 2555912 | tf_op jit(solution)/shard_map/ppermute | solution.py:25
  92.2 5.7 %copy-start.2 = (bf16[128,1024]{1,0:T(8,128)(2,1)S(1)}, bf16[128,1024]{1,0:T(8,128)(2,1)}, u32[]{:S(2)}) copy-start(bf16[128,1024]{1,0:T(8,128)(2,1)} %copy-done.1) | copy-start | bytes 786436
  92.2 5.7 %copy-start.5 = (bf16[128,1024]{1,0:T(8,128)(2,1)S(1)}, bf16[128,1024]{1,0:T(8,128)(2,1)}, u32[]{:S(2)}) copy-start(bf16[128,1024]{1,0:T(8,128)(2,1)} %get-tuple-element.9) | copy-start | bytes 786436
  95.7 9.2 %collective-permute-start.23 = (bf16[128,3328]{1,0:T(8,128)(2,1)S(1)}, bf16[128,3328]{1,0:T(8,128)(2,1)S(1)}, u32[]{:S(2)}, u32[]{:S(2)}) collective-permute-start(bf16[128,3328]{1,0:T(8,128)(2,1)S(1)} %reshape.21), channel_id=1, source_target_pairs={{0,16},{1,17},{2,18},{3,19},{4,20},{5,21},{6,22},{7,23},{8,24},{9,... | collective-permute-start | bytes 2555912 | tf_op jit(solution)/shard_map/ppermute | solution.py:25
  95.8 14.2 %collective-permute-start.24 = (bf16[128,3328]{1,0:T(8,128)(2,1)S(1)}, bf16[128,3328]{1,0:T(8,128)(2,1)S(1)}, u32[]{:S(2)}, u32[]{:S(2)}) collective-permute-start(bf16[128,3328]{1,0:T(8,128)(2,1)S(1)} %reshape.21), channel_id=1, source_target_pairs={{0,32},{1,33},{2,34},{3,35},{4,36},{5,37},{6,38},{7,39},{8,40},{9,... | collective-permute-start | bytes 2555912 | tf_op jit(solution)/shard_map/ppermute | solution.py:25
  97.9 5.5 %copy-start.4 = (bf16[128,1024]{1,0:T(8,128)(2,1)S(1)}, bf16[128,1024]{1,0:T(8,128)(2,1)}, u32[]{:S(2)}) copy-start(bf16[128,1024]{1,0:T(8,128)(2,1)} %copy-done.3) | copy-start | bytes 786436
  97.9 5.5 %copy-start.6 = (bf16[1024,1024]{1,0:T(8,128)(2,1)S(1)}, bf16[1024,1024]{1,0:T(8,128)(2,1)}, u32[]{:S(2)}) copy-start(bf16[1024,1024]{1,0:T(8,128)(2,1)} %get-tuple-element.2) | copy-start | bytes 6291460
  103.0 7.0 %collective-permute-start.1 = (bf16[128,3328]{1,0:T(8,128)(2,1)S(1)}, bf16[128,3328]{1,0:T(8,128)(2,1)S(1)}, u32[]{:S(2)}, u32[]{:S(2)}) collective-permute-start(bf16[128,3328]{1,0:T(8,128)(2,1)S(1)} %slice.33), channel_id=1, source_target_pairs={{0,16},{1,17},{2,18},{3,19},{4,20},{5,21},{6,22},{7,23},{8,24},{9,... | collective-permute-start | bytes 2555912 | tf_op jit(solution)/shard_map/ppermute | solution.py:25
  103.4 15.7 %collective-permute-start.14 = (bf16[128,3328]{1,0:T(8,128)(2,1)S(1)}, bf16[128,3328]{1,0:T(8,128)(2,1)S(1)}, u32[]{:S(2)}, u32[]{:S(2)}) collective-permute-start(bf16[128,3328]{1,0:T(8,128)(2,1)S(1)} %get-tuple-element.15), channel_id=1, source_target_pairs={{0,32},{1,33},{2,34},{3,35},{4,36},{5,37},{6,38},{7,39},{8,40},{9,... | collective-permute-start | bytes 2555912 | tf_op jit(solution)/shard_map/ppermute | solution.py:25
  103.5 15.6 %collective-permute-start.8 = (bf16[128,3328]{1,0:T(8,128)(2,1)}, bf16[128,3328]{1,0:T(8,128)(2,1)S(1)}, u32[]{:S(2)}, u32[]{:S(2)}) collective-permute-start(bf16[128,3328]{1,0:T(8,128)(2,1)} %collective-permute-done.7), channel_id=1, source_target_pairs={{0,16},{1,17},{2,18},{3,19},{4,20},{5,21},{6,22},{7,23},{8,24},{9,... | collective-permute-start | bytes 2555912 | tf_op jit(solution)/shard_map/ppermute | solution.py:25
  104.9 23.3 %collective-permute-start.25 = (bf16[128,3328]{1,0:T(8,128)(2,1)S(1)}, bf16[128,3328]{1,0:T(8,128)(2,1)S(1)}, u32[]{:S(2)}, u32[]{:S(2)}) collective-permute-start(bf16[128,3328]{1,0:T(8,128)(2,1)S(1)} %collective-permute-done.23), channel_id=1, source_target_pairs={{0,32},{1,33},{2,34},{3,35},{4,36},{5,37},{6,38},{7,39},{8,40},{9,... | collective-permute-start | bytes 2555912 | tf_op jit(solution)/shard_map/ppermute | solution.py:25
  110.0 30.8 %collective-permute-start.27 = (bf16[128,3328]{1,0:T(8,128)(2,1)S(1)}, bf16[128,3328]{1,0:T(8,128)(2,1)S(1)}, u32[]{:S(2)}, u32[]{:S(2)}) collective-permute-start(bf16[128,3328]{1,0:T(8,128)(2,1)S(1)} %collective-permute-done.24), channel_id=1, source_target_pairs={{0,16},{1,17},{2,18},{3,19},{4,20},{5,21},{6,22},{7,23},{8,24},{9,... | collective-permute-start | bytes 2555912 | tf_op jit(solution)/shard_map/ppermute | solution.py:25
  110.1 27.3 %collective-permute-start.28 = (bf16[128,3328]{1,0:T(8,128)(2,1)S(1)}, bf16[128,3328]{1,0:T(8,128)(2,1)S(1)}, u32[]{:S(2)}, u32[]{:S(2)}) collective-permute-start(bf16[128,3328]{1,0:T(8,128)(2,1)S(1)} %collective-permute-done.24), channel_id=1, source_target_pairs={{0,32},{1,33},{2,34},{3,35},{4,36},{5,37},{6,38},{7,39},{8,40},{9,... | collective-permute-start | bytes 2555912 | tf_op jit(solution)/shard_map/ppermute | solution.py:25
  119.6 17.9 %collective-permute-start.15 = (bf16[128,3328]{1,0:T(8,128)(2,1)S(1)}, bf16[128,3328]{1,0:T(8,128)(2,1)S(1)}, u32[]{:S(2)}, u32[]{:S(2)}) collective-permute-start(bf16[128,3328]{1,0:T(8,128)(2,1)S(1)} %add_convert_fusion.8), channel_id=1, source_target_pairs={{0,1},{1,0},{2,3},{3,2},{4,5},{5,4},{6,7},{7,6},{8,9},{9,8},{10,11... | collective-permute-start | bytes 2555912 | tf_op jit(solution)/shard_map/ppermute | solution.py:25
  128.2 12.5 %collective-permute-start.26 = (bf16[128,3328]{1,0:T(8,128)(2,1)S(1)}, bf16[128,3328]{1,0:T(8,128)(2,1)S(1)}, u32[]{:S(2)}, u32[]{:S(2)}) collective-permute-start(bf16[128,3328]{1,0:T(8,128)(2,1)S(1)} %collective-permute-done.25), channel_id=1, source_target_pairs={{0,16},{1,17},{2,18},{3,19},{4,20},{5,21},{6,22},{7,23},{8,24},{9,... | collective-permute-start | bytes 2555912 | tf_op jit(solution)/shard_map/ppermute | solution.py:25
  137.4 16.6 %collective-permute-start.29 = (bf16[128,3328]{1,0:T(8,128)(2,1)S(1)}, bf16[128,3328]{1,0:T(8,128)(2,1)S(1)}, u32[]{:S(2)}, u32[]{:S(2)}) collective-permute-start(bf16[128,3328]{1,0:T(8,128)(2,1)S(1)} %collective-permute-done.28), channel_id=1, source_target_pairs={{0,16},{1,17},{2,18},{3,19},{4,20},{5,21},{6,22},{7,23},{8,24},{9,... | collective-permute-start | bytes 2555912 | tf_op jit(solution)/shard_map/ppermute | solution.py:25
  137.4 31.7 %slice-start = ((s8[6815744]{0:T(1024)(128)(4,1)}), s8[4194304]{0:T(1024)(128)(4,1)S(1)}, s32[]{:S(2)}) async-start(s8[6815744]{0:T(1024)(128)(4,1)} %bitcast.19), calls=%async_computation | async-start | bytes 8388608
  137.7 14.3 %collective-permute-start.16 = (bf16[128,3328]{1,0:T(8,128)(2,1)S(1)}, bf16[128,3328]{1,0:T(8,128)(2,1)S(1)}, u32[]{:S(2)}, u32[]{:S(2)}) collective-permute-start(bf16[128,3328]{1,0:T(8,128)(2,1)S(1)} %add_convert_fusion.7), channel_id=1, source_target_pairs={{0,2},{1,3},{2,0},{3,1},{4,6},{5,7},{6,4},{7,5},{8,10},{9,11},{10,... | collective-permute-start | bytes 2555912 | tf_op jit(solution)/shard_map/ppermute | solution.py:25
  140.8 28.3 %slice-start.1 = ((s8[6815744]{0:T(1024)(128)(4,1)}), s8[2621440]{0:T(1024)(128)(4,1)S(1)}, s32[]{:S(2)}) async-start(s8[6815744]{0:T(1024)(128)(4,1)} %bitcast.19), calls=%async_computation.1 | async-start | bytes 5242880
  152.3 12.8 %collective-permute-start.17 = (bf16[128,3328]{1,0:T(8,128)(2,1)S(1)}, bf16[128,3328]{1,0:T(8,128)(2,1)S(1)}, u32[]{:S(2)}, u32[]{:S(2)}) collective-permute-start(bf16[128,3328]{1,0:T(8,128)(2,1)S(1)} %add_convert_fusion.6), channel_id=1, source_target_pairs={{0,4},{1,5},{2,6},{3,7},{4,0},{5,1},{6,2},{7,3},{8,12},{9,13},{10,... | collective-permute-start | bytes 2555912 | tf_op jit(solution)/shard_map/ppermute | solution.py:25
  165.3 15.7 %collective-permute-start.18 = (bf16[128,3328]{1,0:T(8,128)(2,1)S(1)}, bf16[128,3328]{1,0:T(8,128)(2,1)S(1)}, u32[]{:S(2)}, u32[]{:S(2)}) collective-permute-start(bf16[128,3328]{1,0:T(8,128)(2,1)S(1)} %add_convert_fusion.5), channel_id=1, source_target_pairs={{0,8},{1,9},{2,10},{3,11},{4,12},{5,13},{6,14},{7,15},{8,0},{9,1},... | collective-permute-start | bytes 2555912 | tf_op jit(solution)/shard_map/ppermute | solution.py:25

commit v2 on v1

v2 whole, which is shorter than its diff:
```python
import functools

import jax
import jax.numpy as jnp
from jax import lax
from jax.experimental import pallas as pl
from jax.experimental.pallas import tpu as pltpu
from jax.sharding import PartitionSpec as P

HB = 256
SCALE = 64.0
AXES = ("x", "core", "z", "y")
BF16 = jnp.bfloat16
F32 = jnp.float32
VMEM = pl.BlockSpec(memory_space=pltpu.VMEM)
ANY = pl.BlockSpec(memory_space=pl.ANY)


def move(value, route, turn=0):
    nx, nc, nz, ny = (lax.axis_size(axis) for axis in AXES)

    def flat(x, c, z, y):
        return ((x % nx * nc + c) * nz + z) * ny + y

    pairs = [
        (flat(x, c, z, y), flat(*route(x, c, z, y)))
        for x in range(nx)
        for c in range(nc)
        for z in range(nz)
        for y in range(ny)
    ]
    return lax.ppermute(value, AXES, pairs[turn:] + pairs[:turn])


def swap(value, turn=0):
    return move(value, lambda x, c, z, y: (x, 1 - c, z, y), turn)


def forward(value):
    return move(value, lambda x, c, z, y: (x + 1 - 2 * c, c, z, y))


def backward(value):
    return move(value, lambda x, c, z, y: (x - 1 + 2 * c, c, z, y))


def across(value):
    return move(value, lambda x, c, z, y: (x + 2, c, z, y))


def hadamard(order):
    i = jnp.arange(order, dtype=jnp.int32)
    both = jnp.bitwise_and(i[:, None], i[None, :])
    return (1 - 2 * (lax.population_count(both) % 2)).astype(BF16)


def after(value, *earlier):
    return lax.optimization_barrier((value,) + earlier)[0]


def in_hbm(value):
    return pltpu.with_memory_space_constraint(value, pltpu.HBM)


def call(kernel, name, mib, in_specs, out_specs, out_shape, scratch_shapes=(), grid=()):
    return pl.pallas_call(
        kernel,
        grid=grid,
        in_specs=in_specs,
        out_specs=out_specs,
        out_shape=out_shape,
        scratch_shapes=scratch_shapes,
        compiler_params=pltpu.CompilerParams(vmem_limit_bytes=mib * 2**20),
        cost_estimate=pl.CostEstimate(flops=1, bytes_accessed=1, transcendentals=0),
        name=name,
    )


def split_kernel(grad_ref, kept_ref, given_ref, sems):
    x, core = lax.axis_index("x"), lax.axis_index("core")
    cols = kept_ref.shape[-1]
    opposite, here = lax.rem(x + 2, 4), x
    ahead, back = lax.rem(x + 5 - 2 * core, 4), lax.rem(x + 3 + 2 * core, 4)
    kept = ((opposite, core), (here, core), (ahead, core), (ahead, 1 - core))
    given = ((opposite, 1 - core), (here, 1 - core), (back, 1 - core), (back, core))
    copies = []
    for out, blocks in ((kept_ref, kept), (given_ref, given)):
        for i, (chip, its_core) in enumerate(blocks):
            part = pl.ds(pl.multiple_of((chip * 2 + its_core) * cols, cols), cols)
            copies.append(
                pltpu.make_async_copy(grad_ref.at[:, part], out.at[i], sems.at[len(copies)])
            )
            copies[-1].start()
    for copy in copies:
        copy.wait()


def split(out_grad, cols):
    shape = pltpu.VMEM((4, out_grad.shape[0], cols), BF16)
    return call(
        split_kernel, "split", 4, [ANY], [ANY] * 2, [shape] * 2, [pltpu.SemaphoreType.DMA((8,))]
    )(in_hbm(out_grad))


def pair_kernel(kept_ref, got_ref, opp_ref, own_ref, ahead_ref):
    tokens = kept_ref.shape[1]
    for i, (ref, row) in enumerate(
        ((opp_ref, 0), (own_ref, 0), (ahead_ref, 0), (ahead_ref, 2 * tokens))
    ):
        ref[row : row + tokens, :] = kept_ref[i]
        ref[row + tokens : row + 2 * tokens, :] = got_ref[i]


def pair(kept, got):
    tokens, cols = kept.shape[1:]
    return call(
        pair_kernel,
        "pair",
        4,
        [VMEM, VMEM],
        [VMEM] * 3,
        [pltpu.VMEM((rows * tokens, cols), BF16) for rows in (2, 2, 4)],
    )(kept, got)


def store_rows(value, outs):
    row = 0
    for out in outs:
        out[...] = value[row : row + out.shape[0]]
        row += out.shape[0]


def stream(hbm_ref, held_ref, sems):
    copies = []
    for i in range(hbm_ref.shape[0] // HB):
        part = pl.ds(i * HB, HB)
        copies.append(pltpu.make_async_copy(hbm_ref.at[part, :], held_ref.at[part, :], sems.at[i]))
        copies[-1].start()
    return copies


def streamed(ff, cols):
    return [pltpu.VMEM((ff, cols), BF16), pltpu.SemaphoreType.DMA((ff // HB,))]


def quantize_kernel(table_ref, weight_ref, inv_ref, grad_ref, turned_ref, keep_ref, *refs):
    outs, (held, sems) = refs[:-2], refs[-2:]
    copies = stream(weight_ref, held, sems)
    inv = inv_ref[...]
    step = (1.0 / SCALE) / inv
    for i, copy in enumerate(copies):
        part = pl.ds(i * HB, HB)
        copy.wait()
        raw_code = jnp.floor(held[part, :].astype(F32) * inv + 0.5)
        code = jnp.clip(raw_code, -8.0, 7.0)
        keep_ref[part, :] = jnp.where(raw_code == code, 1.0, 0.0).astype(BF16)
        turned = jnp.dot(table_ref[...], code.astype(BF16), preferred_element_type=F32)
        turned_ref[part, :] = (turned * step).astype(BF16)
        result = lax.dot_general(
            grad_ref[...], turned_ref[part, :], (((1,), (1,)), ((), ())), preferred_element_type=F32
        ).astype(BF16)
        store_rows(result, [out.at[:, part] for out in outs])


def quantize(table, weight, inv, grads, rows):
    ff, cols = weight.shape
    return call(
        quantize_kernel,
        "quantize",
        14,
        [VMEM, ANY, VMEM, VMEM],
        [VMEM] * (2 + len(rows)),
        [pltpu.VMEM((ff, cols), BF16)] * 2 + [pltpu.VMEM((count, ff), BF16) for count in rows],
        streamed(ff, cols),
    )(table, in_hbm(weight), inv, grads)


def product_kernel(count, *refs):
    grads, turned_ref, outs = refs[:count], refs[count], refs[count + 1 :]
    rows = sum(out.shape[0] for out in outs) // count
    for i in range(turned_ref.shape[0] // HB):
        part = pl.ds(i * HB, HB)
        result = lax.dot_general(
            jnp.concatenate([ref[:rows, :] for ref in grads]) if count > 1 else grads[0][:rows, :],
            turned_ref[part, :],
            (((1,), (1,)), ((), ())),
            preferred_element_type=F32,
        ).astype(BF16)
        store_rows(result, [out.at[:, part] for out in outs])


def product(grads, turned, rows):
    ff = turned.shape[0]
    return call(
        functools.partial(product_kernel, len(grads)),
        "product",
        8,
        [VMEM] * (len(grads) + 1),
        [VMEM] * len(rows),
        [pltpu.VMEM((size, ff), BF16) for size in rows],
    )(*grads, turned)


def add_kernel(first_rows, pieces, *refs):
    outs = refs[sum(pieces) :]
    terms, start = [], 0
    for count in pieces:
        terms.append(refs[start : start + count])
        start += count
    height = sum(out.shape[0] for out in outs)
    for i in range(outs[0].shape[1] // HB):
        part = pl.ds(i * HB, HB)
        total = None
        for row, term in zip(first_rows, terms):
            value = [ref[:, part] if len(term) > 1 else ref[row : row + height, part] for ref in term]
            value = value[0] if len(value) == 1 else jnp.concatenate(value)
            value = value.astype(F32)
            total = value if total is None else total + value
        store_rows(total.astype(BF16), [out.at[:, part] for out in outs])


def add(name, rows, *terms):
    first_rows = [term[1] if isinstance(term, tuple) else 0 for term in terms]
    terms = [
        term if isinstance(term, list) else [term[0] if isinstance(term, tuple) else term]
        for term in terms
    ]
    ff = terms[0][0].shape[1]
    flat = [piece for term in terms for piece in term]
    return call(
        functools.partial(add_kernel, tuple(first_rows), tuple(len(term) for term in terms)),
        name,
        6,
        [VMEM] * len(flat),
        [VMEM] * len(rows),
        [pltpu.VMEM((count, ff), BF16) for count in rows],
    )(*flat)


def my_sign(step):
    core, z, y = (lax.axis_index(axis) for axis in ("core", "z", "y"))
    bit, y_first = mix_axis(step)
    place = jnp.where((core == 0) == y_first, y, z)
    return jnp.where(jnp.bitwise_and(place, bit) == 0, 1.0, -1.0).astype(F32)


def mix_kernel(step, *refs):
    sign = my_sign(step)
    half = len(refs) // 2
    values, partners, out_ref = refs[:half], refs[half:-1], refs[-1]
    row = 0
    for value_ref, partner_ref in zip(values, partners):
        rows = pl.ds(row, value_ref.shape[0])
        row += value_ref.shape[0]
        for i in range(value_ref.shape[1] // HB):
            part = pl.ds(i * HB, HB)
            total = value_ref[:, part].astype(F32) * sign + partner_ref[:, part].astype(F32)
            out_ref[rows, part] = total.astype(BF16)


def mix(name, step, values, partners, last=False):
    shape = (sum(value.shape[0] for value in values), values[0].shape[1])
    return call(
        functools.partial(mix_kernel, step),
        name,
        6,
        [VMEM] * (2 * len(values)),
        VMEM,
        jax.ShapeDtypeStruct(shape, BF16) if last else pltpu.VMEM(shape, BF16),
    )(*values, *partners)


def rotate_kernel(step, table_ref, value_ref, partner_ref, rotated_ref):
    sign = my_sign(step)
    for i in range(value_ref.shape[1] // HB):
        part = pl.ds(i * HB, HB)
        mix = value_ref[:, part].astype(F32) * sign + partner_ref[:, part].astype(F32)
        turned = lax.dot_general(
            table_ref[...], mix.astype(BF16), (((1,), (1,)), ((), ())), preferred_element_type=F32
        )
        rotated_ref[part, :] = (turned * (1.0 / SCALE)).astype(BF16)


def rotate(table, step, value, partner):
    tokens, ff = value.shape
    return call(
        functools.partial(rotate_kernel, step),
        "rotate",
        8,
        [VMEM] * 3,
        VMEM,
        pltpu.VMEM((ff, tokens), BF16),
    )(table, value, partner)


def partial_sum(rotated, grads, part):
    left = jnp.concatenate([ref[part, :] for ref in rotated], axis=1)
    return jnp.dot(left, grads, preferred_element_type=F32)


def early_kernel(count, pieces, *refs):
    rotated, grads = refs[:count], refs[count:-2]
    out_ref, all_grads = refs[-2:]
    tokens = rotated[0].shape[1]
    row = 0
    for ref, piece in zip(grads, pieces):
        rows = 2 * tokens // piece
        all_grads[pl.ds(row, rows), :] = ref[:rows, :]
        row += rows
    for i in range(out_ref.shape[0] // HB):
        part = pl.ds(i * HB, HB)
        out_ref[part, :] = partial_sum(rotated, all_grads[...], part)


def early_product(rotated, grads):
    count = len(rotated)
    flat = [piece for chip in grads for piece in chip]
    pieces = tuple(len(chip) for chip in grads for _ in chip)
    ff, cols = rotated[0].shape[0], flat[0].shape[1]
    return call(
        functools.partial(early_kernel, count, pieces),
        "early_product",
        10,
        [VMEM] * (count + len(flat)),
        VMEM,
        pltpu.VMEM((ff, cols), F32),
        [pltpu.VMEM((count * rotated[0].shape[1], cols), BF16)],
    )(*rotated, *flat)


def late_kernel(mine_ref, other_ref, grad_ref, keep_ref, early_ref, out_ref, held, sems):
    copies = []
    for i in range(early_ref.shape[0] // HB):
        part = pl.ds(i * HB, HB)
        total = early_ref[part, :] + partial_sum((mine_ref, other_ref), grad_ref[...], part)
        held[part, :] = jnp.where(keep_ref[part, :].astype(F32) > 0.0, total, 0.0).astype(BF16)
        copies.append(pltpu.make_async_copy(held.at[part, :], out_ref.at[part, :], sems.at[i]))
        copies[-1].start()
    for copy in copies:
        copy.wait()


def late_product(mine, other, grads, keep, early):
    return call(
        late_kernel,
        "late_product",
        14,
        [VMEM] * 5,
        ANY,
        jax.ShapeDtypeStruct(early.shape, BF16),
        streamed(*early.shape),
    )(mine, other, grads, keep, early)


def mix_axis(step):
    return 1 << (step % 2), step < 2


def partner(value, step):
    bit, y_first = mix_axis(step)

    def route(x, c, z, y):
        return (x, c, z, y ^ bit) if (c == 0) == y_first else (x, c, z ^ bit, y)

    return move(value, route)


def on_device(hidden, out_grad, weight, inv_scale):
    table = hadamard(HB)
    inv = inv_scale[None, :]
    tokens = hidden.shape[0]
    half = tokens // 2
    whole, halves = (tokens,), (half, half)

    kept, given = split(after(out_grad, table), weight.shape[1])
    got = partner(hidden, 0)
    to_opp, own, to_ahead = pair(kept, swap(given))
    opp, bwd = across(to_opp), forward(to_ahead)
    turned, keep, own_mine, own_other = quantize(table, weight, inv, own, whole * 2)
    own_other = swap(own_other, 1)

    hid = mix("mix", 0, [after(hidden, turned)], [got])
    got = partner(hid, 1)
    bwd = after(bwd, hid)
    fwd = [swap(bwd[(2 + j) * tokens : (3 + j) * tokens], 2 + j) for j in (0, 1)]
    bwd_parts = product([bwd], turned, halves * 2)
    bwd_mine = [swap(bwd_parts[j], 4 + j) for j in (0, 1)]
    bwd_other = [swap(bwd_parts[2 + j], 6 + j) for j in (0, 1)]
    fwd_other, *fwd_mine = product([after(fwd[0], bwd_parts[0]), fwd[1]], turned, whole + halves)
    opp_mine, *opp_other = product([after(opp, fwd_other)], turned, whole + halves)
    opp_other = [swap(opp_other[j], 8 + j) for j in (0, 1)]
    own_sum = add("add_own", halves, after(own_mine, opp_mine), own_other)
    (second_send,) = add("add_second", whole, after(fwd_other, own_sum[0]), bwd_mine)
    second = forward(second_send)
    first = []
    last = second_send
    for j in (0, 1):
        (last,) = add("add_first", (half,), (after(opp_mine, last), j * half), opp_other[j])
        first.append(forward(last))
    hid = mix("mix", 1, [after(hid, last)], [got])
    got = partner(hid, 2)
    second = after(second, hid)
    second_other = swap(second, 10)
    third = []
    last = second
    for j in (0, 1):
        (last,) = add("add_third", (half,), after(first[j], last), fwd_mine[j], bwd_other[j])
        third.append(forward(last))
    hid = mix("mix", 2, [after(hid, last)], [got])
    got = partner(hid, 3)
    last = hid

    values, partners = [], []
    for j in (0, 1):
        (last,) = add(
            "add_grad", (half,), own_sum[j], (second_other, j * half), after(third[j], last)
        )
        values.append(last)
        partners.append(partner(last, 0))
        if j == 0:
            last = rotated = rotate(table, 3, after(hid, last), got)
            bwd_a, fwd_a = forward(rotated), backward(rotated)
            other = swap(rotated, 11)
    for step in range(3):
        for j in (0, 1):
            last = mix("mix_grad", step, [after(values[j], last)], [partners[j]])
            values[j] = last
            partners[j] = partner(last, step + 1)
        if step == 0:
            bwd_a = after(bwd_a, last)
            opp_a = forward(bwd_a)
            fwd_b = swap(bwd_a, 12)
        if step == 1:
            fwd_a = after(fwd_a, last)
            bwd_b = swap(fwd_a, 13)
            last = early = early_product(
                [rotated, other, bwd_a, bwd_b, fwd_b, fwd_a], [[own], [bwd], fwd]
            )
    opp_a = after(opp_a, last)
    weight_grad = late_product(opp_a, swap(opp_a, 14), opp, keep, early)
    hidden_grad = mix("mix_last", 3, [after(values[0], weight_grad), values[1]], partners, last=True)
    return hidden_grad, weight_grad


def solution(mesh):
    grid = jax.sharding.Mesh(mesh.devices.reshape(4, 2, 4, 4), AXES)
    dp, tensor = ("x", "core"), ("z", "y")
    in_specs = (P(dp, tensor), P(dp, None), P(tensor, dp), P(dp))
    out_specs = (P(dp, tensor), P(tensor, dp))
    return jax.shard_map(
        on_device, mesh=grid, in_specs=in_specs, out_specs=out_specs, check_vma=False
    )
```

time: 182 us -> 135 us (0.74)
  matrix products: 34.2 us -> 0 us
  Pallas kernels: 0 us -> 31.3 us
  other arithmetic: 19.4 us -> 0.15 us
  waiting for transfers between devices: 75 us -> 58.9 us
  local copies, waits for them, and re-layouts: 16.2 us -> 0.73 us
  starting transfers between devices: 36.3 us -> 42.8 us
    dot_general x7 -> x0, matrix products: 34.2 us -> none  [the longest x4 14.1 us: product(): lax.dot_general(jnp.concatenate([mine, other]), turned, (((1,), (1,)), ((...]
    pallas_call x0 -> x27, Pallas kernels: none -> 31.3 us  [the longest x1 10 us: quantize(): call(quantize_kernel, 'quantize', 14, [VMEM, ANY, VMEM, VMEM], [VMEM] * (...]
    convert_element_type x13 -> x1, other arithmetic: 19.4 us -> 0.15 us  [hadamard(): return (1 - 2 * (lax.population_count(both) % 2)).astype(BF16)]
    ppermute x30 -> x37, waiting for transfers between devices: 75 us -> 58.9 us  [move(): return lax.ppermute(value, AXES, pairs[turn:] + pairs[:turn])]
    unnamed x38 -> x4, local copies, waits for them, and re-layouts: 10.3 us -> 0.69 us
    ppermute x30 -> x37, starting transfers between devices: 36.3 us -> 42.8 us  [move(): return lax.ppermute(value, AXES, pairs[turn:] + pairs[:turn])]
    reshape x2 -> x0, local copies, waits for them, and re-layouts: 3.07 us -> none  [the longest x1 2.06 us: on_device(): rotated = (rotated * scaling).astype(BF16).reshape(tokens, ff)]
    dynamic_slice x2 -> x0, local copies, waits for them, and re-layouts: 2.51 us -> none  [the longest x1 1.54 us: columns(): return lax.dynamic_slice(out_grad, (0, chip * 2 * cols), (tokens, 2 * cols))]
  transfers between devices with their start and end apart: 30 -> 37, of which waited for: 9 -> 17; matrix products, arithmetic and copies ran while one was open for 37% -> 0% of each run, Pallas kernels for 0% -> 21%
where the time goes in v2:
time: 135 us
  waiting for transfers between devices  58.9 us (44%)
  starting transfers between devices  42.8 us (32%)
  Pallas kernels  31.3 us (23%)
    ppermute x37, waiting for transfers between devices, move(): return lax.ppermute(value, AXES, pairs[turn:] + pairs[:turn])  58.9 us
    ppermute x37, starting transfers between devices, move(): return lax.ppermute(value, AXES, pairs[turn:] + pairs[:turn])  42.8 us
    pallas_call x1, Pallas kernels, quantize(): call(quantize_kernel, 'quantize', 14, [VMEM, ANY, VMEM, VMEM], [VMEM] * (...  10 us
    pallas_call x3, Pallas kernels, product(): call(functools.partial(product_kernel, len(grads)), 'product', 8, [VMEM]...  5.87 us
    pallas_call x1, Pallas kernels, early_product(): call(functools.partial(early_kernel, count, pieces), 'early_product', 10,...  5.46 us
    pallas_call x1, Pallas kernels, late_product(): call(late_kernel, 'late_product', 14, [VMEM] * 5, ANY, jax.ShapeDtypeStru...  3.53 us
    pallas_call x10, Pallas kernels, mix(): call(functools.partial(mix_kernel, step), name, 6, [VMEM] * (2 * len(valu...  2.79 us
  transfers between devices with their start and end apart: 37, of which 17 were waited for; matrix products, arithmetic and copies ran while one was open for 0% of the time, Pallas kernels for 21%

profile of v2, /device:TPU:0, one launch (start us, length us, event | category | flops | bytes accessed | tf_op | source)
XLA Modules:
  0.0 134.8 jit_solution(1354089623763995790)
XLA Ops:
  0.6 0.2 fusion.3.table_ref
  0.8 1.7 %split.1 = (bf16[4,128,1024]{2,1,0:T(8,128)(2,1)S(1)}, bf16[4,128,1024]{2,1,0:T(8,128)(2,1)S(1)}) custom-call(bf16[128,8192]{1,0:T(8,128)(2,1)} %grad_ref), custom_call_target="tpu_custom_call" | custom-call | flops 1 | bytes 1 | tf_op jit(solution)/shard_map/split/pallas_call | solution.py:100
  2.6 2.6 %collective-permute-done.got_ref = bf16[4,128,1024]{2,1,0:T(8,128)(2,1)S(1)} collective-permute-done((bf16[4,128,1024]{2,1,0:T(8,128)(2,1)S(1)}, bf16[4,128,1024]{2,1,0:T(8,128)(2,1)S(1)}, u32[]{:S(2)}, u32[]{:S(2)}) %collective-permute-start) | collective-permute-done | bytes 1048608 | tf_op jit(solution)/shard_map/ppermute | solution.py:32
  5.4 1.6 %collective-permute-start.2 = (bf16[512,1024]{1,0:T(8,128)(2,1)S(1)}, bf16[512,1024]{1,0:T(8,128)(2,1)S(1)}, u32[]{:S(2)}, u32[]{:S(2)}) collective-permute-start(bf16[512,1024]{1,0:T(8,128)(2,1)S(1)} %get-tuple-element.56), channel_id=1, source_target_pairs={{0,32},{1,33},{2,34},{3,35},{4,36},{5,37},{6,38},{7,39},{8,40},{9,... | collective-permute-start | bytes 3145736 | tf_op jit(solution)/shard_map/ppermute | solution.py:32
  7.0 1.6 %collective-permute-start.3 = (bf16[128,3328]{1,0:T(8,128)(2,1)}, bf16[128,3328]{1,0:T(8,128)(2,1)S(1)}, u32[]{:S(2)}, u32[]{:S(2)}) collective-permute-start(bf16[128,3328]{1,0:T(8,128)(2,1)} %refs_0_), channel_id=1, source_target_pairs={{0,1},{1,0},{2,3},{3,2},{4,5},{5,4},{6,7},{7,6},{8,9},{9,8},{10,11... | collective-permute-start | bytes 2555912 | tf_op jit(solution)/shard_map/ppermute | solution.py:32
  8.6 0.7 copy-done.1
  9.3 10.0 %quantize.1 = (bf16[3328,1024]{1,0:T(8,128)(2,1)S(1)}, bf16[3328,1024]{1,0:T(8,128)(2,1)S(1)}, bf16[128,3328]{1,0:T(8,128)(2,1)S(1)}, bf16[128,3328]{1,0:T(8,128)(2,1)S(1)}) custom-call(bf16[256,256]{1,0:T(8,128)(2,1)S(1)} %fusion.3.table_ref, bf16[3328,1024]{1,0:T(8,128)(2,1)} %weight_ref.1, f32[1,1024]{1,0:T(1,128)S(1)} %bitcast.1, ...), custom_call_target="tpu_custom_call" | custom-call | flops 1 | bytes 1 | tf_op jit(solution)/shard_map/quantize/pallas_call | solution.py:167
  19.3 1.3 collective-permute-start.6
  20.6 0.3 mix.3.refs_0_
  20.8 0.6 collective-permute-done.2.refs_0_.refs_7_
  21.6 0.5 collective-permute-start.5
  22.1 1.9 %collective-permute-start.1 = (bf16[256,1024]{1,0:T(8,128)(2,1)S(1)}, bf16[256,1024]{1,0:T(8,128)(2,1)S(1)}, u32[]{:S(2)}, u32[]{:S(2)}) collective-permute-start(bf16[256,1024]{1,0:T(8,128)(2,1)S(1)} %get-tuple-element.55), channel_id=1, source_target_pairs={{0,64},{1,65},{2,66},{3,67},{4,68},{5,69},{6,70},{7,71},{8,72},{9,... | collective-permute-start | bytes 1572872 | tf_op jit(solution)/shard_map/ppermute | solution.py:32
  24.0 2.0 %product.3 = (bf16[64,3328]{1,0:T(8,128)(2,1)S(1)}, bf16[64,3328]{1,0:T(8,128)(2,1)S(1)}, bf16[64,3328]{1,0:T(8,128)(2,1)S(1)}, bf16[64,3328]{1,0:T(8,128)(2,1)S(1)}) custom-call(bf16[512,1024]{1,0:T(8,128)(2,1)S(1)} %collective-permute-done.2.refs_0_.refs_7_, bf16[3328,1024]{1,0:T(8,128)(2,1)S(1)} %get-tuple-element.57.refs_1_.refs_2_), custom_call_target="tpu_custom_call" | custom-call | flops 1 | bytes 1 | tf_op jit(solution)/shard_map/product/pallas_call | solution.py:194
  26.0 0.5 collective-permute-start.8
  26.5 3.2 %collective-permute-start.12 = (bf16[128,3328]{1,0:T(8,128)(2,1)S(1)}, bf16[128,3328]{1,0:T(8,128)(2,1)S(1)}, u32[]{:S(2)}, u32[]{:S(2)}) collective-permute-start(bf16[128,3328]{1,0:T(8,128)(2,1)S(1)} %mix.3.refs_0_), channel_id=1, source_target_pairs={{0,2},{1,3},{2,0},{3,1},{4,6},{5,7},{6,4},{7,5},{8,10},{9,11},{10,... | collective-permute-start | bytes 2555912 | tf_op jit(solution)/shard_map/ppermute | solution.py:32
  29.7 2.0 %product.4 = (bf16[128,3328]{1,0:T(8,128)(2,1)S(1)}, bf16[64,3328]{1,0:T(8,128)(2,1)S(1)}, bf16[64,3328]{1,0:T(8,128)(2,1)S(1)}) custom-call(bf16[128,1024]{1,0:T(8,128)(2,1)S(1)} %collective-permute-done.4.refs_0_.refs_8_, bf16[128,1024]{1,0:T(8,128)(2,1)S(1)} %collective-permute-done.5.refs_1_.refs_9_, bf16[3328,1024]{1,0:T(8,128)(2,1)S(1)} %get-tuple-element.57.refs_1_.refs_2_), custom_call_target="tpu_custom_call" | custom-call | flops 1 | bytes 1 | tf_op jit(solution)/shard_map/product/pallas_call | solution.py:194
  31.7 5.8 %collective-permute-done.1.refs_0_.grad_ref = bf16[256,1024]{1,0:T(8,128)(2,1)S(1)} collective-permute-done((bf16[256,1024]{1,0:T(8,128)(2,1)S(1)}, bf16[256,1024]{1,0:T(8,128)(2,1)S(1)}, u32[]{:S(2)}, u32[]{:S(2)}) %collective-permute-start.1) | collective-permute-done | bytes 524320 | tf_op jit(solution)/shard_map/ppermute | solution.py:32
  37.5 2.0 %product.5 = (bf16[128,3328]{1,0:T(8,128)(2,1)S(1)}, bf16[64,3328]{1,0:T(8,128)(2,1)S(1)}, bf16[64,3328]{1,0:T(8,128)(2,1)S(1)}) custom-call(bf16[256,1024]{1,0:T(8,128)(2,1)S(1)} %collective-permute-done.1.refs_0_.grad_ref, bf16[3328,1024]{1,0:T(8,128)(2,1)S(1)} %get-tuple-element.57.refs_1_.refs_2_), custom_call_target="tpu_custom_call" | custom-call | flops 1 | bytes 1 | tf_op jit(solution)/shard_map/product/pallas_call | solution.py:194
  39.5 0.2 add_own.1
  39.8 0.5 collective-permute-start.11
  40.3 0.2 add_second.1
  40.5 0.4 collective-permute-start.9
  40.9 0.6 collective-permute-done.10.refs_1_
  41.6 0.5 collective-permute-done.11.refs_1_
  42.3 0.3 mix.4.refs_0_
  42.5 2.1 %collective-permute-start.19 = (bf16[128,3328]{1,0:T(8,128)(2,1)S(1)}, bf16[128,3328]{1,0:T(8,128)(2,1)S(1)}, u32[]{:S(2)}, u32[]{:S(2)}) collective-permute-start(bf16[128,3328]{1,0:T(8,128)(2,1)S(1)} %mix.4.refs_0_), channel_id=1, source_target_pairs={{0,4},{1,5},{2,6},{3,7},{4,0},{5,1},{6,2},{7,3},{8,12},{9,13},{10,... | collective-permute-start | bytes 2555912 | tf_op jit(solution)/shard_map/ppermute | solution.py:32
  44.6 0.3 collective-permute-start.14
  44.9 0.6 collective-permute-start.15
  45.5 0.9 collective-permute-start.17
  46.4 8.1 %collective-permute-done.9 = bf16[128,3328]{1,0:T(8,128)(2,1)S(1)} collective-permute-done((bf16[128,3328]{1,0:T(8,128)(2,1)S(1)}, bf16[128,3328]{1,0:T(8,128)(2,1)S(1)}, u32[]{:S(2)}, u32[]{:S(2)}) %collective-permute-start.9) | collective-permute-done | bytes 852000 | tf_op jit(solution)/shard_map/ppermute | solution.py:32
  54.5 4.6 %collective-permute-done.14.refs_0_ = bf16[64,3328]{1,0:T(8,128)(2,1)S(1)} collective-permute-done((bf16[64,3328]{1,0:T(8,128)(2,1)S(1)}, bf16[64,3328]{1,0:T(8,128)(2,1)S(1)}, u32[]{:S(2)}, u32[]{:S(2)}) %collective-permute-start.14) | collective-permute-done | bytes 426016 | tf_op jit(solution)/shard_map/ppermute | solution.py:32
  59.0 0.2 add_third.2
  59.2 4.4 %collective-permute-done.17.refs_0_ = bf16[64,3328]{1,0:T(8,128)(2,1)S(1)} collective-permute-done((bf16[64,3328]{1,0:T(8,128)(2,1)S(1)}, bf16[64,3328]{1,0:T(8,128)(2,1)S(1)}, u32[]{:S(2)}, u32[]{:S(2)}) %collective-permute-start.17) | collective-permute-done | bytes 426016 | tf_op jit(solution)/shard_map/ppermute | solution.py:32
  63.6 0.2 add_third.3
  63.8 0.3 mix.5.value_ref
  64.0 4.0 %collective-permute-start.21 = (bf16[128,3328]{1,0:T(8,128)(2,1)S(1)}, bf16[128,3328]{1,0:T(8,128)(2,1)S(1)}, u32[]{:S(2)}, u32[]{:S(2)}) collective-permute-start(bf16[128,3328]{1,0:T(8,128)(2,1)S(1)} %mix.5.value_ref), channel_id=1, source_target_pairs={{0,8},{1,9},{2,10},{3,11},{4,12},{5,13},{6,14},{7,15},{8,0},{9,1},... | collective-permute-start | bytes 2555912 | tf_op jit(solution)/shard_map/ppermute | solution.py:32
  68.1 0.6 collective-permute-start.20
  68.6 8.8 %collective-permute-done.16.refs_2_ = bf16[64,3328]{1,0:T(8,128)(2,1)S(1)} collective-permute-done((bf16[64,3328]{1,0:T(8,128)(2,1)S(1)}, bf16[64,3328]{1,0:T(8,128)(2,1)S(1)}, u32[]{:S(2)}, u32[]{:S(2)}) %collective-permute-start.16) | collective-permute-done | bytes 426016 | tf_op jit(solution)/shard_map/ppermute | solution.py:32
  77.4 0.2 add_grad.2.refs_0_
  77.6 1.7 %collective-permute-start.22 = (bf16[64,3328]{1,0:T(8,128)(2,1)S(1)}, bf16[64,3328]{1,0:T(8,128)(2,1)S(1)}, u32[]{:S(2)}, u32[]{:S(2)}) collective-permute-start(bf16[64,3328]{1,0:T(8,128)(2,1)S(1)} %add_grad.2.refs_0_), channel_id=1, source_target_pairs={{0,1},{1,0},{2,3},{3,2},{4,5},{5,4},{6,7},{7,6},{8,9},{9,8},{10,11... | collective-permute-start | bytes 1277960 | tf_op jit(solution)/shard_map/ppermute | solution.py:32
  79.2 2.5 %collective-permute-done.21.partner_ref = bf16[128,3328]{1,0:T(8,128)(2,1)S(1)} collective-permute-done((bf16[128,3328]{1,0:T(8,128)(2,1)S(1)}, bf16[128,3328]{1,0:T(8,128)(2,1)S(1)}, u32[]{:S(2)}, u32[]{:S(2)}) %collective-permute-start.21) | collective-permute-done | bytes 852000 | tf_op jit(solution)/shard_map/ppermute | solution.py:32
  81.7 0.6 rotate.1.refs_0_
  82.4 0.2 add_grad.3.refs_0_
  82.5 2.6 %collective-permute-start.23 = (bf16[64,3328]{1,0:T(8,128)(2,1)S(1)}, bf16[64,3328]{1,0:T(8,128)(2,1)S(1)}, u32[]{:S(2)}, u32[]{:S(2)}) collective-permute-start(bf16[64,3328]{1,0:T(8,128)(2,1)S(1)} %add_grad.3.refs_0_), channel_id=1, source_target_pairs={{0,1},{1,0},{2,3},{3,2},{4,5},{5,4},{6,7},{7,6},{8,9},{9,8},{10,11... | collective-permute-start | bytes 1277960 | tf_op jit(solution)/shard_map/ppermute | solution.py:32
  85.1 2.0 %collective-permute-start.26 = (bf16[3328,128]{1,0:T(8,128)(2,1)S(1)}, bf16[3328,128]{1,0:T(8,128)(2,1)S(1)}, u32[]{:S(2)}, u32[]{:S(2)}) collective-permute-start(bf16[3328,128]{1,0:T(8,128)(2,1)S(1)} %rotate.1.refs_0_), channel_id=1, source_target_pairs={{0,32},{1,33},{2,34},{3,35},{4,36},{5,37},{6,38},{7,39},{8,40},{9,... | collective-permute-start | bytes 2555912 | tf_op jit(solution)/shard_map/ppermute | solution.py:32
  87.3 4.0 %collective-permute-start.24 = (bf16[64,3328]{1,0:T(8,128)(2,1)S(1)}, bf16[64,3328]{1,0:T(8,128)(2,1)S(1)}, u32[]{:S(2)}, u32[]{:S(2)}) collective-permute-start(bf16[64,3328]{1,0:T(8,128)(2,1)S(1)} %mix_grad.6.refs_0_), channel_id=1, source_target_pairs={{0,2},{1,3},{2,0},{3,1},{4,6},{5,7},{6,4},{7,5},{8,10},{9,11},{10,... | collective-permute-start | bytes 1277960 | tf_op jit(solution)/shard_map/ppermute | solution.py:32
  91.3 0.1 mix_grad.7.refs_0_
  91.4 5.5 %collective-permute-start.28 = (bf16[64,3328]{1,0:T(8,128)(2,1)S(1)}, bf16[64,3328]{1,0:T(8,128)(2,1)S(1)}, u32[]{:S(2)}, u32[]{:S(2)}) collective-permute-start(bf16[64,3328]{1,0:T(8,128)(2,1)S(1)} %mix_grad.7.refs_0_), channel_id=1, source_target_pairs={{0,2},{1,3},{2,0},{3,1},{4,6},{5,7},{6,4},{7,5},{8,10},{9,11},{10,... | collective-permute-start | bytes 1277960 | tf_op jit(solution)/shard_map/ppermute | solution.py:32
  97.0 2.7 %collective-permute-done.24.refs_1_ = bf16[64,3328]{1,0:T(8,128)(2,1)S(1)} collective-permute-done((bf16[64,3328]{1,0:T(8,128)(2,1)S(1)}, bf16[64,3328]{1,0:T(8,128)(2,1)S(1)}, u32[]{:S(2)}, u32[]{:S(2)}) %collective-permute-start.24) | collective-permute-done | bytes 426016 | tf_op jit(solution)/shard_map/ppermute | solution.py:32
  99.9 4.4 %collective-permute-done.28.refs_1_ = bf16[64,3328]{1,0:T(8,128)(2,1)S(1)} collective-permute-done((bf16[64,3328]{1,0:T(8,128)(2,1)S(1)}, bf16[64,3328]{1,0:T(8,128)(2,1)S(1)}, u32[]{:S(2)}, u32[]{:S(2)}) %collective-permute-start.28) | collective-permute-done | bytes 426016 | tf_op jit(solution)/shard_map/ppermute | solution.py:32
  104.3 0.1 mix_grad.9.refs_0_
  104.5 0.5 collective-permute-start.30
  105.0 1.8 %collective-permute-start.31 = (bf16[64,3328]{1,0:T(8,128)(2,1)S(1)}, bf16[64,3328]{1,0:T(8,128)(2,1)S(1)}, u32[]{:S(2)}, u32[]{:S(2)}) collective-permute-start(bf16[64,3328]{1,0:T(8,128)(2,1)S(1)} %mix_grad.8.refs_0_), channel_id=1, source_target_pairs={{0,4},{1,5},{2,6},{3,7},{4,0},{5,1},{6,2},{7,3},{8,12},{9,13},{10,... | collective-permute-start | bytes 1277960 | tf_op jit(solution)/shard_map/ppermute | solution.py:32
  106.8 0.3 collective-permute-start.33
  107.1 1.0 collective-permute-done.30.refs_4_
  108.1 5.5 %early_product.1.early_ref = f32[3328,1024]{1,0:T(8,128)S(1)} custom-call(bf16[3328,128]{1,0:T(8,128)(2,1)S(1)} %rotate.1.refs_0_, bf16[3328,128]{1,0:T(8,128)(2,1)S(1)} %collective-permute-done.25.refs_1_, bf16[3328,128]{1,0:T(8,128)(2,1)S(1)} %collective-permute-done.26.refs_2_, bf16[3328,128]{1,0:T(8,128)(2,1)S(1)} %collective-permute-done.29.refs_3_, ...), custom_call_target="tpu_custom_call" | custom-call | flops 1 | bytes 1 | tf_op jit(solution)/shard_map/early_product/pallas_call | solution.py:320
  113.6 0.1 mix_grad.10.refs_0_
  113.7 4.0 %collective-permute-done.33.refs_1_ = bf16[64,3328]{1,0:T(8,128)(2,1)S(1)} collective-permute-done((bf16[64,3328]{1,0:T(8,128)(2,1)S(1)}, bf16[64,3328]{1,0:T(8,128)(2,1)S(1)}, u32[]{:S(2)}, u32[]{:S(2)}) %collective-permute-start.33) | collective-permute-done | bytes 426016 | tf_op jit(solution)/shard_map/ppermute | solution.py:32
  117.9 1.1 collective-permute-done.32.mine_ref
  118.9 4.0 %collective-permute-start.36 = (bf16[64,3328]{1,0:T(8,128)(2,1)S(1)}, bf16[64,3328]{1,0:T(8,128)(2,1)S(1)}, u32[]{:S(2)}, u32[]{:S(2)}) collective-permute-start(bf16[64,3328]{1,0:T(8,128)(2,1)S(1)} %mix_grad.11.refs_1_), channel_id=1, source_target_pairs={{0,8},{1,9},{2,10},{3,11},{4,12},{5,13},{6,14},{7,15},{8,0},{9,1},... | collective-permute-start | bytes 1277960 | tf_op jit(solution)/shard_map/ppermute | solution.py:32
  123.0 3.5 %late_product.1 = bf16[3328,1024]{1,0:T(8,128)(2,1)} custom-call(bf16[3328,128]{1,0:T(8,128)(2,1)S(1)} %collective-permute-done.32.mine_ref, bf16[3328,128]{1,0:T(8,128)(2,1)S(1)} %collective-permute-done.34.other_ref, bf16[256,1024]{1,0:T(8,128)(2,1)S(1)} %collective-permute-done.1.refs_0_.grad_ref, bf16[3328,1024]{1,0:T(8,128)(2,1)S(1)} %get-tuple-element.96.keep_ref, ...), custom_call_target="tpu_custom_call" | custom-call | flops 1 | bytes 1 | tf_op jit(solution)/shard_map/late_product/pallas_call | solution.py:344
  126.5 2.5 %collective-permute-done.36.refs_3_ = bf16[64,3328]{1,0:T(8,128)(2,1)S(1)} collective-permute-done((bf16[64,3328]{1,0:T(8,128)(2,1)S(1)}, bf16[64,3328]{1,0:T(8,128)(2,1)S(1)}, u32[]{:S(2)}, u32[]{:S(2)}) %collective-permute-start.36) | collective-permute-done | bytes 426016 | tf_op jit(solution)/shard_map/ppermute | solution.py:32
  129.0 4.6 %collective-permute-done.35.refs_2_ = bf16[64,3328]{1,0:T(8,128)(2,1)S(1)} collective-permute-done((bf16[64,3328]{1,0:T(8,128)(2,1)S(1)}, bf16[64,3328]{1,0:T(8,128)(2,1)S(1)}, u32[]{:S(2)}, u32[]{:S(2)}) %collective-permute-start.35) | collective-permute-done | bytes 426016 | tf_op jit(solution)/shard_map/ppermute | solution.py:32
  133.6 1.2 mix_last.1
  (43 shorter events, 1.3 us)
Async XLA Ops:
  0.6 20.0 %copy-start = (bf16[128,3328]{1,0:T(8,128)(2,1)S(1)}, bf16[128,3328]{1,0:T(8,128)(2,1)}, u32[]{:S(2)}) copy-start(bf16[128,3328]{1,0:T(8,128)(2,1)} %refs_0_) | copy-start | bytes 2555908
  2.5 2.7 %collective-permute-start = (bf16[4,128,1024]{2,1,0:T(8,128)(2,1)S(1)}, bf16[4,128,1024]{2,1,0:T(8,128)(2,1)S(1)}, u32[]{:S(2)}, u32[]{:S(2)}) collective-permute-start(bf16[4,128,1024]{2,1,0:T(8,128)(2,1)S(1)} %get-tuple-element.52), channel_id=1, source_target_pairs={{0,16},{1,17},{2,18},{3,19},{4,20},{5,21},{6,22},{7,23},{8,24},{9,... | collective-permute-start | bytes 3145736 | tf_op jit(solution)/shard_map/ppermute | solution.py:32
  5.4 16.1 %collective-permute-start.2 = (bf16[512,1024]{1,0:T(8,128)(2,1)S(1)}, bf16[512,1024]{1,0:T(8,128)(2,1)S(1)}, u32[]{:S(2)}, u32[]{:S(2)}) collective-permute-start(bf16[512,1024]{1,0:T(8,128)(2,1)S(1)} %get-tuple-element.56), channel_id=1, source_target_pairs={{0,32},{1,33},{2,34},{3,35},{4,36},{5,37},{6,38},{7,39},{8,40},{9,... | collective-permute-start | bytes 3145736 | tf_op jit(solution)/shard_map/ppermute | solution.py:32
  7.0 13.6 %collective-permute-start.3 = (bf16[128,3328]{1,0:T(8,128)(2,1)}, bf16[128,3328]{1,0:T(8,128)(2,1)S(1)}, u32[]{:S(2)}, u32[]{:S(2)}) collective-permute-start(bf16[128,3328]{1,0:T(8,128)(2,1)} %refs_0_), channel_id=1, source_target_pairs={{0,1},{1,0},{2,3},{3,2},{4,5},{5,4},{6,7},{7,6},{8,9},{9,8},{10,11... | collective-permute-start | bytes 2555912 | tf_op jit(solution)/shard_map/ppermute | solution.py:32
  8.6 0.7 copy-start.1
  19.3 20.1 %collective-permute-start.6 = (bf16[128,3328]{1,0:T(8,128)(2,1)S(1)}, bf16[128,3328]{1,0:T(8,128)(2,1)S(1)}, u32[]{:S(2)}, u32[]{:S(2)}) collective-permute-start(bf16[128,3328]{1,0:T(8,128)(2,1)S(1)} %get-tuple-element.66), channel_id=1, source_target_pairs={{1,17},{2,18},{3,19},{4,20},{5,21},{6,22},{7,23},{8,24},{9,25},{10... | collective-permute-start | bytes 2555912 | tf_op jit(solution)/shard_map/ppermute | solution.py:32
  21.5 4.5 %collective-permute-start.4 = (bf16[128,1024]{1,0:T(8,128)(2,1)S(1)}, bf16[128,1024]{1,0:T(8,128)(2,1)S(1)}, u32[]{:S(2)}, u32[]{:S(2)}) collective-permute-start(bf16[128,1024]{1,0:T(8,128)(2,1)S(1)} %get-tuple-element.99), channel_id=1, source_target_pairs={{2,18},{3,19},{4,20},{5,21},{6,22},{7,23},{8,24},{9,25},{10,26},{1... | collective-permute-start | bytes 786440 | tf_op jit(solution)/shard_map/ppermute | solution.py:32
  21.6 5.0 %collective-permute-start.5 = (bf16[128,1024]{1,0:T(8,128)(2,1)S(1)}, bf16[128,1024]{1,0:T(8,128)(2,1)S(1)}, u32[]{:S(2)}, u32[]{:S(2)}) collective-permute-start(bf16[128,1024]{1,0:T(8,128)(2,1)S(1)} %get-tuple-element.98), channel_id=1, source_target_pairs={{3,19},{4,20},{5,21},{6,22},{7,23},{8,24},{9,25},{10,26},{11,27},{... | collective-permute-start | bytes 786440 | tf_op jit(solution)/shard_map/ppermute | solution.py:32
  22.1 15.4 %collective-permute-start.1 = (bf16[256,1024]{1,0:T(8,128)(2,1)S(1)}, bf16[256,1024]{1,0:T(8,128)(2,1)S(1)}, u32[]{:S(2)}, u32[]{:S(2)}) collective-permute-start(bf16[256,1024]{1,0:T(8,128)(2,1)S(1)} %get-tuple-element.55), channel_id=1, source_target_pairs={{0,64},{1,65},{2,66},{3,67},{4,68},{5,69},{6,70},{7,71},{8,72},{9,... | collective-permute-start | bytes 1572872 | tf_op jit(solution)/shard_map/ppermute | solution.py:32
  25.9 14.4 %collective-permute-start.7 = (bf16[64,3328]{1,0:T(8,128)(2,1)S(1)}, bf16[64,3328]{1,0:T(8,128)(2,1)S(1)}, u32[]{:S(2)}, u32[]{:S(2)}) collective-permute-start(bf16[64,3328]{1,0:T(8,128)(2,1)S(1)} %get-tuple-element.60), channel_id=1, source_target_pairs={{4,20},{5,21},{6,22},{7,23},{8,24},{9,25},{10,26},{11,27},{12,28},... | collective-permute-start | bytes 1277960 | tf_op jit(solution)/shard_map/ppermute | solution.py:32
  26.0 14.3 %collective-permute-start.8 = (bf16[64,3328]{1,0:T(8,128)(2,1)S(1)}, bf16[64,3328]{1,0:T(8,128)(2,1)S(1)}, u32[]{:S(2)}, u32[]{:S(2)}) collective-permute-start(bf16[64,3328]{1,0:T(8,128)(2,1)S(1)} %get-tuple-element.69), channel_id=1, source_target_pairs={{5,21},{6,22},{7,23},{8,24},{9,25},{10,26},{11,27},{12,28},{13,29}... | collective-permute-start | bytes 1277960 | tf_op jit(solution)/shard_map/ppermute | solution.py:32
  26.5 15.7 %collective-permute-start.12 = (bf16[128,3328]{1,0:T(8,128)(2,1)S(1)}, bf16[128,3328]{1,0:T(8,128)(2,1)S(1)}, u32[]{:S(2)}, u32[]{:S(2)}) collective-permute-start(bf16[128,3328]{1,0:T(8,128)(2,1)S(1)} %mix.3.refs_0_), channel_id=1, source_target_pairs={{0,2},{1,3},{2,0},{3,1},{4,6},{5,7},{6,4},{7,5},{8,10},{9,11},{10,... | collective-permute-start | bytes 2555912 | tf_op jit(solution)/shard_map/ppermute | solution.py:32
  39.7 1.8 %collective-permute-start.10 = (bf16[64,3328]{1,0:T(8,128)(2,1)S(1)}, bf16[64,3328]{1,0:T(8,128)(2,1)S(1)}, u32[]{:S(2)}, u32[]{:S(2)}) collective-permute-start(bf16[64,3328]{1,0:T(8,128)(2,1)S(1)} %get-tuple-element.71), channel_id=1, source_target_pairs={{8,24},{9,25},{10,26},{11,27},{12,28},{13,29},{14,30},{15,31},{16,... | collective-permute-start | bytes 1277960 | tf_op jit(solution)/shard_map/ppermute | solution.py:32
  39.8 2.4 %collective-permute-start.11 = (bf16[64,3328]{1,0:T(8,128)(2,1)S(1)}, bf16[64,3328]{1,0:T(8,128)(2,1)S(1)}, u32[]{:S(2)}, u32[]{:S(2)}) collective-permute-start(bf16[64,3328]{1,0:T(8,128)(2,1)S(1)} %get-tuple-element.73), channel_id=1, source_target_pairs={{9,25},{10,26},{11,27},{12,28},{13,29},{14,30},{15,31},{16,0},{17,... | collective-permute-start | bytes 1277960 | tf_op jit(solution)/shard_map/ppermute | solution.py:32
  40.5 14.0 %collective-permute-start.9 = (bf16[128,3328]{1,0:T(8,128)(2,1)S(1)}, bf16[128,3328]{1,0:T(8,128)(2,1)S(1)}, u32[]{:S(2)}, u32[]{:S(2)}) collective-permute-start(bf16[128,3328]{1,0:T(8,128)(2,1)S(1)} %add_second.1), channel_id=1, source_target_pairs={{0,32},{1,33},{2,34},{3,35},{4,36},{5,37},{6,38},{7,39},{8,40},{9,... | collective-permute-start | bytes 2555912 | tf_op jit(solution)/shard_map/ppermute | solution.py:32
  42.5 21.2 %collective-permute-start.19 = (bf16[128,3328]{1,0:T(8,128)(2,1)S(1)}, bf16[128,3328]{1,0:T(8,128)(2,1)S(1)}, u32[]{:S(2)}, u32[]{:S(2)}) collective-permute-start(bf16[128,3328]{1,0:T(8,128)(2,1)S(1)} %mix.4.refs_0_), channel_id=1, source_target_pairs={{0,4},{1,5},{2,6},{3,7},{4,0},{5,1},{6,2},{7,3},{8,12},{9,13},{10,... | collective-permute-start | bytes 2555912 | tf_op jit(solution)/shard_map/ppermute | solution.py:32
  44.6 14.4 %collective-permute-start.14 = (bf16[64,3328]{1,0:T(8,128)(2,1)S(1)}, bf16[64,3328]{1,0:T(8,128)(2,1)S(1)}, u32[]{:S(2)}, u32[]{:S(2)}) collective-permute-start(bf16[64,3328]{1,0:T(8,128)(2,1)S(1)} %add_first.2), channel_id=1, source_target_pairs={{0,32},{1,33},{2,34},{3,35},{4,36},{5,37},{6,38},{7,39},{8,40},{9,... | collective-permute-start | bytes 1277960 | tf_op jit(solution)/shard_map/ppermute | solution.py:32
  44.9 14.1 %collective-permute-start.15 = (bf16[64,3328]{1,0:T(8,128)(2,1)S(1)}, bf16[64,3328]{1,0:T(8,128)(2,1)S(1)}, u32[]{:S(2)}, u32[]{:S(2)}) collective-permute-start(bf16[64,3328]{1,0:T(8,128)(2,1)S(1)} %get-tuple-element.78), channel_id=1, source_target_pairs={{6,22},{7,23},{8,24},{9,25},{10,26},{11,27},{12,28},{13,29},{14,30... | collective-permute-start | bytes 1277960 | tf_op jit(solution)/shard_map/ppermute | solution.py:32
  45.5 18.1 %collective-permute-start.17 = (bf16[64,3328]{1,0:T(8,128)(2,1)S(1)}, bf16[64,3328]{1,0:T(8,128)(2,1)S(1)}, u32[]{:S(2)}, u32[]{:S(2)}) collective-permute-start(bf16[64,3328]{1,0:T(8,128)(2,1)S(1)} %add_first.3), channel_id=1, source_target_pairs={{0,32},{1,33},{2,34},{3,35},{4,36},{5,37},{6,38},{7,39},{8,40},{9,... | collective-permute-start | bytes 1277960 | tf_op jit(solution)/shard_map/ppermute | solution.py:32
  54.4 9.1 %collective-permute-start.18 = (bf16[64,3328]{1,0:T(8,128)(2,1)S(1)}, bf16[64,3328]{1,0:T(8,128)(2,1)S(1)}, u32[]{:S(2)}, u32[]{:S(2)}) collective-permute-start(bf16[64,3328]{1,0:T(8,128)(2,1)S(1)} %get-tuple-element.81), channel_id=1, source_target_pairs={{7,23},{8,24},{9,25},{10,26},{11,27},{12,28},{13,29},{14,30},{15,3... | collective-permute-start | bytes 1277960 | tf_op jit(solution)/shard_map/ppermute | solution.py:32
  59.0 18.4 %collective-permute-start.13 = (bf16[128,3328]{1,0:T(8,128)(2,1)S(1)}, bf16[128,3328]{1,0:T(8,128)(2,1)S(1)}, u32[]{:S(2)}, u32[]{:S(2)}) collective-permute-start(bf16[128,3328]{1,0:T(8,128)(2,1)S(1)} %collective-permute-done.9), channel_id=1, source_target_pairs={{10,26},{11,27},{12,28},{13,29},{14,30},{15,31},{16,0},{17,1},{18,... | collective-permute-start | bytes 2555912 | tf_op jit(solution)/shard_map/ppermute | solution.py:32
  64.0 17.7 %collective-permute-start.21 = (bf16[128,3328]{1,0:T(8,128)(2,1)S(1)}, bf16[128,3328]{1,0:T(8,128)(2,1)S(1)}, u32[]{:S(2)}, u32[]{:S(2)}) collective-permute-start(bf16[128,3328]{1,0:T(8,128)(2,1)S(1)} %mix.5.value_ref), channel_id=1, source_target_pairs={{0,8},{1,9},{2,10},{3,11},{4,12},{5,13},{6,14},{7,15},{8,0},{9,1},... | collective-permute-start | bytes 2555912 | tf_op jit(solution)/shard_map/ppermute | solution.py:32
  68.1 9.3 %collective-permute-start.16 = (bf16[64,3328]{1,0:T(8,128)(2,1)S(1)}, bf16[64,3328]{1,0:T(8,128)(2,1)S(1)}, u32[]{:S(2)}, u32[]{:S(2)}) collective-permute-start(bf16[64,3328]{1,0:T(8,128)(2,1)S(1)} %add_third.2), channel_id=1, source_target_pairs={{0,32},{1,33},{2,34},{3,35},{4,36},{5,37},{6,38},{7,39},{8,40},{9,... | collective-permute-start | bytes 1277960 | tf_op jit(solution)/shard_map/ppermute | solution.py:32
  68.1 14.3 %collective-permute-start.20 = (bf16[64,3328]{1,0:T(8,128)(2,1)S(1)}, bf16[64,3328]{1,0:T(8,128)(2,1)S(1)}, u32[]{:S(2)}, u32[]{:S(2)}) collective-permute-start(bf16[64,3328]{1,0:T(8,128)(2,1)S(1)} %add_third.3), channel_id=1, source_target_pairs={{0,32},{1,33},{2,34},{3,35},{4,36},{5,37},{6,38},{7,39},{8,40},{9,... | collective-permute-start | bytes 1277960 | tf_op jit(solution)/shard_map/ppermute | solution.py:32
  77.6 9.6 %collective-permute-start.22 = (bf16[64,3328]{1,0:T(8,128)(2,1)S(1)}, bf16[64,3328]{1,0:T(8,128)(2,1)S(1)}, u32[]{:S(2)}, u32[]{:S(2)}) collective-permute-start(bf16[64,3328]{1,0:T(8,128)(2,1)S(1)} %add_grad.2.refs_0_), channel_id=1, source_target_pairs={{0,1},{1,0},{2,3},{3,2},{4,5},{5,4},{6,7},{7,6},{8,9},{9,8},{10,11... | collective-permute-start | bytes 1277960 | tf_op jit(solution)/shard_map/ppermute | solution.py:32
  82.5 8.8 %collective-permute-start.23 = (bf16[64,3328]{1,0:T(8,128)(2,1)S(1)}, bf16[64,3328]{1,0:T(8,128)(2,1)S(1)}, u32[]{:S(2)}, u32[]{:S(2)}) collective-permute-start(bf16[64,3328]{1,0:T(8,128)(2,1)S(1)} %add_grad.3.refs_0_), channel_id=1, source_target_pairs={{0,1},{1,0},{2,3},{3,2},{4,5},{5,4},{6,7},{7,6},{8,9},{9,8},{10,11... | collective-permute-start | bytes 1277960 | tf_op jit(solution)/shard_map/ppermute | solution.py:32
  85.1 19.3 %collective-permute-start.27 = (bf16[3328,128]{1,0:T(8,128)(2,1)S(1)}, bf16[3328,128]{1,0:T(8,128)(2,1)S(1)}, u32[]{:S(2)}, u32[]{:S(2)}) collective-permute-start(bf16[3328,128]{1,0:T(8,128)(2,1)S(1)} %rotate.1.refs_0_), channel_id=1, source_target_pairs={{0,96},{1,97},{2,98},{3,99},{4,100},{5,101},{6,102},{7,103},{8,104... | collective-permute-start | bytes 2555912 | tf_op jit(solution)/shard_map/ppermute | solution.py:32
  85.1 19.4 %collective-permute-start.26 = (bf16[3328,128]{1,0:T(8,128)(2,1)S(1)}, bf16[3328,128]{1,0:T(8,128)(2,1)S(1)}, u32[]{:S(2)}, u32[]{:S(2)}) collective-permute-start(bf16[3328,128]{1,0:T(8,128)(2,1)S(1)} %rotate.1.refs_0_), channel_id=1, source_target_pairs={{0,32},{1,33},{2,34},{3,35},{4,36},{5,37},{6,38},{7,39},{8,40},{9,... | collective-permute-start | bytes 2555912 | tf_op jit(solution)/shard_map/ppermute | solution.py:32
  87.3 12.4 %collective-permute-start.24 = (bf16[64,3328]{1,0:T(8,128)(2,1)S(1)}, bf16[64,3328]{1,0:T(8,128)(2,1)S(1)}, u32[]{:S(2)}, u32[]{:S(2)}) collective-permute-start(bf16[64,3328]{1,0:T(8,128)(2,1)S(1)} %mix_grad.6.refs_0_), channel_id=1, source_target_pairs={{0,2},{1,3},{2,0},{3,1},{4,6},{5,7},{6,4},{7,5},{8,10},{9,11},{10,... | collective-permute-start | bytes 1277960 | tf_op jit(solution)/shard_map/ppermute | solution.py:32
  91.4 12.8 %collective-permute-start.28 = (bf16[64,3328]{1,0:T(8,128)(2,1)S(1)}, bf16[64,3328]{1,0:T(8,128)(2,1)S(1)}, u32[]{:S(2)}, u32[]{:S(2)}) collective-permute-start(bf16[64,3328]{1,0:T(8,128)(2,1)S(1)} %mix_grad.7.refs_0_), channel_id=1, source_target_pairs={{0,2},{1,3},{2,0},{3,1},{4,6},{5,7},{6,4},{7,5},{8,10},{9,11},{10,... | collective-permute-start | bytes 1277960 | tf_op jit(solution)/shard_map/ppermute | solution.py:32
  97.0 9.8 %collective-permute-start.25 = (bf16[3328,128]{1,0:T(8,128)(2,1)S(1)}, bf16[3328,128]{1,0:T(8,128)(2,1)S(1)}, u32[]{:S(2)}, u32[]{:S(2)}) collective-permute-start(bf16[3328,128]{1,0:T(8,128)(2,1)S(1)} %rotate.1.refs_0_), channel_id=1, source_target_pairs={{11,27},{12,28},{13,29},{14,30},{15,31},{16,0},{17,1},{18,2},{19,3... | collective-permute-start | bytes 2555912 | tf_op jit(solution)/shard_map/ppermute | solution.py:32
  104.4 2.6 %collective-permute-start.29 = (bf16[3328,128]{1,0:T(8,128)(2,1)S(1)}, bf16[3328,128]{1,0:T(8,128)(2,1)S(1)}, u32[]{:S(2)}, u32[]{:S(2)}) collective-permute-start(bf16[3328,128]{1,0:T(8,128)(2,1)S(1)} %collective-permute-done.27.refs_5_), channel_id=1, source_target_pairs={{13,29},{14,30},{15,31},{16,0},{17,1},{18,2},{19,3},{20,4},{21,5},... | collective-permute-start | bytes 2555912 | tf_op jit(solution)/shard_map/ppermute | solution.py:32
  104.5 3.6 %collective-permute-start.30 = (bf16[3328,128]{1,0:T(8,128)(2,1)S(1)}, bf16[3328,128]{1,0:T(8,128)(2,1)S(1)}, u32[]{:S(2)}, u32[]{:S(2)}) collective-permute-start(bf16[3328,128]{1,0:T(8,128)(2,1)S(1)} %collective-permute-done.26.refs_2_), channel_id=1, source_target_pairs={{12,28},{13,29},{14,30},{15,31},{16,0},{17,1},{18,2},{19,3},{20,4}... | collective-permute-start | bytes 2555912 | tf_op jit(solution)/shard_map/ppermute | solution.py:32
  105.0 13.9 %collective-permute-start.32 = (bf16[3328,128]{1,0:T(8,128)(2,1)S(1)}, bf16[3328,128]{1,0:T(8,128)(2,1)S(1)}, u32[]{:S(2)}, u32[]{:S(2)}) collective-permute-start(bf16[3328,128]{1,0:T(8,128)(2,1)S(1)} %collective-permute-done.26.refs_2_), channel_id=1, source_target_pairs={{0,32},{1,33},{2,34},{3,35},{4,36},{5,37},{6,38},{7,39},{8,40},{9,... | collective-permute-start | bytes 2555912 | tf_op jit(solution)/shard_map/ppermute | solution.py:32
  105.0 8.5 %collective-permute-start.31 = (bf16[64,3328]{1,0:T(8,128)(2,1)S(1)}, bf16[64,3328]{1,0:T(8,128)(2,1)S(1)}, u32[]{:S(2)}, u32[]{:S(2)}) collective-permute-start(bf16[64,3328]{1,0:T(8,128)(2,1)S(1)} %mix_grad.8.refs_0_), channel_id=1, source_target_pairs={{0,4},{1,5},{2,6},{3,7},{4,0},{5,1},{6,2},{7,3},{8,12},{9,13},{10,... | collective-permute-start | bytes 1277960 | tf_op jit(solution)/shard_map/ppermute | solution.py:32
  106.8 10.9 %collective-permute-start.33 = (bf16[64,3328]{1,0:T(8,128)(2,1)S(1)}, bf16[64,3328]{1,0:T(8,128)(2,1)S(1)}, u32[]{:S(2)}, u32[]{:S(2)}) collective-permute-start(bf16[64,3328]{1,0:T(8,128)(2,1)S(1)} %mix_grad.9.refs_0_), channel_id=1, source_target_pairs={{0,4},{1,5},{2,6},{3,7},{4,0},{5,1},{6,2},{7,3},{8,12},{9,13},{10,... | collective-permute-start | bytes 1277960 | tf_op jit(solution)/shard_map/ppermute | solution.py:32
  118.9 4.0 %collective-permute-start.34 = (bf16[3328,128]{1,0:T(8,128)(2,1)S(1)}, bf16[3328,128]{1,0:T(8,128)(2,1)S(1)}, u32[]{:S(2)}, u32[]{:S(2)}) collective-permute-start(bf16[3328,128]{1,0:T(8,128)(2,1)S(1)} %collective-permute-done.32.mine_ref), channel_id=1, source_target_pairs={{14,30},{15,31},{16,0},{17,1},{18,2},{19,3},{20,4},{21,5},{22,6},{... | collective-permute-start | bytes 2555912 | tf_op jit(solution)/shard_map/ppermute | solution.py:32
  118.9 10.1 %collective-permute-start.36 = (bf16[64,3328]{1,0:T(8,128)(2,1)S(1)}, bf16[64,3328]{1,0:T(8,128)(2,1)S(1)}, u32[]{:S(2)}, u32[]{:S(2)}) collective-permute-start(bf16[64,3328]{1,0:T(8,128)(2,1)S(1)} %mix_grad.11.refs_1_), channel_id=1, source_target_pairs={{0,8},{1,9},{2,10},{3,11},{4,12},{5,13},{6,14},{7,15},{8,0},{9,1},... | collective-permute-start | bytes 1277960 | tf_op jit(solution)/shard_map/ppermute | solution.py:32
  122.9 10.7 %collective-permute-start.35 = (bf16[64,3328]{1,0:T(8,128)(2,1)S(1)}, bf16[64,3328]{1,0:T(8,128)(2,1)S(1)}, u32[]{:S(2)}, u32[]{:S(2)}) collective-permute-start(bf16[64,3328]{1,0:T(8,128)(2,1)S(1)} %mix_grad.10.refs_0_), channel_id=1, source_target_pairs={{0,8},{1,9},{2,10},{3,11},{4,12},{5,13},{6,14},{7,15},{8,0},{9,1},... | collective-permute-start | bytes 1277960 | tf_op jit(solution)/shard_map/ppermute | solution.py:32

commit v3 on v2

--- a/solution.py
+++ b/solution.py
@@ -9,6 +9,7 @@
 
 HB = 256
 SCALE = 64.0
+BEHIND = (0, 2, 1, 3)
 AXES = ("x", "core", "z", "y")
 BF16 = jnp.bfloat16
 F32 = jnp.float32
@@ -44,6 +45,10 @@
     return move(value, lambda x, c, z, y: (x - 1 + 2 * c, c, z, y))
 
 
+def forward_crossed(value):
+    return move(value, lambda x, c, z, y: (x + 1 - 2 * c, 1 - c, z, y))
+
+
 def across(value):
     return move(value, lambda x, c, z, y: (x + 2, c, z, y))
 
@@ -62,7 +67,7 @@
     return pltpu.with_memory_space_constraint(value, pltpu.HBM)
 
 
-def call(kernel, name, mib, in_specs, out_specs, out_shape, scratch_shapes=(), grid=()):
+def call(kernel, name, mib, in_specs, out_specs, out_shape, scratch_shapes=(), grid=(), flops=1):
     return pl.pallas_call(
         kernel,
         grid=grid,
@@ -71,7 +76,7 @@
         out_shape=out_shape,
         scratch_shapes=scratch_shapes,
         compiler_params=pltpu.CompilerParams(vmem_limit_bytes=mib * 2**20),
-        cost_estimate=pl.CostEstimate(flops=1, bytes_accessed=1, transcendentals=0),
+        cost_estimate=pl.CostEstimate(flops=flops, bytes_accessed=1, transcendentals=0),
         name=name,
     )
 
@@ -189,7 +194,7 @@
         store_rows(result, [out.at[:, part] for out in outs])
 
 
-def product(grads, turned, rows):
+def product(grads, turned, rows, flops=1):
     ff = turned.shape[0]
     return call(
         functools.partial(product_kernel, len(grads)),
@@ -198,6 +203,7 @@
         [VMEM] * (len(grads) + 1),
         [VMEM] * len(rows),
         [pltpu.VMEM((size, ff), BF16) for size in rows],
+        flops=flops,
     )(*grads, turned)
 
 
@@ -298,41 +304,44 @@
     return jnp.dot(left, grads, preferred_element_type=F32)
 
 
-def early_kernel(count, pieces, *refs):
-    rotated, grads = refs[:count], refs[count:-2]
-    out_ref, all_grads = refs[-2:]
-    tokens = rotated[0].shape[1]
-    row = 0
-    for ref, piece in zip(grads, pieces):
-        rows = 2 * tokens // piece
-        all_grads[pl.ds(row, rows), :] = ref[:rows, :]
-        row += rows
+def gather_rows(blocks, refs, all_grads):
+    tokens = all_grads.shape[0] // len(blocks)
+    for i, (which, row) in enumerate(blocks):
+        all_grads[pl.ds(i * tokens, tokens), :] = refs[which][row * tokens : (row + 1) * tokens, :]
+
+
+def early_kernel(blocks, *refs):
+    count = len(blocks)
+    rotated, grads, (out_ref, all_grads) = refs[:count], refs[count:-2], refs[-2:]
+    gather_rows(blocks, grads, all_grads)
     for i in range(out_ref.shape[0] // HB):
         part = pl.ds(i * HB, HB)
         out_ref[part, :] = partial_sum(rotated, all_grads[...], part)
 
 
-def early_product(rotated, grads):
-    count = len(rotated)
-    flat = [piece for chip in grads for piece in chip]
-    pieces = tuple(len(chip) for chip in grads for _ in chip)
-    ff, cols = rotated[0].shape[0], flat[0].shape[1]
-    return call(
-        functools.partial(early_kernel, count, pieces),
+def early_product(rotated, blocks, grads):
+    ff, tokens = rotated[0].shape
+    cols = grads[0].shape[1]
+    return call(
+        functools.partial(early_kernel, blocks),
         "early_product",
         10,
-        [VMEM] * (count + len(flat)),
+        [VMEM] * (len(rotated) + len(grads)),
         VMEM,
         pltpu.VMEM((ff, cols), F32),
-        [pltpu.VMEM((count * rotated[0].shape[1], cols), BF16)],
-    )(*rotated, *flat)
-
-
-def late_kernel(mine_ref, other_ref, grad_ref, keep_ref, early_ref, out_ref, held, sems):
+        [pltpu.VMEM((len(rotated) * tokens, cols), BF16)],
+    )(*rotated, *grads)
+
+
+def late_kernel(blocks, *refs):
+    count = len(blocks)
+    rotated, grads = refs[:count], refs[count:-6]
+    keep_ref, early_ref, out_ref, all_grads, held, sems = refs[-6:]
+    gather_rows(blocks, grads, all_grads)
     copies = []
     for i in range(early_ref.shape[0] // HB):
         part = pl.ds(i * HB, HB)
-        total = early_ref[part, :] + partial_sum((mine_ref, other_ref), grad_ref[...], part)
+        total = early_ref[part, :] + partial_sum(rotated, all_grads[...], part)
         held[part, :] = jnp.where(keep_ref[part, :].astype(F32) > 0.0, total, 0.0).astype(BF16)
         copies.append(pltpu.make_async_copy(held.at[part, :], out_ref.at[part, :], sems.at[i]))
         copies[-1].start()
@@ -340,20 +349,119 @@
         copy.wait()
 
 
-def late_product(mine, other, grads, keep, early):
-    return call(
-        late_kernel,
+def late_product(rotated, blocks, grads, keep, early):
+    tokens = rotated[0].shape[1]
+    return call(
+        functools.partial(late_kernel, blocks),
         "late_product",
         14,
-        [VMEM] * 5,
+        [VMEM] * (len(rotated) + len(grads) + 2),
         ANY,
         jax.ShapeDtypeStruct(early.shape, BF16),
-        streamed(*early.shape),
-    )(mine, other, grads, keep, early)
+        [pltpu.VMEM((len(rotated) * tokens, early.shape[1]), BF16)] + streamed(*early.shape),
+    )(*rotated, *grads, keep, early)
+
+
+def place(stage):
+    core, z, y = (lax.axis_index(axis) for axis in ("core", "z", "y"))
+    return jnp.where((core == 0) == (stage == 0), y, z)
+
+
+def quarter(index, rows):
+    return pl.ds(pl.multiple_of(jnp.bitwise_and(index, 3) * rows, rows), rows)
+
+
+def deal_kernel(stage, *refs):
+    terms, outs = refs[:-4], refs[-4:]
+    mine = place(stage)
+    rows = outs[0].shape[0]
+    for k, out in enumerate(outs):
+        part_rows = quarter(mine + k, rows)
+        for i in range(out.shape[1] // HB):
+            part = pl.ds(i * HB, HB)
+            out[:, part] = sum(ref[part_rows, part].astype(F32) for ref in terms).astype(BF16)
+
+
+def deal(name, stage, *terms):
+    tokens, ff = terms[0].shape
+    return call(
+        functools.partial(deal_kernel, stage),
+        name,
+        6,
+        [VMEM] * len(terms),
+        [VMEM] * 4,
+        [pltpu.VMEM((tokens // 4, ff), BF16)] * 4,
+    )(*terms)
+
+
+def spread(pieces, stage):
+    def route(distance):
+        def to(x, c, z, y):
+            if (c == 0) == (stage == 0):
+                return (x, c, z, (y + distance) % 4)
+            return (x, c, (z + distance) % 4, y)
+
+        return to
+
+    return [pieces[0]] + [move(pieces[k], route(k)) for k in BEHIND[1:]]
+
+
+def mix_quarters_kernel(stage, *refs):
+    values, outs = refs[:4], refs[4:]
+    mine = place(stage)
+    for k, out in enumerate(outs):
+        signs = []
+        for m in BEHIND:
+            both = jnp.bitwise_and(jnp.bitwise_and(mine + k, mine - m), 3)
+            odd = jnp.bitwise_and(both + (both >> 1), 1)
+            signs.append((1 - 2 * odd).astype(F32))
+        for i in range(out.shape[1] // HB):
+            part = pl.ds(i * HB, HB)
+            total = sum(ref[:, part].astype(F32) * sign for ref, sign in zip(values, signs))
+            out[:, part] = total.astype(BF16)
+
+
+def mix_quarters(stage, values):
+    return call(
+        functools.partial(mix_quarters_kernel, stage),
+        "mix_quarters",
+        6,
+        [VMEM] * 4,
+        [VMEM] * 4,
+        [pltpu.VMEM(values[0].shape, BF16)] * 4,
+    )(*values)
+
+
+def collect_kernel(*refs):
+    values, outs = refs[:4], refs[4:]
+    rows = values[0].shape[0]
+    if len(outs) == 1:
+        for k, ref in zip(BEHIND, values):
+            outs[0][quarter(place(1) - k, rows), :] = ref[...]
+        return
+    outs, held = outs[:4], outs[4]
+    for k, ref in zip(BEHIND, values):
+        held[quarter(place(0) - k, rows), :] = ref[...]
+    for k, out in enumerate(outs):
+        out[...] = held[quarter(place(1) + k, rows), :]
+
+
+def collect(values, last):
+    rows, ff = values[0].shape
+    whole = (4 * rows, ff)
+    return call(
+        collect_kernel,
+        "collect",
+        6,
+        [VMEM] * 4,
+        VMEM if last else [VMEM] * 4,
+        jax.ShapeDtypeStruct(whole, BF16) if last else [pltpu.VMEM((rows, ff), BF16)] * 4,
+        [] if last else [pltpu.VMEM(whole, BF16)],
+    )(*values)
 
 
 def mix_axis(step):
-    return 1 << (step % 2), step < 2
+    return 1 << (step // 2), step % 2 == 0
 
 
 def partner(value, step):
@@ -381,64 +489,51 @@
 
     hid = mix("mix", 0, [after(hidden, turned)], [got])
     got = partner(hid, 1)
-    bwd = after(bwd, hid)
+    opp_mine, *opp_other = product([after(opp, hid)], turned, whole + halves)
+    opp_other = [swap(opp_other[j], 8 + j) for j in (0, 1)]
+    (first_send,) = add("add_first", whole, opp_mine, opp_other)
+    first = forward(first_send)
+    bwd = after(bwd, first_send)
     fwd = [swap(bwd[(2 + j) * tokens : (3 + j) * tokens], 2 + j) for j in (0, 1)]
     bwd_parts = product([bwd], turned, halves * 2)
     bwd_mine = [swap(bwd_parts[j], 4 + j) for j in (0, 1)]
     bwd_other = [swap(bwd_parts[2 + j], 6 + j) for j in (0, 1)]
-    fwd_other, *fwd_mine = product([after(fwd[0], bwd_parts[0]), fwd[1]], turned, whole + halves)
-    opp_mine, *opp_other = product([after(opp, fwd_other)], turned, whole + halves)
-    opp_other = [swap(opp_other[j], 8 + j) for j in (0, 1)]
-    own_sum = add("add_own", halves, after(own_mine, opp_mine), own_other)
-    (second_send,) = add("add_second", whole, after(fwd_other, own_sum[0]), bwd_mine)
-    second = forward(second_send)
-    first = []
-    last = second_send
-    for j in (0, 1):
-        (last,) = add("add_first", (half,), (after(opp_mine, last), j * half), opp_other[j])
-        first.append(forward(last))
-    hid = mix("mix", 1, [after(hid, last)], [got])
+    hid = mix("mix", 1, [after(hid, bwd_parts[0])], [got])
     got = partner(hid, 2)
-    second = after(second, hid)
-    second_other = swap(second, 10)
-    third = []
-    last = second
-    for j in (0, 1):
-        (last,) = add("add_third", (half,), after(first[j], last), fwd_mine[j], bwd_other[j])
-        third.append(forward(last))
-    hid = mix("mix", 2, [after(hid, last)], [got])
+    (own_sum,) = add("add_own", whole, after(own_mine, hid), own_other)
+    fwd_other, *fwd_mine = product(
+        [after(fwd[0], own_sum, first), fwd[1]], turned, whole + halves
+    )
+    (third_send,) = add("add_third", whole, after(first, fwd_other), list(fwd_mine), bwd_other)
+    third = forward(third_send)
+    (second_send,) = add("add_second", whole, after(fwd_other, third_send), bwd_mine)
+    second = forward_crossed(second_send)
+    hid = mix("mix", 2, [after(hid, second_send)], [got])
     got = partner(hid, 3)
-    last = hid
-
-    values, partners = [], []
-    for j in (0, 1):
-        (last,) = add(
-            "add_grad", (half,), own_sum[j], (second_other, j * half), after(third[j], last)
-        )
-        values.append(last)
-        partners.append(partner(last, 0))
-        if j == 0:
-            last = rotated = rotate(table, 3, after(hid, last), got)
-            bwd_a, fwd_a = forward(rotated), backward(rotated)
-            other = swap(rotated, 11)
-    for step in range(3):
-        for j in (0, 1):
-            last = mix("mix_grad", step, [after(values[j], last)], [partners[j]])
-            values[j] = last
-            partners[j] = partner(last, step + 1)
-        if step == 0:
-            bwd_a = after(bwd_a, last)
-            opp_a = forward(bwd_a)
-            fwd_b = swap(bwd_a, 12)
-        if step == 1:
-            fwd_a = after(fwd_a, last)
-            bwd_b = swap(fwd_a, 13)
-            last = early = early_product(
-                [rotated, other, bwd_a, bwd_b, fwd_b, fwd_a], [[own], [bwd], fwd]
-            )
-    opp_a = after(opp_a, last)
-    weight_grad = late_product(opp_a, swap(opp_a, 14), opp, keep, early)
-    hidden_grad = mix("mix_last", 3, [after(values[0], weight_grad), values[1]], partners, last=True)
+
+    pieces = deal("deal_grad", 0, own_sum, after(second, hid), after(third, hid))
+    values = spread(pieces, 0)
+    rotated = rotate(table, 3, after(hid, pieces[0]), got)
+    bwd_a, fwd_a = forward(rotated), backward(rotated)
+    other = swap(rotated, 11)
+    pieces = mix_quarters(0, [after(values[0], rotated)] + values[1:])
+    values = spread(pieces, 0)
+    pieces = collect([after(values[0], bwd_a, fwd_a)] + values[1:], False)
+    opp_a = forward(bwd_a)
+    fwd_b, bwd_b = swap(after(bwd_a, pieces[0]), 12), swap(after(fwd_a, pieces[0]), 13)
+    values = spread(pieces, 1)
+    early = early_product(
+        [rotated, other, bwd_a, bwd_b, fwd_b, fwd_a],
+        ((0, 0), (0, 1), (1, 0), (1, 1), (2, 0), (3, 0)),
+        [own, bwd] + fwd,
+    )
+    pieces = mix_quarters(1, [after(values[0], early)] + values[1:])
+    values = spread(pieces, 1)
+    opp_a = after(opp_a, pieces[0])
+    weight_grad = late_product(
+        [opp_a, swap(opp_a, 14)], ((0, 0), (0, 1)), [opp], keep, early
+    )
+    hidden_grad = collect([after(values[0], weight_grad)] + values[1:], True)
     return hidden_grad, weight_grad
 
 

time: 135 us -> 118 us (0.87)
  waiting for transfers between devices: 58.9 us -> 32.9 us
  starting transfers between devices: 42.8 us -> 51.1 us
    ppermute x37 -> x38, waiting for transfers between devices: 58.9 us -> 32.9 us  [move(): return lax.ppermute(value, AXES, pairs[turn:] + pairs[:turn])]
    ppermute x37 -> x38, starting transfers between devices: 42.8 us -> 51.1 us  [move(): return lax.ppermute(value, AXES, pairs[turn:] + pairs[:turn])]
    pallas_call x2 -> x7, Pallas kernels: 8.98 us -> 11.7 us  [the longest x1 5.46 us: early_product(): call(functools.partial(early_kernel, blocks), 'early_product', 10, [VMEM]...]
    pallas_call x10 -> x3, Pallas kernels: 2.79 us -> 0.79 us  [mix(): call(functools.partial(mix_kernel, step), name, 6, [VMEM] * (2 * len(valu...]
  transfers between devices with their start and end apart: 37 -> 38, of which waited for: 17 -> 18; matrix products, arithmetic and copies ran while one was open for 0% -> 0% of each run, Pallas kernels for 21% -> 24%
where the time goes in v3:
time: 118 us
  starting transfers between devices  51.1 us (43%)
  waiting for transfers between devices  32.9 us (28%)
  Pallas kernels  31.8 us (27%)
    ppermute x38, starting transfers between devices, move(): return lax.ppermute(value, AXES, pairs[turn:] + pairs[:turn])  51.1 us
    ppermute x38, waiting for transfers between devices, move(): return lax.ppermute(value, AXES, pairs[turn:] + pairs[:turn])  32.9 us
    pallas_call x1, Pallas kernels, quantize(): call(quantize_kernel, 'quantize', 14, [VMEM, ANY, VMEM, VMEM], [VMEM] * (...  10 us
    pallas_call x3, Pallas kernels, product(): call(functools.partial(product_kernel, len(grads)), 'product', 8, [VMEM]...  5.88 us
    pallas_call x1, Pallas kernels, early_product(): call(functools.partial(early_kernel, blocks), 'early_product', 10, [VMEM]...  5.46 us
    pallas_call x1, Pallas kernels, late_product(): call(functools.partial(late_kernel, blocks), 'late_product', 14, [VMEM] *...  3.55 us
  transfers between devices with their start and end apart: 38, of which 18 were waited for; matrix products, arithmetic and copies ran while one was open for 0% of the time, Pallas kernels for 24%

profile of v3, /device:TPU:0, one launch (start us, length us, event | category | flops | bytes accessed | tf_op | source)
XLA Modules:
  0.0 117.5 jit_solution(7651688487821316746)
XLA Ops:
  0.8 1.7 %split.1 = (bf16[4,128,1024]{2,1,0:T(8,128)(2,1)S(1)}, bf16[4,128,1024]{2,1,0:T(8,128)(2,1)S(1)}) custom-call(bf16[128,8192]{1,0:T(8,128)(2,1)} %grad_ref), custom_call_target="tpu_custom_call" | custom-call | flops 1 | bytes 1 | tf_op jit(solution)/shard_map/split/pallas_call | solution.py:105
  2.6 1.7 %collective-permute-start.1 = (bf16[128,3328]{1,0:T(8,128)(2,1)}, bf16[128,3328]{1,0:T(8,128)(2,1)S(1)}, u32[]{:S(2)}, u32[]{:S(2)}) collective-permute-start(bf16[128,3328]{1,0:T(8,128)(2,1)} %refs_0_), channel_id=1, source_target_pairs={{0,1},{1,0},{2,3},{3,2},{4,5},{5,4},{6,7},{7,6},{8,9},{9,8},{10,11... | collective-permute-start | bytes 2555912 | tf_op jit(solution)/shard_map/ppermute | solution.py:33
  4.3 0.9 collective-permute-done.got_ref
  5.4 3.2 %collective-permute-start.3 = (bf16[256,1024]{1,0:T(8,128)(2,1)S(1)}, bf16[256,1024]{1,0:T(8,128)(2,1)S(1)}, u32[]{:S(2)}, u32[]{:S(2)}) collective-permute-start(bf16[256,1024]{1,0:T(8,128)(2,1)S(1)} %get-tuple-element.65), channel_id=1, source_target_pairs={{0,64},{1,65},{2,66},{3,67},{4,68},{5,69},{6,70},{7,71},{8,72},{9,... | collective-permute-start | bytes 1572872 | tf_op jit(solution)/shard_map/ppermute | solution.py:33
  8.5 0.6 collective-permute-start.2
  9.1 0.7 copy-done.1
  9.8 10.0 %quantize.1 = (bf16[3328,1024]{1,0:T(8,128)(2,1)S(1)}, bf16[3328,1024]{1,0:T(8,128)(2,1)S(1)}, bf16[128,3328]{1,0:T(8,128)(2,1)S(1)}, bf16[128,3328]{1,0:T(8,128)(2,1)S(1)}) custom-call(bf16[256,256]{1,0:T(8,128)(2,1)S(1)} %fusion.3.table_ref, bf16[3328,1024]{1,0:T(8,128)(2,1)} %weight_ref.1, f32[1,1024]{1,0:T(1,128)S(1)} %bitcast.1, ...), custom_call_target="tpu_custom_call" | custom-call | flops 1 | bytes 1 | tf_op jit(solution)/shard_map/quantize/pallas_call | solution.py:172
  19.9 0.3 mix.3.refs_0_
  20.2 2.0 %collective-permute-start.6 = (bf16[128,3328]{1,0:T(8,128)(2,1)S(1)}, bf16[128,3328]{1,0:T(8,128)(2,1)S(1)}, u32[]{:S(2)}, u32[]{:S(2)}) collective-permute-start(bf16[128,3328]{1,0:T(8,128)(2,1)S(1)} %mix.3.refs_0_), channel_id=1, source_target_pairs={{0,4},{1,5},{2,6},{3,7},{4,0},{5,1},{6,2},{7,3},{8,12},{9,13},{10,... | collective-permute-start | bytes 2555912 | tf_op jit(solution)/shard_map/ppermute | solution.py:33
  22.2 2.0 %product.3 = (bf16[128,3328]{1,0:T(8,128)(2,1)S(1)}, bf16[64,3328]{1,0:T(8,128)(2,1)S(1)}, bf16[64,3328]{1,0:T(8,128)(2,1)S(1)}) custom-call(bf16[256,1024]{1,0:T(8,128)(2,1)S(1)} %collective-permute-done.3.refs_0_.refs_2_, bf16[3328,1024]{1,0:T(8,128)(2,1)S(1)} %get-tuple-element.62.refs_1_.refs_2_), custom_call_target="tpu_custom_call" | custom-call | flops 1 | bytes 1 | tf_op jit(solution)/shard_map/product/pallas_call | solution.py:199
  24.2 0.5 collective-permute-start.5
  24.8 1.2 collective-permute-done.4.refs_1_
  26.0 0.6 collective-permute-done.5.refs_2_
  26.8 1.2 %collective-permute-start.9 = (bf16[128,3328]{1,0:T(8,128)(2,1)S(1)}, bf16[128,3328]{1,0:T(8,128)(2,1)S(1)}, u32[]{:S(2)}, u32[]{:S(2)}) collective-permute-start(bf16[128,3328]{1,0:T(8,128)(2,1)S(1)} %add_first.1), channel_id=1, source_target_pairs={{0,32},{1,33},{2,34},{3,35},{4,36},{5,37},{6,38},{7,39},{8,40},{9,... | collective-permute-start | bytes 2555912 | tf_op jit(solution)/shard_map/ppermute | solution.py:33
  28.0 4.1 %collective-permute-done.2.refs_0_.refs_7_ = bf16[512,1024]{1,0:T(8,128)(2,1)S(1)} collective-permute-done((bf16[512,1024]{1,0:T(8,128)(2,1)S(1)}, bf16[512,1024]{1,0:T(8,128)(2,1)S(1)}, u32[]{:S(2)}, u32[]{:S(2)}) %collective-permute-start.2) | collective-permute-done | bytes 1048608 | tf_op jit(solution)/shard_map/ppermute | solution.py:33
  32.1 2.0 %product.4 = (bf16[64,3328]{1,0:T(8,128)(2,1)S(1)}, bf16[64,3328]{1,0:T(8,128)(2,1)S(1)}, bf16[64,3328]{1,0:T(8,128)(2,1)S(1)}, bf16[64,3328]{1,0:T(8,128)(2,1)S(1)}) custom-call(bf16[512,1024]{1,0:T(8,128)(2,1)S(1)} %collective-permute-done.2.refs_0_.refs_7_, bf16[3328,1024]{1,0:T(8,128)(2,1)S(1)} %get-tuple-element.62.refs_1_.refs_2_), custom_call_target="tpu_custom_call" | custom-call | flops 1 | bytes 1 | tf_op jit(solution)/shard_map/product/pallas_call | solution.py:199
  34.1 0.3 mix.4.refs_0_
  34.4 3.4 %collective-permute-start.16 = (bf16[128,3328]{1,0:T(8,128)(2,1)S(1)}, bf16[128,3328]{1,0:T(8,128)(2,1)S(1)}, u32[]{:S(2)}, u32[]{:S(2)}) collective-permute-start(bf16[128,3328]{1,0:T(8,128)(2,1)S(1)} %mix.4.refs_0_), channel_id=1, source_target_pairs={{0,2},{1,3},{2,0},{3,1},{4,6},{5,7},{6,4},{7,5},{8,10},{9,11},{10,... | collective-permute-start | bytes 2555912 | tf_op jit(solution)/shard_map/ppermute | solution.py:33
  37.8 0.7 collective-permute-start.10
  38.6 0.4 collective-permute-start.11
  39.0 0.6 collective-permute-done.10.refs_1_.refs_9_
  39.7 0.4 collective-permute-start.12
  40.0 0.4 collective-permute-start.14
  40.4 0.9 collective-permute-done.9.refs_0_
  41.3 0.3 collective-permute-start.13
  41.8 2.0 %product.5 = (bf16[128,3328]{1,0:T(8,128)(2,1)S(1)}, bf16[64,3328]{1,0:T(8,128)(2,1)S(1)}, bf16[64,3328]{1,0:T(8,128)(2,1)S(1)}) custom-call(bf16[128,1024]{1,0:T(8,128)(2,1)S(1)} %collective-permute-done.8.refs_0_.refs_8_, bf16[128,1024]{1,0:T(8,128)(2,1)S(1)} %collective-permute-done.10.refs_1_.refs_9_, ...), custom_call_target="tpu_custom_call" | custom-call | flops 1 | bytes 1 | tf_op jit(solution)/shard_map/product/pallas_call | solution.py:199
  43.8 0.3 add_third.1
  44.1 1.4 %collective-permute-start.17 = (bf16[128,3328]{1,0:T(8,128)(2,1)S(1)}, bf16[128,3328]{1,0:T(8,128)(2,1)S(1)}, u32[]{:S(2)}, u32[]{:S(2)}) collective-permute-start(bf16[128,3328]{1,0:T(8,128)(2,1)S(1)} %add_third.1), channel_id=1, source_target_pairs={{0,32},{1,33},{2,34},{3,35},{4,36},{5,37},{6,38},{7,39},{8,40},{9,... | collective-permute-start | bytes 2555912 | tf_op jit(solution)/shard_map/ppermute | solution.py:33
  45.5 0.2 add_second.1
  45.7 0.2 collective-permute-start.15
  46.0 2.7 %collective-permute-done.16.refs_1_ = bf16[128,3328]{1,0:T(8,128)(2,1)S(1)} collective-permute-done((bf16[128,3328]{1,0:T(8,128)(2,1)S(1)}, bf16[128,3328]{1,0:T(8,128)(2,1)S(1)}, u32[]{:S(2)}, u32[]{:S(2)}) %collective-permute-start.16) | collective-permute-done | bytes 852000 | tf_op jit(solution)/shard_map/ppermute | solution.py:33
  48.7 0.3 mix.5.value_ref
  48.9 4.0 %collective-permute-start.18 = (bf16[128,3328]{1,0:T(8,128)(2,1)S(1)}, bf16[128,3328]{1,0:T(8,128)(2,1)S(1)}, u32[]{:S(2)}, u32[]{:S(2)}) collective-permute-start(bf16[128,3328]{1,0:T(8,128)(2,1)S(1)} %mix.5.value_ref), channel_id=1, source_target_pairs={{0,8},{1,9},{2,10},{3,11},{4,12},{5,13},{6,14},{7,15},{8,0},{9,1},... | collective-permute-start | bytes 2555912 | tf_op jit(solution)/shard_map/ppermute | solution.py:33
  53.0 5.1 %collective-permute-done.17.refs_2_ = bf16[128,3328]{1,0:T(8,128)(2,1)S(1)} collective-permute-done((bf16[128,3328]{1,0:T(8,128)(2,1)S(1)}, bf16[128,3328]{1,0:T(8,128)(2,1)S(1)}, u32[]{:S(2)}, u32[]{:S(2)}) %collective-permute-start.17) | collective-permute-done | bytes 852000 | tf_op jit(solution)/shard_map/ppermute | solution.py:33
  58.1 7.1 %collective-permute-done.15.refs_1_ = bf16[128,3328]{1,0:T(8,128)(2,1)S(1)} collective-permute-done((bf16[128,3328]{1,0:T(8,128)(2,1)S(1)}, bf16[128,3328]{1,0:T(8,128)(2,1)S(1)}, u32[]{:S(2)}, u32[]{:S(2)}) %collective-permute-start.15) | collective-permute-done | bytes 852000 | tf_op jit(solution)/shard_map/ppermute | solution.py:33
  65.2 0.3 deal_grad.1
  65.5 0.6 rotate.1.refs_0_
  66.2 3.7 %collective-permute-start.23 = (bf16[3328,128]{1,0:T(8,128)(2,1)S(1)}, bf16[3328,128]{1,0:T(8,128)(2,1)S(1)}, u32[]{:S(2)}, u32[]{:S(2)}) collective-permute-start(bf16[3328,128]{1,0:T(8,128)(2,1)S(1)} %rotate.1.refs_0_), channel_id=1, source_target_pairs={{0,96},{1,97},{2,98},{3,99},{4,100},{5,101},{6,102},{7,103},{8,104... | collective-permute-start | bytes 2555912 | tf_op jit(solution)/shard_map/ppermute | solution.py:33
  69.9 3.0 %collective-permute-start.19 = (bf16[32,3328]{1,0:T(8,128)(2,1)S(1)}, bf16[32,3328]{1,0:T(8,128)(2,1)S(1)}, u32[]{:S(2)}, u32[]{:S(2)}) collective-permute-start(bf16[32,3328]{1,0:T(8,128)(2,1)S(1)} %get-tuple-element.90), channel_id=1, source_target_pairs={{0,2},{1,3},{2,0},{3,1},{4,6},{5,7},{6,4},{7,5},{8,10},{9,11},{10,... | collective-permute-start | bytes 638984 | tf_op jit(solution)/shard_map/ppermute | solution.py:33
  72.9 0.8 collective-permute-start.20
  73.8 2.4 %collective-permute-start.21 = (bf16[32,3328]{1,0:T(8,128)(2,1)S(1)}, bf16[32,3328]{1,0:T(8,128)(2,1)S(1)}, u32[]{:S(2)}, u32[]{:S(2)}) collective-permute-start(bf16[32,3328]{1,0:T(8,128)(2,1)S(1)} %get-tuple-element.92), channel_id=1, source_target_pairs={{0,3},{1,0},{2,1},{3,2},{4,7},{5,4},{6,5},{7,6},{8,11},{9,8},{10,9... | collective-permute-start | bytes 638984 | tf_op jit(solution)/shard_map/ppermute | solution.py:33
  76.2 1.1 collective-permute-done.19.refs_1_
  77.2 2.7 %collective-permute-done.20.refs_2_ = bf16[32,3328]{1,0:T(8,128)(2,1)S(1)} collective-permute-done((bf16[32,3328]{1,0:T(8,128)(2,1)S(1)}, bf16[32,3328]{1,0:T(8,128)(2,1)S(1)}, u32[]{:S(2)}, u32[]{:S(2)}) %collective-permute-start.20) | collective-permute-done | bytes 213024 | tf_op jit(solution)/shard_map/ppermute | solution.py:33
  80.0 0.7 mix_quarters.2
  80.6 2.0 %collective-permute-start.24 = (bf16[32,3328]{1,0:T(8,128)(2,1)S(1)}, bf16[32,3328]{1,0:T(8,128)(2,1)S(1)}, u32[]{:S(2)}, u32[]{:S(2)}) collective-permute-start(bf16[32,3328]{1,0:T(8,128)(2,1)S(1)} %get-tuple-element.95), channel_id=1, source_target_pairs={{0,2},{1,3},{2,0},{3,1},{4,6},{5,7},{6,4},{7,5},{8,10},{9,11},{10,... | collective-permute-start | bytes 638984 | tf_op jit(solution)/shard_map/ppermute | solution.py:33
  82.7 2.1 %collective-permute-start.25 = (bf16[32,3328]{1,0:T(8,128)(2,1)S(1)}, bf16[32,3328]{1,0:T(8,128)(2,1)S(1)}, u32[]{:S(2)}, u32[]{:S(2)}) collective-permute-start(bf16[32,3328]{1,0:T(8,128)(2,1)S(1)} %get-tuple-element.96), channel_id=1, source_target_pairs={{0,1},{1,2},{2,3},{3,0},{4,5},{5,6},{6,7},{7,4},{8,9},{9,10},{10,1... | collective-permute-start | bytes 638984 | tf_op jit(solution)/shard_map/ppermute | solution.py:33
  84.8 1.1 collective-permute-start.26
  85.9 3.2 %collective-permute-done.23.refs_5_ = bf16[3328,128]{1,0:T(8,128)(2,1)S(1)} collective-permute-done((bf16[3328,128]{1,0:T(8,128)(2,1)S(1)}, bf16[3328,128]{1,0:T(8,128)(2,1)S(1)}, u32[]{:S(2)}, u32[]{:S(2)}) %collective-permute-start.23) | collective-permute-done | bytes 852000 | tf_op jit(solution)/shard_map/ppermute | solution.py:33
  89.1 1.0 collective-permute-done.22.refs_2_
  90.1 0.2 collective-permute-done.25.refs_2_
  90.4 0.6 collective-permute-done.26.refs_3_
  91.1 0.5 collective-permute-start.29
  91.8 3.9 %collective-permute-start.30 = (bf16[32,3328]{1,0:T(8,128)(2,1)S(1)}, bf16[32,3328]{1,0:T(8,128)(2,1)S(1)}, u32[]{:S(2)}, u32[]{:S(2)}) collective-permute-start(bf16[32,3328]{1,0:T(8,128)(2,1)S(1)} %get-tuple-element.102), channel_id=1, source_target_pairs={{0,8},{1,9},{2,10},{3,11},{4,12},{5,13},{6,14},{7,15},{8,0},{9,1},... | collective-permute-start | bytes 638984 | tf_op jit(solution)/shard_map/ppermute | solution.py:33
  95.7 1.0 collective-permute-start.31
  96.7 2.2 %collective-permute-start.32 = (bf16[32,3328]{1,0:T(8,128)(2,1)S(1)}, bf16[32,3328]{1,0:T(8,128)(2,1)S(1)}, u32[]{:S(2)}, u32[]{:S(2)}) collective-permute-start(bf16[32,3328]{1,0:T(8,128)(2,1)S(1)} %get-tuple-element.104), channel_id=1, source_target_pairs={{0,12},{1,13},{2,14},{3,15},{4,0},{5,1},{6,2},{7,3},{8,4},{9,5},{1... | collective-permute-start | bytes 638984 | tf_op jit(solution)/shard_map/ppermute | solution.py:33
  98.9 5.5 %early_product.1.refs_4_ = f32[3328,1024]{1,0:T(8,128)S(1)} custom-call(bf16[3328,128]{1,0:T(8,128)(2,1)S(1)} %rotate.1.refs_0_, bf16[3328,128]{1,0:T(8,128)(2,1)S(1)} %collective-permute-done.27.refs_1_, bf16[3328,128]{1,0:T(8,128)(2,1)S(1)} %collective-permute-done.22.refs_2_, bf16[3328,128]{1,0:T(8,128)(2,1)S(1)} %collective-permute-done.28.refs_3_, ...), custom_call_target="tpu_custom_call" | custom-call | flops 1 | bytes 1 | tf_op jit(solution)/shard_map/early_product/pallas_call | solution.py:325
  104.4 0.7 mix_quarters.3
  105.1 0.4 collective-permute-done.33.refs_0_
  105.6 3.9 %collective-permute-start.35 = (bf16[32,3328]{1,0:T(8,128)(2,1)S(1)}, bf16[32,3328]{1,0:T(8,128)(2,1)S(1)}, u32[]{:S(2)}, u32[]{:S(2)}) collective-permute-start(bf16[32,3328]{1,0:T(8,128)(2,1)S(1)} %get-tuple-element.109), channel_id=1, source_target_pairs={{0,8},{1,9},{2,10},{3,11},{4,12},{5,13},{6,14},{7,15},{8,0},{9,1},... | collective-permute-start | bytes 638984 | tf_op jit(solution)/shard_map/ppermute | solution.py:33
  109.4 1.0 collective-permute-start.36
  110.4 2.2 %collective-permute-start.37 = (bf16[32,3328]{1,0:T(8,128)(2,1)S(1)}, bf16[32,3328]{1,0:T(8,128)(2,1)S(1)}, u32[]{:S(2)}, u32[]{:S(2)}) collective-permute-start(bf16[32,3328]{1,0:T(8,128)(2,1)S(1)} %get-tuple-element.111), channel_id=1, source_target_pairs={{0,12},{1,13},{2,14},{3,15},{4,0},{5,1},{6,2},{7,3},{8,4},{9,5},{1... | collective-permute-start | bytes 638984 | tf_op jit(solution)/shard_map/ppermute | solution.py:33
  112.7 3.6 %late_product.1 = bf16[3328,1024]{1,0:T(8,128)(2,1)} custom-call(bf16[3328,128]{1,0:T(8,128)(2,1)S(1)} %collective-permute-done.33.refs_0_, bf16[3328,128]{1,0:T(8,128)(2,1)S(1)} %collective-permute-done.34.refs_1_, bf16[256,1024]{1,0:T(8,128)(2,1)S(1)} %collective-permute-done.3.refs_0_.refs_2_, bf16[3328,1024]{1,0:T(8,128)(2,1)S(1)} %get-tuple-element.107.refs_3_, ...), custom_call_target="tpu_custom_call" | custom-call | flops 1 | bytes 1 | tf_op jit(solution)/shard_map/late_product/pallas_call | solution.py:354
  116.2 0.2 collective-permute-done.36.refs_2_
  116.5 1.0 collect.3
  (39 shorter events, 1.6 us)
Async XLA Ops:
  0.6 19.3 %copy-start = (bf16[128,3328]{1,0:T(8,128)(2,1)S(1)}, bf16[128,3328]{1,0:T(8,128)(2,1)}, u32[]{:S(2)}) copy-start(bf16[128,3328]{1,0:T(8,128)(2,1)} %refs_0_) | copy-start | bytes 2555908
  2.5 2.7 %collective-permute-start = (bf16[4,128,1024]{2,1,0:T(8,128)(2,1)S(1)}, bf16[4,128,1024]{2,1,0:T(8,128)(2,1)S(1)}, u32[]{:S(2)}, u32[]{:S(2)}) collective-permute-start(bf16[4,128,1024]{2,1,0:T(8,128)(2,1)S(1)} %get-tuple-element.59), channel_id=1, source_target_pairs={{0,16},{1,17},{2,18},{3,19},{4,20},{5,21},{6,22},{7,23},{8,24},{9,... | collective-permute-start | bytes 3145736 | tf_op jit(solution)/shard_map/ppermute | solution.py:33
  2.6 17.3 %collective-permute-start.1 = (bf16[128,3328]{1,0:T(8,128)(2,1)}, bf16[128,3328]{1,0:T(8,128)(2,1)S(1)}, u32[]{:S(2)}, u32[]{:S(2)}) collective-permute-start(bf16[128,3328]{1,0:T(8,128)(2,1)} %refs_0_), channel_id=1, source_target_pairs={{0,1},{1,0},{2,3},{3,2},{4,5},{5,4},{6,7},{7,6},{8,9},{9,8},{10,11... | collective-permute-start | bytes 2555912 | tf_op jit(solution)/shard_map/ppermute | solution.py:33
  5.4 16.8 %collective-permute-start.3 = (bf16[256,1024]{1,0:T(8,128)(2,1)S(1)}, bf16[256,1024]{1,0:T(8,128)(2,1)S(1)}, u32[]{:S(2)}, u32[]{:S(2)}) collective-permute-start(bf16[256,1024]{1,0:T(8,128)(2,1)S(1)} %get-tuple-element.65), channel_id=1, source_target_pairs={{0,64},{1,65},{2,66},{3,67},{4,68},{5,69},{6,70},{7,71},{8,72},{9,... | collective-permute-start | bytes 1572872 | tf_op jit(solution)/shard_map/ppermute | solution.py:33
  8.5 23.6 %collective-permute-start.2 = (bf16[512,1024]{1,0:T(8,128)(2,1)S(1)}, bf16[512,1024]{1,0:T(8,128)(2,1)S(1)}, u32[]{:S(2)}, u32[]{:S(2)}) collective-permute-start(bf16[512,1024]{1,0:T(8,128)(2,1)S(1)} %get-tuple-element.64), channel_id=1, source_target_pairs={{0,32},{1,33},{2,34},{3,35},{4,36},{5,37},{6,38},{7,39},{8,40},{9,... | collective-permute-start | bytes 3145736 | tf_op jit(solution)/shard_map/ppermute | solution.py:33
  9.1 0.7 copy-start.1
  20.2 13.9 %collective-permute-start.6 = (bf16[128,3328]{1,0:T(8,128)(2,1)S(1)}, bf16[128,3328]{1,0:T(8,128)(2,1)S(1)}, u32[]{:S(2)}, u32[]{:S(2)}) collective-permute-start(bf16[128,3328]{1,0:T(8,128)(2,1)S(1)} %mix.3.refs_0_), channel_id=1, source_target_pairs={{0,4},{1,5},{2,6},{3,7},{4,0},{5,1},{6,2},{7,3},{8,12},{9,13},{10,... | collective-permute-start | bytes 2555912 | tf_op jit(solution)/shard_map/ppermute | solution.py:33
  24.1 1.8 %collective-permute-start.4 = (bf16[64,3328]{1,0:T(8,128)(2,1)S(1)}, bf16[64,3328]{1,0:T(8,128)(2,1)S(1)}, u32[]{:S(2)}, u32[]{:S(2)}) collective-permute-start(bf16[64,3328]{1,0:T(8,128)(2,1)S(1)} %get-tuple-element.68), channel_id=1, source_target_pairs={{8,24},{9,25},{10,26},{11,27},{12,28},{13,29},{14,30},{15,31},{16,... | collective-permute-start | bytes 1277960 | tf_op jit(solution)/shard_map/ppermute | solution.py:33
  24.2 2.4 %collective-permute-start.5 = (bf16[64,3328]{1,0:T(8,128)(2,1)S(1)}, bf16[64,3328]{1,0:T(8,128)(2,1)S(1)}, u32[]{:S(2)}, u32[]{:S(2)}) collective-permute-start(bf16[64,3328]{1,0:T(8,128)(2,1)S(1)} %get-tuple-element.69), channel_id=1, source_target_pairs={{9,25},{10,26},{11,27},{12,28},{13,29},{14,30},{15,31},{16,0},{17,... | collective-permute-start | bytes 1277960 | tf_op jit(solution)/shard_map/ppermute | solution.py:33
  24.7 13.9 %collective-permute-start.7 = (bf16[128,3328]{1,0:T(8,128)(2,1)S(1)}, bf16[128,3328]{1,0:T(8,128)(2,1)S(1)}, u32[]{:S(2)}, u32[]{:S(2)}) collective-permute-start(bf16[128,3328]{1,0:T(8,128)(2,1)S(1)} %get-tuple-element.74), channel_id=1, source_target_pairs={{1,17},{2,18},{3,19},{4,20},{5,21},{6,22},{7,23},{8,24},{9,25},{10... | collective-permute-start | bytes 2555912 | tf_op jit(solution)/shard_map/ppermute | solution.py:33
  26.8 14.5 %collective-permute-start.9 = (bf16[128,3328]{1,0:T(8,128)(2,1)S(1)}, bf16[128,3328]{1,0:T(8,128)(2,1)S(1)}, u32[]{:S(2)}, u32[]{:S(2)}) collective-permute-start(bf16[128,3328]{1,0:T(8,128)(2,1)S(1)} %add_first.1), channel_id=1, source_target_pairs={{0,32},{1,33},{2,34},{3,35},{4,36},{5,37},{6,38},{7,39},{8,40},{9,... | collective-permute-start | bytes 2555912 | tf_op jit(solution)/shard_map/ppermute | solution.py:33
  34.4 14.3 %collective-permute-start.16 = (bf16[128,3328]{1,0:T(8,128)(2,1)S(1)}, bf16[128,3328]{1,0:T(8,128)(2,1)S(1)}, u32[]{:S(2)}, u32[]{:S(2)}) collective-permute-start(bf16[128,3328]{1,0:T(8,128)(2,1)S(1)} %mix.4.refs_0_), channel_id=1, source_target_pairs={{0,2},{1,3},{2,0},{3,1},{4,6},{5,7},{6,4},{7,5},{8,10},{9,11},{10,... | collective-permute-start | bytes 2555912 | tf_op jit(solution)/shard_map/ppermute | solution.py:33
  37.8 1.9 %collective-permute-start.10 = (bf16[128,1024]{1,0:T(8,128)(2,1)S(1)}, bf16[128,1024]{1,0:T(8,128)(2,1)S(1)}, u32[]{:S(2)}, u32[]{:S(2)}) collective-permute-start(bf16[128,1024]{1,0:T(8,128)(2,1)S(1)} %get-tuple-element.112), channel_id=1, source_target_pairs={{3,19},{4,20},{5,21},{6,22},{7,23},{8,24},{9,25},{10,26},{11,27},{... | collective-permute-start | bytes 786440 | tf_op jit(solution)/shard_map/ppermute | solution.py:33
  38.5 1.5 %collective-permute-start.8 = (bf16[128,1024]{1,0:T(8,128)(2,1)S(1)}, bf16[128,1024]{1,0:T(8,128)(2,1)S(1)}, u32[]{:S(2)}, u32[]{:S(2)}) collective-permute-start(bf16[128,1024]{1,0:T(8,128)(2,1)S(1)} %get-tuple-element.113), channel_id=1, source_target_pairs={{2,18},{3,19},{4,20},{5,21},{6,22},{7,23},{8,24},{9,25},{10,26},{1... | collective-permute-start | bytes 786440 | tf_op jit(solution)/shard_map/ppermute | solution.py:33
  38.6 5.2 %collective-permute-start.11 = (bf16[64,3328]{1,0:T(8,128)(2,1)S(1)}, bf16[64,3328]{1,0:T(8,128)(2,1)S(1)}, u32[]{:S(2)}, u32[]{:S(2)}) collective-permute-start(bf16[64,3328]{1,0:T(8,128)(2,1)S(1)} %get-tuple-element.80), channel_id=1, source_target_pairs={{6,22},{7,23},{8,24},{9,25},{10,26},{11,27},{12,28},{13,29},{14,30... | collective-permute-start | bytes 1277960 | tf_op jit(solution)/shard_map/ppermute | solution.py:33
  39.7 4.1 %collective-permute-start.12 = (bf16[64,3328]{1,0:T(8,128)(2,1)S(1)}, bf16[64,3328]{1,0:T(8,128)(2,1)S(1)}, u32[]{:S(2)}, u32[]{:S(2)}) collective-permute-start(bf16[64,3328]{1,0:T(8,128)(2,1)S(1)} %get-tuple-element.81), channel_id=1, source_target_pairs={{7,23},{8,24},{9,25},{10,26},{11,27},{12,28},{13,29},{14,30},{15,3... | collective-permute-start | bytes 1277960 | tf_op jit(solution)/shard_map/ppermute | solution.py:33
  40.0 5.5 %collective-permute-start.14 = (bf16[64,3328]{1,0:T(8,128)(2,1)S(1)}, bf16[64,3328]{1,0:T(8,128)(2,1)S(1)}, u32[]{:S(2)}, u32[]{:S(2)}) collective-permute-start(bf16[64,3328]{1,0:T(8,128)(2,1)S(1)} %get-tuple-element.83), channel_id=1, source_target_pairs={{5,21},{6,22},{7,23},{8,24},{9,25},{10,26},{11,27},{12,28},{13,29}... | collective-permute-start | bytes 1277960 | tf_op jit(solution)/shard_map/ppermute | solution.py:33
  41.3 4.3 %collective-permute-start.13 = (bf16[64,3328]{1,0:T(8,128)(2,1)S(1)}, bf16[64,3328]{1,0:T(8,128)(2,1)S(1)}, u32[]{:S(2)}, u32[]{:S(2)}) collective-permute-start(bf16[64,3328]{1,0:T(8,128)(2,1)S(1)} %get-tuple-element.71), channel_id=1, source_target_pairs={{4,20},{5,21},{6,22},{7,23},{8,24},{9,25},{10,26},{11,27},{12,28},... | collective-permute-start | bytes 1277960 | tf_op jit(solution)/shard_map/ppermute | solution.py:33
  44.1 14.0 %collective-permute-start.17 = (bf16[128,3328]{1,0:T(8,128)(2,1)S(1)}, bf16[128,3328]{1,0:T(8,128)(2,1)S(1)}, u32[]{:S(2)}, u32[]{:S(2)}) collective-permute-start(bf16[128,3328]{1,0:T(8,128)(2,1)S(1)} %add_third.1), channel_id=1, source_target_pairs={{0,32},{1,33},{2,34},{3,35},{4,36},{5,37},{6,38},{7,39},{8,40},{9,... | collective-permute-start | bytes 2555912 | tf_op jit(solution)/shard_map/ppermute | solution.py:33
  45.7 19.5 %collective-permute-start.15 = (bf16[128,3328]{1,0:T(8,128)(2,1)S(1)}, bf16[128,3328]{1,0:T(8,128)(2,1)S(1)}, u32[]{:S(2)}, u32[]{:S(2)}) collective-permute-start(bf16[128,3328]{1,0:T(8,128)(2,1)S(1)} %add_second.1), channel_id=1, source_target_pairs={{0,48},{1,49},{2,50},{3,51},{4,52},{5,53},{6,54},{7,55},{8,56},{9,... | collective-permute-start | bytes 2555912 | tf_op jit(solution)/shard_map/ppermute | solution.py:33
  48.9 16.6 %collective-permute-start.18 = (bf16[128,3328]{1,0:T(8,128)(2,1)S(1)}, bf16[128,3328]{1,0:T(8,128)(2,1)S(1)}, u32[]{:S(2)}, u32[]{:S(2)}) collective-permute-start(bf16[128,3328]{1,0:T(8,128)(2,1)S(1)} %mix.5.value_ref), channel_id=1, source_target_pairs={{0,8},{1,9},{2,10},{3,11},{4,12},{5,13},{6,14},{7,15},{8,0},{9,1},... | collective-permute-start | bytes 2555912 | tf_op jit(solution)/shard_map/ppermute | solution.py:33
  66.2 22.9 %collective-permute-start.23 = (bf16[3328,128]{1,0:T(8,128)(2,1)S(1)}, bf16[3328,128]{1,0:T(8,128)(2,1)S(1)}, u32[]{:S(2)}, u32[]{:S(2)}) collective-permute-start(bf16[3328,128]{1,0:T(8,128)(2,1)S(1)} %rotate.1.refs_0_), channel_id=1, source_target_pairs={{0,96},{1,97},{2,98},{3,99},{4,100},{5,101},{6,102},{7,103},{8,104... | collective-permute-start | bytes 2555912 | tf_op jit(solution)/shard_map/ppermute | solution.py:33
  69.9 20.2 %collective-permute-start.22 = (bf16[3328,128]{1,0:T(8,128)(2,1)S(1)}, bf16[3328,128]{1,0:T(8,128)(2,1)S(1)}, u32[]{:S(2)}, u32[]{:S(2)}) collective-permute-start(bf16[3328,128]{1,0:T(8,128)(2,1)S(1)} %rotate.1.refs_0_), channel_id=1, source_target_pairs={{0,32},{1,33},{2,34},{3,35},{4,36},{5,37},{6,38},{7,39},{8,40},{9,... | collective-permute-start | bytes 2555912 | tf_op jit(solution)/shard_map/ppermute | solution.py:33
  69.9 7.3 %collective-permute-start.19 = (bf16[32,3328]{1,0:T(8,128)(2,1)S(1)}, bf16[32,3328]{1,0:T(8,128)(2,1)S(1)}, u32[]{:S(2)}, u32[]{:S(2)}) collective-permute-start(bf16[32,3328]{1,0:T(8,128)(2,1)S(1)} %get-tuple-element.90), channel_id=1, source_target_pairs={{0,2},{1,3},{2,0},{3,1},{4,6},{5,7},{6,4},{7,5},{8,10},{9,11},{10,... | collective-permute-start | bytes 638984 | tf_op jit(solution)/shard_map/ppermute | solution.py:33
  72.9 7.1 %collective-permute-start.20 = (bf16[32,3328]{1,0:T(8,128)(2,1)S(1)}, bf16[32,3328]{1,0:T(8,128)(2,1)S(1)}, u32[]{:S(2)}, u32[]{:S(2)}) collective-permute-start(bf16[32,3328]{1,0:T(8,128)(2,1)S(1)} %get-tuple-element.91), channel_id=1, source_target_pairs={{0,1},{1,2},{2,3},{3,0},{4,5},{5,6},{6,7},{7,4},{8,9},{9,10},{10,1... | collective-permute-start | bytes 638984 | tf_op jit(solution)/shard_map/ppermute | solution.py:33
  73.8 6.2 %collective-permute-start.21 = (bf16[32,3328]{1,0:T(8,128)(2,1)S(1)}, bf16[32,3328]{1,0:T(8,128)(2,1)S(1)}, u32[]{:S(2)}, u32[]{:S(2)}) collective-permute-start(bf16[32,3328]{1,0:T(8,128)(2,1)S(1)} %get-tuple-element.92), channel_id=1, source_target_pairs={{0,3},{1,0},{2,1},{3,2},{4,7},{5,4},{6,5},{7,6},{8,11},{9,8},{10,9... | collective-permute-start | bytes 638984 | tf_op jit(solution)/shard_map/ppermute | solution.py:33
  80.6 9.5 %collective-permute-start.24 = (bf16[32,3328]{1,0:T(8,128)(2,1)S(1)}, bf16[32,3328]{1,0:T(8,128)(2,1)S(1)}, u32[]{:S(2)}, u32[]{:S(2)}) collective-permute-start(bf16[32,3328]{1,0:T(8,128)(2,1)S(1)} %get-tuple-element.95), channel_id=1, source_target_pairs={{0,2},{1,3},{2,0},{3,1},{4,6},{5,7},{6,4},{7,5},{8,10},{9,11},{10,... | collective-permute-start | bytes 638984 | tf_op jit(solution)/shard_map/ppermute | solution.py:33
  82.7 7.7 %collective-permute-start.25 = (bf16[32,3328]{1,0:T(8,128)(2,1)S(1)}, bf16[32,3328]{1,0:T(8,128)(2,1)S(1)}, u32[]{:S(2)}, u32[]{:S(2)}) collective-permute-start(bf16[32,3328]{1,0:T(8,128)(2,1)S(1)} %get-tuple-element.96), channel_id=1, source_target_pairs={{0,1},{1,2},{2,3},{3,0},{4,5},{5,6},{6,7},{7,4},{8,9},{9,10},{10,1... | collective-permute-start | bytes 638984 | tf_op jit(solution)/shard_map/ppermute | solution.py:33
  84.8 6.1 %collective-permute-start.26 = (bf16[32,3328]{1,0:T(8,128)(2,1)S(1)}, bf16[32,3328]{1,0:T(8,128)(2,1)S(1)}, u32[]{:S(2)}, u32[]{:S(2)}) collective-permute-start(bf16[32,3328]{1,0:T(8,128)(2,1)S(1)} %get-tuple-element.97), channel_id=1, source_target_pairs={{0,3},{1,0},{2,1},{3,2},{4,7},{5,4},{6,5},{7,6},{8,11},{9,8},{10,9... | collective-permute-start | bytes 638984 | tf_op jit(solution)/shard_map/ppermute | solution.py:33
  89.1 6.6 %collective-permute-start.27 = (bf16[3328,128]{1,0:T(8,128)(2,1)S(1)}, bf16[3328,128]{1,0:T(8,128)(2,1)S(1)}, u32[]{:S(2)}, u32[]{:S(2)}) collective-permute-start(bf16[3328,128]{1,0:T(8,128)(2,1)S(1)} %rotate.1.refs_0_), channel_id=1, source_target_pairs={{11,27},{12,28},{13,29},{14,30},{15,31},{16,0},{17,1},{18,2},{19,3... | collective-permute-start | bytes 2555912 | tf_op jit(solution)/shard_map/ppermute | solution.py:33
  91.1 5.7 %collective-permute-start.28 = (bf16[3328,128]{1,0:T(8,128)(2,1)S(1)}, bf16[3328,128]{1,0:T(8,128)(2,1)S(1)}, u32[]{:S(2)}, u32[]{:S(2)}) collective-permute-start(bf16[3328,128]{1,0:T(8,128)(2,1)S(1)} %collective-permute-done.23.refs_5_), channel_id=1, source_target_pairs={{13,29},{14,30},{15,31},{16,0},{17,1},{18,2},{19,3},{20,4},{21,5},... | collective-permute-start | bytes 2555912 | tf_op jit(solution)/shard_map/ppermute | solution.py:33
  91.1 7.8 %collective-permute-start.29 = (bf16[3328,128]{1,0:T(8,128)(2,1)S(1)}, bf16[3328,128]{1,0:T(8,128)(2,1)S(1)}, u32[]{:S(2)}, u32[]{:S(2)}) collective-permute-start(bf16[3328,128]{1,0:T(8,128)(2,1)S(1)} %collective-permute-done.22.refs_2_), channel_id=1, source_target_pairs={{12,28},{13,29},{14,30},{15,31},{16,0},{17,1},{18,2},{19,3},{20,4}... | collective-permute-start | bytes 2555912 | tf_op jit(solution)/shard_map/ppermute | solution.py:33
  91.6 13.9 %collective-permute-start.33 = (bf16[3328,128]{1,0:T(8,128)(2,1)S(1)}, bf16[3328,128]{1,0:T(8,128)(2,1)S(1)}, u32[]{:S(2)}, u32[]{:S(2)}) collective-permute-start(bf16[3328,128]{1,0:T(8,128)(2,1)S(1)} %collective-permute-done.22.refs_2_), channel_id=1, source_target_pairs={{0,32},{1,33},{2,34},{3,35},{4,36},{5,37},{6,38},{7,39},{8,40},{9,... | collective-permute-start | bytes 2555912 | tf_op jit(solution)/shard_map/ppermute | solution.py:33
  91.8 12.6 %collective-permute-start.30 = (bf16[32,3328]{1,0:T(8,128)(2,1)S(1)}, bf16[32,3328]{1,0:T(8,128)(2,1)S(1)}, u32[]{:S(2)}, u32[]{:S(2)}) collective-permute-start(bf16[32,3328]{1,0:T(8,128)(2,1)S(1)} %get-tuple-element.102), channel_id=1, source_target_pairs={{0,8},{1,9},{2,10},{3,11},{4,12},{5,13},{6,14},{7,15},{8,0},{9,1},... | collective-permute-start | bytes 638984 | tf_op jit(solution)/shard_map/ppermute | solution.py:33
  95.7 8.7 %collective-permute-start.31 = (bf16[32,3328]{1,0:T(8,128)(2,1)S(1)}, bf16[32,3328]{1,0:T(8,128)(2,1)S(1)}, u32[]{:S(2)}, u32[]{:S(2)}) collective-permute-start(bf16[32,3328]{1,0:T(8,128)(2,1)S(1)} %get-tuple-element.103), channel_id=1, source_target_pairs={{0,4},{1,5},{2,6},{3,7},{4,8},{5,9},{6,10},{7,11},{8,12},{9,13},{1... | collective-permute-start | bytes 638984 | tf_op jit(solution)/shard_map/ppermute | solution.py:33
  96.7 7.7 %collective-permute-start.32 = (bf16[32,3328]{1,0:T(8,128)(2,1)S(1)}, bf16[32,3328]{1,0:T(8,128)(2,1)S(1)}, u32[]{:S(2)}, u32[]{:S(2)}) collective-permute-start(bf16[32,3328]{1,0:T(8,128)(2,1)S(1)} %get-tuple-element.104), channel_id=1, source_target_pairs={{0,12},{1,13},{2,14},{3,15},{4,0},{5,1},{6,2},{7,3},{8,4},{9,5},{1... | collective-permute-start | bytes 638984 | tf_op jit(solution)/shard_map/ppermute | solution.py:33
  105.5 7.1 %collective-permute-start.34 = (bf16[3328,128]{1,0:T(8,128)(2,1)S(1)}, bf16[3328,128]{1,0:T(8,128)(2,1)S(1)}, u32[]{:S(2)}, u32[]{:S(2)}) collective-permute-start(bf16[3328,128]{1,0:T(8,128)(2,1)S(1)} %collective-permute-done.33.refs_0_), channel_id=1, source_target_pairs={{14,30},{15,31},{16,0},{17,1},{18,2},{19,3},{20,4},{21,5},{22,6},{... | collective-permute-start | bytes 2555912 | tf_op jit(solution)/shard_map/ppermute | solution.py:33
  105.6 10.7 %collective-permute-start.35 = (bf16[32,3328]{1,0:T(8,128)(2,1)S(1)}, bf16[32,3328]{1,0:T(8,128)(2,1)S(1)}, u32[]{:S(2)}, u32[]{:S(2)}) collective-permute-start(bf16[32,3328]{1,0:T(8,128)(2,1)S(1)} %get-tuple-element.109), channel_id=1, source_target_pairs={{0,8},{1,9},{2,10},{3,11},{4,12},{5,13},{6,14},{7,15},{8,0},{9,1},... | collective-permute-start | bytes 638984 | tf_op jit(solution)/shard_map/ppermute | solution.py:33
  109.4 7.1 %collective-permute-start.36 = (bf16[32,3328]{1,0:T(8,128)(2,1)S(1)}, bf16[32,3328]{1,0:T(8,128)(2,1)S(1)}, u32[]{:S(2)}, u32[]{:S(2)}) collective-permute-start(bf16[32,3328]{1,0:T(8,128)(2,1)S(1)} %get-tuple-element.110), channel_id=1, source_target_pairs={{0,4},{1,5},{2,6},{3,7},{4,8},{5,9},{6,10},{7,11},{8,12},{9,13},{1... | collective-permute-start | bytes 638984 | tf_op jit(solution)/shard_map/ppermute | solution.py:33
  110.4 6.1 %collective-permute-start.37 = (bf16[32,3328]{1,0:T(8,128)(2,1)S(1)}, bf16[32,3328]{1,0:T(8,128)(2,1)S(1)}, u32[]{:S(2)}, u32[]{:S(2)}) collective-permute-start(bf16[32,3328]{1,0:T(8,128)(2,1)S(1)} %get-tuple-element.111), channel_id=1, source_target_pairs={{0,12},{1,13},{2,14},{3,15},{4,0},{5,1},{6,2},{7,3},{8,4},{9,5},{1... | collective-permute-start | bytes 638984 | tf_op jit(solution)/shard_map/ppermute | solution.py:33

commit v4 on v3

--- a/solution.py
+++ b/solution.py
@@ -9,6 +9,7 @@
 
 HB = 256
 SCALE = 64.0
+THIRD_FLOPS = 2 * 10**9
 BEHIND = (0, 2, 1, 3)
 AXES = ("x", "core", "z", "y")
 BF16 = jnp.bfloat16
@@ -148,8 +149,7 @@
     return [pltpu.VMEM((ff, cols), BF16), pltpu.SemaphoreType.DMA((ff // HB,))]
 
 
-def quantize_kernel(table_ref, weight_ref, inv_ref, grad_ref, turned_ref, keep_ref, *refs):
-    outs, (held, sems) = refs[:-2], refs[-2:]
+def quantize_kernel(table_ref, weight_ref, inv_ref, turned_ref, keep_ref, held, sems):
     copies = stream(weight_ref, held, sems)
     inv = inv_ref[...]
     step = (1.0 / SCALE) / inv
@@ -161,49 +161,42 @@
         keep_ref[part, :] = jnp.where(raw_code == code, 1.0, 0.0).astype(BF16)
         turned = jnp.dot(table_ref[...], code.astype(BF16), preferred_element_type=F32)
         turned_ref[part, :] = (turned * step).astype(BF16)
-        result = lax.dot_general(
-            grad_ref[...], turned_ref[part, :], (((1,), (1,)), ((), ())), preferred_element_type=F32
-        ).astype(BF16)
-        store_rows(result, [out.at[:, part] for out in outs])
-
-
-def quantize(table, weight, inv, grads, rows):
+
+
+def quantize(table, weight, inv):
     ff, cols = weight.shape
     return call(
         quantize_kernel,
         "quantize",
         14,
-        [VMEM, ANY, VMEM, VMEM],
-        [VMEM] * (2 + len(rows)),
-        [pltpu.VMEM((ff, cols), BF16)] * 2 + [pltpu.VMEM((count, ff), BF16) for count in rows],
+        [VMEM, ANY, VMEM],
+        [VMEM] * 2,
+        [pltpu.VMEM((ff, cols), BF16)] * 2,
         streamed(ff, cols),
-    )(table, in_hbm(weight), inv, grads)
-
-
-def product_kernel(count, *refs):
-    grads, turned_ref, outs = refs[:count], refs[count], refs[count + 1 :]
-    rows = sum(out.shape[0] for out in outs) // count
+    )(table, in_hbm(weight), inv)
+
+
+def product_kernel(takes, *refs):
+    grads, turned_ref, outs = refs[: len(takes)], refs[len(takes)], refs[len(takes) + 1 :]
+    left = [ref[:rows, :] for ref, rows in zip(grads, takes)]
+    left = left[0] if len(left) == 1 else jnp.concatenate(left)
     for i in range(turned_ref.shape[0] // HB):
         part = pl.ds(i * HB, HB)
         result = lax.dot_general(
-            jnp.concatenate([ref[:rows, :] for ref in grads]) if count > 1 else grads[0][:rows, :],
-            turned_ref[part, :],
-            (((1,), (1,)), ((), ())),
-            preferred_element_type=F32,
+            left, turned_ref[part, :], (((1,), (1,)), ((), ())), preferred_element_type=F32
         ).astype(BF16)
         store_rows(result, [out.at[:, part] for out in outs])
 
 
-def product(grads, turned, rows, flops=1):
+def product(grads, takes, turned, rows):
     ff = turned.shape[0]
     return call(
-        functools.partial(product_kernel, len(grads)),
+        functools.partial(product_kernel, takes),
         "product",
-        8,
+        10,
         [VMEM] * (len(grads) + 1),
         [VMEM] * len(rows),
         [pltpu.VMEM((size, ff), BF16) for size in rows],
-        flops=flops,
     )(*grads, turned)
 
 
@@ -225,7 +218,7 @@
         store_rows(total.astype(BF16), [out.at[:, part] for out in outs])
 
 
-def add(name, rows, *terms):
+def add(name, rows, *terms, flops=1):
     first_rows = [term[1] if isinstance(term, tuple) else 0 for term in terms]
     terms = [
         term if isinstance(term, list) else [term[0] if isinstance(term, tuple) else term]
@@ -240,6 +233,7 @@
         [VMEM] * len(flat),
         [VMEM] * len(rows),
         [pltpu.VMEM((count, ff), BF16) for count in rows],
+        flops=flops,
     )(*flat)
 
 
@@ -250,53 +244,54 @@
     return jnp.where(jnp.bitwise_and(place, bit) == 0, 1.0, -1.0).astype(F32)
 
 
-def mix_kernel(step, *refs):
-    sign = my_sign(step)
-    half = len(refs) // 2
-    values, partners, out_ref = refs[:half], refs[half:-1], refs[-1]
-    row = 0
-    for value_ref, partner_ref in zip(values, partners):
-        rows = pl.ds(row, value_ref.shape[0])
-        row += value_ref.shape[0]
-        for i in range(value_ref.shape[1] // HB):
-            part = pl.ds(i * HB, HB)
-            total = value_ref[:, part].astype(F32) * sign + partner_ref[:, part].astype(F32)
-            out_ref[rows, part] = total.astype(BF16)
-
-
-def mix(name, step, values, partners, last=False):
-    shape = (sum(value.shape[0] for value in values), values[0].shape[1])
-    return call(
-        functools.partial(mix_kernel, step),
-        name,
-        6,
-        [VMEM] * (2 * len(values)),
-        VMEM,
-        jax.ShapeDtypeStruct(shape, BF16) if last else pltpu.VMEM(shape, BF16),
-    )(*values, *partners)
-
-
-def rotate_kernel(step, table_ref, value_ref, partner_ref, rotated_ref):
+def mix_kernel(step, value_ref, partner_ref, *outs):
     sign = my_sign(step)
     for i in range(value_ref.shape[1] // HB):
         part = pl.ds(i * HB, HB)
-        mix = value_ref[:, part].astype(F32) * sign + partner_ref[:, part].astype(F32)
+        total = value_ref[:, part].astype(F32) * sign + partner_ref[:, part].astype(F32)
+        store_rows(total.astype(BF16), [out.at[:, part] for out in outs])
+
+
+def mix(step, value, partner, rows):
+    ff = value.shape[1]
+    return call(
+        functools.partial(mix_kernel, step),
+        "mix",
+        6,
+        [VMEM] * 2,
+        [VMEM] * len(rows),
+        [pltpu.VMEM((count, ff), BF16) for count in rows],
+    )(value, partner)
+
+
+def rotate_kernel(step, table_ref, *refs):
+    sign = my_sign(step)
+    values, partners, rotated_ref = refs[: len(refs) // 2], refs[len(refs) // 2 : -1], refs[-1]
+    for i in range(rotated_ref.shape[0] // HB):
+        part = pl.ds(i * HB, HB)
+        mixed = jnp.concatenate(
+            [
+                (value[:, part].astype(F32) * sign + partner[:, part].astype(F32)).astype(BF16)
+                for value, partner in zip(values, partners)
+            ]
+        )
         turned = lax.dot_general(
-            table_ref[...], mix.astype(BF16), (((1,), (1,)), ((), ())), preferred_element_type=F32
+            table_ref[...], mixed, (((1,), (1,)), ((), ())), preferred_element_type=F32
         )
         rotated_ref[part, :] = (turned * (1.0 / SCALE)).astype(BF16)
 
 
-def rotate(table, step, value, partner):
-    tokens, ff = value.shape
+def rotate(table, step, values, partners):
+    ff = values[0].shape[1]
+    tokens = sum(value.shape[0] for value in values)
     return call(
         functools.partial(rotate_kernel, step),
         "rotate",
         8,
-        [VMEM] * 3,
+        [VMEM] * (1 + 2 * len(values)),
         VMEM,
         pltpu.VMEM((ff, tokens), BF16),
-    )(table, value, partner)
+    )(table, *values, *partners)
 
 
 def partial_sum(rotated, grads, part):
@@ -484,36 +479,42 @@
     got = partner(hidden, 0)
     to_opp, own, to_ahead = pair(kept, swap(given))
     opp, bwd = across(to_opp), forward(to_ahead)
-    turned, keep, own_mine, own_other = quantize(table, weight, inv, own, whole * 2)
-    own_other = swap(own_other, 1)
-
-    hid = mix("mix", 0, [after(hidden, turned)], [got])
+    turned, keep = quantize(table, after(weight, own), inv)
+
+    (hid,) = mix(0, after(hidden, turned), got, whole)
     got = partner(hid, 1)
-    opp_mine, *opp_other = product([after(opp, hid)], turned, whole + halves)
+    opp_mine, *opp_other = product([after(opp, hid)], (2 * tokens,), turned, whole + halves)
     opp_other = [swap(opp_other[j], 8 + j) for j in (0, 1)]
     (first_send,) = add("add_first", whole, opp_mine, opp_other)
     first = forward(first_send)
-    bwd = after(bwd, first_send)
+    own_mine, own_other = product([after(own, first_send)], (2 * tokens,), turned, whole * 2)
+    own_other = swap(own_other, 1)
+    (hid,) = mix(1, after(hid, own_mine), got, whole)
+    got = partner(hid, 2)
+    bwd = after(bwd, hid)
     fwd = [swap(bwd[(2 + j) * tokens : (3 + j) * tokens], 2 + j) for j in (0, 1)]
-    bwd_parts = product([bwd], turned, halves * 2)
+    *bwd_parts, fwd_other, fwd_mine, fwd_mine_rest = product(
+        [bwd] + fwd, (2 * tokens, tokens, tokens), turned, halves * 2 + whole + halves
+    )
     bwd_mine = [swap(bwd_parts[j], 4 + j) for j in (0, 1)]
     bwd_other = [swap(bwd_parts[2 + j], 6 + j) for j in (0, 1)]
-    hid = mix("mix", 1, [after(hid, bwd_parts[0])], [got])
-    got = partner(hid, 2)
-    (own_sum,) = add("add_own", whole, after(own_mine, hid), own_other)
-    fwd_other, *fwd_mine = product(
-        [after(fwd[0], own_sum, first), fwd[1]], turned, whole + halves
+    (own_sum,) = add("add_own", whole, after(own_mine, fwd_other), own_other)
+    (third_send,) = add(
+        "add_third",
+        whole,
+        after(first, own_sum),
+        [fwd_mine, fwd_mine_rest],
+        bwd_other,
+        flops=THIRD_FLOPS,
     )
-    (third_send,) = add("add_third", whole, after(first, fwd_other), list(fwd_mine), bwd_other)
     third = forward(third_send)
     (second_send,) = add("add_second", whole, after(fwd_other, third_send), bwd_mine)
     second = forward_crossed(second_send)
-    hid = mix("mix", 2, [after(hid, second_send)], [got])
-    got = partner(hid, 3)
-
-    pieces = deal("deal_grad", 0, own_sum, after(second, hid), after(third, hid))
+    hid = list(mix(2, after(hid, second_send), got, halves))
+    got = [partner(piece, 3) for piece in hid]
+    rotated = rotate(table, 3, hid, got)
+    pieces = deal("deal_grad", 0, own_sum, after(second, rotated), after(third, rotated))
     values = spread(pieces, 0)
-    rotated = rotate(table, 3, after(hid, pieces[0]), got)
     bwd_a, fwd_a = forward(rotated), backward(rotated)
     other = swap(rotated, 11)
     pieces = mix_quarters(0, [after(values[0], rotated)] + values[1:])

time: 118 us -> 116 us (0.983)
  waiting for transfers between devices: 32.9 us -> 30.5 us
  starting transfers between devices: 51.1 us -> 53.1 us
    ppermute x38 -> x39, waiting for transfers between devices: 32.9 us -> 30.5 us  [move(): return lax.ppermute(value, AXES, pairs[turn:] + pairs[:turn])]
    ppermute x38 -> x39, starting transfers between devices: 51.1 us -> 53.1 us  [move(): return lax.ppermute(value, AXES, pairs[turn:] + pairs[:turn])]
  transfers between devices with their start and end apart: 38 -> 39, of which waited for: 18 -> 21; matrix products, arithmetic and copies ran while one was open for 0% -> 0% of each run, Pallas kernels for 24% -> 24%
where the time goes in v4:
time: 116 us
  starting transfers between devices  53.1 us (46%)
  Pallas kernels  30.9 us (27%)
  waiting for transfers between devices  30.5 us (26%)
    ppermute x39, starting transfers between devices, move(): return lax.ppermute(value, AXES, pairs[turn:] + pairs[:turn])  53.1 us
    ppermute x39, waiting for transfers between devices, move(): return lax.ppermute(value, AXES, pairs[turn:] + pairs[:turn])  30.5 us
    pallas_call x1, Pallas kernels, quantize(): call(quantize_kernel, 'quantize', 14, [VMEM, ANY, VMEM], [VMEM] * 2, [plt...  7.73 us
    pallas_call x3, Pallas kernels, product(): call(functools.partial(product_kernel, takes), 'product', 10, [VMEM] * (l...  7.68 us
    pallas_call x1, Pallas kernels, early_product(): call(functools.partial(early_kernel, blocks), 'early_product', 10, [VMEM]...  5.46 us
    pallas_call x1, Pallas kernels, late_product(): call(functools.partial(late_kernel, blocks), 'late_product', 14, [VMEM] *...  3.24 us
  transfers between devices with their start and end apart: 39, of which 21 were waited for; matrix products, arithmetic and copies ran while one was open for 0% of the time, Pallas kernels for 24%

profile of v4, /device:TPU:0, one launch (start us, length us, event | category | flops | bytes accessed | tf_op | source)
XLA Modules:
  0.0 116.3 jit_solution(17636136420283047633)
XLA Ops:
  0.8 1.7 %split.1 = (bf16[4,128,1024]{2,1,0:T(8,128)(2,1)S(1)}, bf16[4,128,1024]{2,1,0:T(8,128)(2,1)S(1)}) custom-call(bf16[128,8192]{1,0:T(8,128)(2,1)} %grad_ref), custom_call_target="tpu_custom_call" | custom-call | flops 1 | bytes 1 | tf_op jit(solution)/shard_map/split/pallas_call | solution.py:106
  2.6 1.7 %collective-permute-start.2 = (bf16[128,3328]{1,0:T(8,128)(2,1)}, bf16[128,3328]{1,0:T(8,128)(2,1)S(1)}, u32[]{:S(2)}, u32[]{:S(2)}) collective-permute-start(bf16[128,3328]{1,0:T(8,128)(2,1)} %value_ref), channel_id=1, source_target_pairs={{0,1},{1,0},{2,3},{3,2},{4,5},{5,4},{6,7},{7,6},{8,9},{9,8},{10,11... | collective-permute-start | bytes 2555912 | tf_op jit(solution)/shard_map/ppermute | solution.py:34
  4.3 0.9 collective-permute-done.got_ref
  5.4 3.2 %collective-permute-start.1 = (bf16[256,1024]{1,0:T(8,128)(2,1)S(1)}, bf16[256,1024]{1,0:T(8,128)(2,1)S(1)}, u32[]{:S(2)}, u32[]{:S(2)}) collective-permute-start(bf16[256,1024]{1,0:T(8,128)(2,1)S(1)} %get-tuple-element.63), channel_id=1, source_target_pairs={{0,64},{1,65},{2,66},{3,67},{4,68},{5,69},{6,70},{7,71},{8,72},{9,... | collective-permute-start | bytes 1572872 | tf_op jit(solution)/shard_map/ppermute | solution.py:34
  8.5 0.6 collective-permute-start.5
  9.1 0.7 copy-done.1
  9.8 7.7 %quantize.1 = (bf16[3328,1024]{1,0:T(8,128)(2,1)S(1)}, bf16[3328,1024]{1,0:T(8,128)(2,1)S(1)}) custom-call(bf16[256,256]{1,0:T(8,128)(2,1)S(1)} %fusion.3.table_ref, bf16[3328,1024]{1,0:T(8,128)(2,1)} %weight_ref, f32[1,1024]{1,0:T(1,128)S(1)} %bitcast.1), custom_call_target="tpu_custom_call" | custom-call | flops 1 | bytes 1 | tf_op jit(solution)/shard_map/quantize/pallas_call | solution.py:168
  17.6 0.3 mix.3.value_ref
  17.8 2.0 %collective-permute-start.6 = (bf16[128,3328]{1,0:T(8,128)(2,1)S(1)}, bf16[128,3328]{1,0:T(8,128)(2,1)S(1)}, u32[]{:S(2)}, u32[]{:S(2)}) collective-permute-start(bf16[128,3328]{1,0:T(8,128)(2,1)S(1)} %mix.3.value_ref), channel_id=1, source_target_pairs={{0,4},{1,5},{2,6},{3,7},{4,0},{5,1},{6,2},{7,3},{8,12},{9,13},{10,... | collective-permute-start | bytes 2555912 | tf_op jit(solution)/shard_map/ppermute | solution.py:34
  19.8 1.2 %collective-permute-done.1.refs_0_.refs_2_ = bf16[256,1024]{1,0:T(8,128)(2,1)S(1)} collective-permute-done((bf16[256,1024]{1,0:T(8,128)(2,1)S(1)}, bf16[256,1024]{1,0:T(8,128)(2,1)S(1)}, u32[]{:S(2)}, u32[]{:S(2)}) %collective-permute-start.1) | collective-permute-done | bytes 524320 | tf_op jit(solution)/shard_map/ppermute | solution.py:34
  21.0 2.0 %product.3 = (bf16[128,3328]{1,0:T(8,128)(2,1)S(1)}, bf16[64,3328]{1,0:T(8,128)(2,1)S(1)}, bf16[64,3328]{1,0:T(8,128)(2,1)S(1)}) custom-call(bf16[256,1024]{1,0:T(8,128)(2,1)S(1)} %collective-permute-done.1.refs_0_.refs_2_, bf16[3328,1024]{1,0:T(8,128)(2,1)S(1)} %get-tuple-element.65.refs_1_.refs_3_), custom_call_target="tpu_custom_call" | custom-call | flops 1 | bytes 1 | tf_op jit(solution)/shard_map/product/pallas_call | solution.py:193
  23.1 0.5 collective-permute-start.4
  23.6 1.3 %collective-permute-done.3.refs_1_ = bf16[64,3328]{1,0:T(8,128)(2,1)S(1)} collective-permute-done((bf16[64,3328]{1,0:T(8,128)(2,1)S(1)}, bf16[64,3328]{1,0:T(8,128)(2,1)S(1)}, u32[]{:S(2)}, u32[]{:S(2)}) %collective-permute-start.3) | collective-permute-done | bytes 426016 | tf_op jit(solution)/shard_map/ppermute | solution.py:34
  24.8 0.6 collective-permute-done.4.refs_2_
  25.6 2.4 %collective-permute-start.10 = (bf16[128,3328]{1,0:T(8,128)(2,1)S(1)}, bf16[128,3328]{1,0:T(8,128)(2,1)S(1)}, u32[]{:S(2)}, u32[]{:S(2)}) collective-permute-start(bf16[128,3328]{1,0:T(8,128)(2,1)S(1)} %add_first.1), channel_id=1, source_target_pairs={{0,32},{1,33},{2,34},{3,35},{4,36},{5,37},{6,38},{7,39},{8,40},{9,... | collective-permute-start | bytes 2555912 | tf_op jit(solution)/shard_map/ppermute | solution.py:34
  28.0 2.0 %product.4 = (bf16[128,3328]{1,0:T(8,128)(2,1)S(1)}, bf16[128,3328]{1,0:T(8,128)(2,1)S(1)}) custom-call(bf16[256,1024]{1,0:T(8,128)(2,1)S(1)} %get-tuple-element.71.refs_0_.refs_6_, bf16[3328,1024]{1,0:T(8,128)(2,1)S(1)} %get-tuple-element.65.refs_1_.refs_3_), custom_call_target="tpu_custom_call" | custom-call | flops 1 | bytes 1 | tf_op jit(solution)/shard_map/product/pallas_call | solution.py:193
  30.0 1.4 %collective-permute-start.9 = (bf16[128,3328]{1,0:T(8,128)(2,1)S(1)}, bf16[128,3328]{1,0:T(8,128)(2,1)S(1)}, u32[]{:S(2)}, u32[]{:S(2)}) collective-permute-start(bf16[128,3328]{1,0:T(8,128)(2,1)S(1)} %get-tuple-element.78), channel_id=1, source_target_pairs={{1,17},{2,18},{3,19},{4,20},{5,21},{6,22},{7,23},{8,24},{9,25},{10... | collective-permute-start | bytes 2555912 | tf_op jit(solution)/shard_map/ppermute | solution.py:34
  31.4 0.3 mix.4.value_ref
  31.7 0.5 collective-permute-done.5.refs_0_.refs_7_
  32.2 0.4 collective-permute-start.8
  32.8 3.3 %collective-permute-start.16 = (bf16[128,3328]{1,0:T(8,128)(2,1)S(1)}, bf16[128,3328]{1,0:T(8,128)(2,1)S(1)}, u32[]{:S(2)}, u32[]{:S(2)}) collective-permute-start(bf16[128,3328]{1,0:T(8,128)(2,1)S(1)} %mix.4.value_ref), channel_id=1, source_target_pairs={{0,2},{1,3},{2,0},{3,1},{4,6},{5,7},{6,4},{7,5},{8,10},{9,11},{10,... | collective-permute-start | bytes 2555912 | tf_op jit(solution)/shard_map/ppermute | solution.py:34
  36.0 3.7 %product.5 = (bf16[64,3328]{1,0:T(8,128)(2,1)S(1)}, bf16[64,3328]{1,0:T(8,128)(2,1)S(1)}, bf16[64,3328]{1,0:T(8,128)(2,1)S(1)}, bf16[64,3328]{1,0:T(8,128)(2,1)S...) custom-call(bf16[512,1024]{1,0:T(8,128)(2,1)S(1)} %collective-permute-done.5.refs_0_., ...), custom_call_target="tpu_custom_call" | custom-call | flops 1 | bytes 1 | tf_op jit(solution)/shard_map/product/pallas_call | solution.py:193
  39.8 0.7 collective-permute-start.11
  40.6 0.7 collective-permute-done.10.refs_0_
  41.3 0.3 collective-permute-start.13
  42.0 0.5 collective-permute-done.12.refs_4_
  42.5 0.3 add_third.1
  42.8 0.3 collective-permute-done.13.refs_1_
  43.1 0.6 collective-permute-done.14.refs_2_
  43.9 1.5 %collective-permute-start.15 = (bf16[128,3328]{1,0:T(8,128)(2,1)S(1)}, bf16[128,3328]{1,0:T(8,128)(2,1)S(1)}, u32[]{:S(2)}, u32[]{:S(2)}) collective-permute-start(bf16[128,3328]{1,0:T(8,128)(2,1)S(1)} %add_second.1), channel_id=1, source_target_pairs={{0,48},{1,49},{2,50},{3,51},{4,52},{5,53},{6,54},{7,55},{8,56},{9,... | collective-permute-start | bytes 2555912 | tf_op jit(solution)/shard_map/ppermute | solution.py:34
  45.4 1.4 %collective-permute-start.19 = (bf16[128,3328]{1,0:T(8,128)(2,1)S(1)}, bf16[128,3328]{1,0:T(8,128)(2,1)S(1)}, u32[]{:S(2)}, u32[]{:S(2)}) collective-permute-start(bf16[128,3328]{1,0:T(8,128)(2,1)S(1)} %add_third.1), channel_id=1, source_target_pairs={{0,32},{1,33},{2,34},{3,35},{4,36},{5,37},{6,38},{7,39},{8,40},{9,... | collective-permute-start | bytes 2555912 | tf_op jit(solution)/shard_map/ppermute | solution.py:34
  47.2 4.0 %collective-permute-start.17 = (bf16[64,3328]{1,0:T(8,128)(2,1)S(1)}, bf16[64,3328]{1,0:T(8,128)(2,1)S(1)}, u32[]{:S(2)}, u32[]{:S(2)}) collective-permute-start(bf16[64,3328]{1,0:T(8,128)(2,1)S(1)} %get-tuple-element.88.refs_0_), channel_id=1, source_target_pairs={{0,8},{1,9},{2,10},{3,11},{4,12},{5,13},{6,14},{7,15},{8,0},{9,1},... | collective-permute-start | bytes 1277960 | tf_op jit(solution)/shard_map/ppermute | solution.py:34
  51.4 6.0 %collective-permute-done.17.refs_2_ = bf16[64,3328]{1,0:T(8,128)(2,1)S(1)} collective-permute-done((bf16[64,3328]{1,0:T(8,128)(2,1)S(1)}, bf16[64,3328]{1,0:T(8,128)(2,1)S(1)}, u32[]{:S(2)}, u32[]{:S(2)}) %collective-permute-start.17) | collective-permute-done | bytes 426016 | tf_op jit(solution)/shard_map/ppermute | solution.py:34
  57.4 4.6 %collective-permute-done.18.refs_3_ = bf16[64,3328]{1,0:T(8,128)(2,1)S(1)} collective-permute-done((bf16[64,3328]{1,0:T(8,128)(2,1)S(1)}, bf16[64,3328]{1,0:T(8,128)(2,1)S(1)}, u32[]{:S(2)}, u32[]{:S(2)}) %collective-permute-start.18) | collective-permute-done | bytes 426016 | tf_op jit(solution)/shard_map/ppermute | solution.py:34
  61.9 0.6 rotate.1.refs_0_
  62.6 2.2 %collective-permute-start.24 = (bf16[3328,128]{1,0:T(8,128)(2,1)S(1)}, bf16[3328,128]{1,0:T(8,128)(2,1)S(1)}, u32[]{:S(2)}, u32[]{:S(2)}) collective-permute-start(bf16[3328,128]{1,0:T(8,128)(2,1)S(1)} %rotate.1.refs_0_), channel_id=1, source_target_pairs={{0,96},{1,97},{2,98},{3,99},{4,100},{5,101},{6,102},{7,103},{8,104... | collective-permute-start | bytes 2555912 | tf_op jit(solution)/shard_map/ppermute | solution.py:34
  64.8 3.6 %collective-permute-done.19.refs_2_ = bf16[128,3328]{1,0:T(8,128)(2,1)S(1)} collective-permute-done((bf16[128,3328]{1,0:T(8,128)(2,1)S(1)}, bf16[128,3328]{1,0:T(8,128)(2,1)S(1)}, u32[]{:S(2)}, u32[]{:S(2)}) %collective-permute-start.19) | collective-permute-done | bytes 852000 | tf_op jit(solution)/shard_map/ppermute | solution.py:34
  68.4 0.3 deal_grad.1
  68.7 3.3 %collective-permute-start.20 = (bf16[32,3328]{1,0:T(8,128)(2,1)S(1)}, bf16[32,3328]{1,0:T(8,128)(2,1)S(1)}, u32[]{:S(2)}, u32[]{:S(2)}) collective-permute-start(bf16[32,3328]{1,0:T(8,128)(2,1)S(1)} %get-tuple-element.94), channel_id=1, source_target_pairs={{0,2},{1,3},{2,0},{3,1},{4,6},{5,7},{6,4},{7,5},{8,10},{9,11},{10,... | collective-permute-start | bytes 638984 | tf_op jit(solution)/shard_map/ppermute | solution.py:34
  72.0 0.7 collective-permute-start.21
  72.7 2.6 %collective-permute-start.22 = (bf16[32,3328]{1,0:T(8,128)(2,1)S(1)}, bf16[32,3328]{1,0:T(8,128)(2,1)S(1)}, u32[]{:S(2)}, u32[]{:S(2)}) collective-permute-start(bf16[32,3328]{1,0:T(8,128)(2,1)S(1)} %get-tuple-element.96), channel_id=1, source_target_pairs={{0,3},{1,0},{2,1},{3,2},{4,7},{5,4},{6,5},{7,6},{8,11},{9,8},{10,9... | collective-permute-start | bytes 638984 | tf_op jit(solution)/shard_map/ppermute | solution.py:34
  75.2 0.9 collective-permute-done.20.refs_1_
  76.1 2.9 %collective-permute-done.21.refs_2_ = bf16[32,3328]{1,0:T(8,128)(2,1)S(1)} collective-permute-done((bf16[32,3328]{1,0:T(8,128)(2,1)S(1)}, bf16[32,3328]{1,0:T(8,128)(2,1)S(1)}, u32[]{:S(2)}, u32[]{:S(2)}) %collective-permute-start.21) | collective-permute-done | bytes 213024 | tf_op jit(solution)/shard_map/ppermute | solution.py:34
  79.0 0.7 mix_quarters.2
  79.7 1.9 %collective-permute-start.25 = (bf16[32,3328]{1,0:T(8,128)(2,1)S(1)}, bf16[32,3328]{1,0:T(8,128)(2,1)S(1)}, u32[]{:S(2)}, u32[]{:S(2)}) collective-permute-start(bf16[32,3328]{1,0:T(8,128)(2,1)S(1)} %get-tuple-element.99), channel_id=1, source_target_pairs={{0,2},{1,3},{2,0},{3,1},{4,6},{5,7},{6,4},{7,5},{8,10},{9,11},{10,... | collective-permute-start | bytes 638984 | tf_op jit(solution)/shard_map/ppermute | solution.py:34
  81.6 2.3 %collective-permute-start.26 = (bf16[32,3328]{1,0:T(8,128)(2,1)S(1)}, bf16[32,3328]{1,0:T(8,128)(2,1)S(1)}, u32[]{:S(2)}, u32[]{:S(2)}) collective-permute-start(bf16[32,3328]{1,0:T(8,128)(2,1)S(1)} %get-tuple-element.100), channel_id=1, source_target_pairs={{0,1},{1,2},{2,3},{3,0},{4,5},{5,6},{6,7},{7,4},{8,9},{9,10},{10,1... | collective-permute-start | bytes 638984 | tf_op jit(solution)/shard_map/ppermute | solution.py:34
  83.9 0.9 collective-permute-start.27
  84.8 0.5 collective-permute-done.23.refs_2_
  85.3 1.9 %collective-permute-done.25.refs_1_ = bf16[32,3328]{1,0:T(8,128)(2,1)S(1)} collective-permute-done((bf16[32,3328]{1,0:T(8,128)(2,1)S(1)}, bf16[32,3328]{1,0:T(8,128)(2,1)S(1)}, u32[]{:S(2)}, u32[]{:S(2)}) %collective-permute-start.25) | collective-permute-done | bytes 213024 | tf_op jit(solution)/shard_map/ppermute | solution.py:34
  87.2 2.2 %collective-permute-done.26.refs_2_ = bf16[32,3328]{1,0:T(8,128)(2,1)S(1)} collective-permute-done((bf16[32,3328]{1,0:T(8,128)(2,1)S(1)}, bf16[32,3328]{1,0:T(8,128)(2,1)S(1)}, u32[]{:S(2)}, u32[]{:S(2)}) %collective-permute-start.26) | collective-permute-done | bytes 213024 | tf_op jit(solution)/shard_map/ppermute | solution.py:34
  89.4 0.6 collective-permute-done.27.refs_3_
  90.2 0.5 collective-permute-start.30
  90.7 0.8 collective-permute-start.34
  91.5 3.7 %collective-permute-start.31 = (bf16[32,3328]{1,0:T(8,128)(2,1)S(1)}, bf16[32,3328]{1,0:T(8,128)(2,1)S(1)}, u32[]{:S(2)}, u32[]{:S(2)}) collective-permute-start(bf16[32,3328]{1,0:T(8,128)(2,1)S(1)} %get-tuple-element.106), channel_id=1, source_target_pairs={{0,8},{1,9},{2,10},{3,11},{4,12},{5,13},{6,14},{7,15},{8,0},{9,1},... | collective-permute-start | bytes 638984 | tf_op jit(solution)/shard_map/ppermute | solution.py:34
  95.2 1.0 collective-permute-start.32
  96.2 2.2 %collective-permute-start.33 = (bf16[32,3328]{1,0:T(8,128)(2,1)S(1)}, bf16[32,3328]{1,0:T(8,128)(2,1)S(1)}, u32[]{:S(2)}, u32[]{:S(2)}) collective-permute-start(bf16[32,3328]{1,0:T(8,128)(2,1)S(1)} %get-tuple-element.108), channel_id=1, source_target_pairs={{0,12},{1,13},{2,14},{3,15},{4,0},{5,1},{6,2},{7,3},{8,4},{9,5},{1... | collective-permute-start | bytes 638984 | tf_op jit(solution)/shard_map/ppermute | solution.py:34
  98.4 5.5 %early_product.1.refs_4_ = f32[3328,1024]{1,0:T(8,128)S(1)} custom-call(bf16[3328,128]{1,0:T(8,128)(2,1)S(1)} %rotate.1.refs_0_, bf16[3328,128]{1,0:T(8,128)(2,1)S(1)} %collective-permute-done.28.refs_1_, bf16[3328,128]{1,0:T(8,128)(2,1)S(1)} %collective-permute-done.23.refs_2_, bf16[3328,128]{1,0:T(8,128)(2,1)S(1)} %collective-permute-done.29.refs_3_, ...), custom_call_target="tpu_custom_call" | custom-call | flops 1 | bytes 1 | tf_op jit(solution)/shard_map/early_product/pallas_call | solution.py:320
  103.9 0.7 mix_quarters.3
  104.7 3.5 %collective-permute-start.36 = (bf16[32,3328]{1,0:T(8,128)(2,1)S(1)}, bf16[32,3328]{1,0:T(8,128)(2,1)S(1)}, u32[]{:S(2)}, u32[]{:S(2)}) collective-permute-start(bf16[32,3328]{1,0:T(8,128)(2,1)S(1)} %get-tuple-element.113), channel_id=1, source_target_pairs={{0,8},{1,9},{2,10},{3,11},{4,12},{5,13},{6,14},{7,15},{8,0},{9,1},... | collective-permute-start | bytes 638984 | tf_op jit(solution)/shard_map/ppermute | solution.py:34
  108.2 1.0 collective-permute-start.37
  109.2 2.2 %collective-permute-start.38 = (bf16[32,3328]{1,0:T(8,128)(2,1)S(1)}, bf16[32,3328]{1,0:T(8,128)(2,1)S(1)}, u32[]{:S(2)}, u32[]{:S(2)}) collective-permute-start(bf16[32,3328]{1,0:T(8,128)(2,1)S(1)} %get-tuple-element.115), channel_id=1, source_target_pairs={{0,12},{1,13},{2,14},{3,15},{4,0},{5,1},{6,2},{7,3},{8,4},{9,5},{1... | collective-permute-start | bytes 638984 | tf_op jit(solution)/shard_map/ppermute | solution.py:34
  111.4 3.2 %late_product.1 = bf16[3328,1024]{1,0:T(8,128)(2,1)} custom-call(bf16[3328,128]{1,0:T(8,128)(2,1)S(1)} %collective-permute-done.34.refs_0_, bf16[3328,128]{1,0:T(8,128)(2,1)S(1)} %collective-permute-done.35.refs_1_, bf16[256,1024]{1,0:T(8,128)(2,1)S(1)} %collective-permute-done.1.refs_0_.refs_2_, bf16[3328,1024]{1,0:T(8,128)(2,1)S(1)} %get-tuple-element.111.refs_3_, ...), custom_call_target="tpu_custom_call" | custom-call | flops 1 | bytes 1 | tf_op jit(solution)/shard_map/late_product/pallas_call | solution.py:349
  114.7 0.6 collective-permute-done.37.refs_2_
  115.3 1.0 collect.3
  (41 shorter events, 2.5 us)
Async XLA Ops:
  0.6 16.9 %copy-start = (bf16[128,3328]{1,0:T(8,128)(2,1)S(1)}, bf16[128,3328]{1,0:T(8,128)(2,1)}, u32[]{:S(2)}) copy-start(bf16[128,3328]{1,0:T(8,128)(2,1)} %value_ref) | copy-start | bytes 2555908
  2.5 2.7 %collective-permute-start = (bf16[4,128,1024]{2,1,0:T(8,128)(2,1)S(1)}, bf16[4,128,1024]{2,1,0:T(8,128)(2,1)S(1)}, u32[]{:S(2)}, u32[]{:S(2)}) collective-permute-start(bf16[4,128,1024]{2,1,0:T(8,128)(2,1)S(1)} %get-tuple-element.61), channel_id=1, source_target_pairs={{0,16},{1,17},{2,18},{3,19},{4,20},{5,21},{6,22},{7,23},{8,24},{9,... | collective-permute-start | bytes 3145736 | tf_op jit(solution)/shard_map/ppermute | solution.py:34
  2.6 15.0 %collective-permute-start.2 = (bf16[128,3328]{1,0:T(8,128)(2,1)}, bf16[128,3328]{1,0:T(8,128)(2,1)S(1)}, u32[]{:S(2)}, u32[]{:S(2)}) collective-permute-start(bf16[128,3328]{1,0:T(8,128)(2,1)} %value_ref), channel_id=1, source_target_pairs={{0,1},{1,0},{2,3},{3,2},{4,5},{5,4},{6,7},{7,6},{8,9},{9,8},{10,11... | collective-permute-start | bytes 2555912 | tf_op jit(solution)/shard_map/ppermute | solution.py:34
  5.4 15.7 %collective-permute-start.1 = (bf16[256,1024]{1,0:T(8,128)(2,1)S(1)}, bf16[256,1024]{1,0:T(8,128)(2,1)S(1)}, u32[]{:S(2)}, u32[]{:S(2)}) collective-permute-start(bf16[256,1024]{1,0:T(8,128)(2,1)S(1)} %get-tuple-element.63), channel_id=1, source_target_pairs={{0,64},{1,65},{2,66},{3,67},{4,68},{5,69},{6,70},{7,71},{8,72},{9,... | collective-permute-start | bytes 1572872 | tf_op jit(solution)/shard_map/ppermute | solution.py:34
  8.5 23.6 %collective-permute-start.5 = (bf16[512,1024]{1,0:T(8,128)(2,1)S(1)}, bf16[512,1024]{1,0:T(8,128)(2,1)S(1)}, u32[]{:S(2)}, u32[]{:S(2)}) collective-permute-start(bf16[512,1024]{1,0:T(8,128)(2,1)S(1)} %get-tuple-element.73), channel_id=1, source_target_pairs={{0,32},{1,33},{2,34},{3,35},{4,36},{5,37},{6,38},{7,39},{8,40},{9,... | collective-permute-start | bytes 3145736 | tf_op jit(solution)/shard_map/ppermute | solution.py:34
  9.1 0.7 copy-start.1
  17.8 13.5 %collective-permute-start.6 = (bf16[128,3328]{1,0:T(8,128)(2,1)S(1)}, bf16[128,3328]{1,0:T(8,128)(2,1)S(1)}, u32[]{:S(2)}, u32[]{:S(2)}) collective-permute-start(bf16[128,3328]{1,0:T(8,128)(2,1)S(1)} %mix.3.value_ref), channel_id=1, source_target_pairs={{0,4},{1,5},{2,6},{3,7},{4,0},{5,1},{6,2},{7,3},{8,12},{9,13},{10,... | collective-permute-start | bytes 2555912 | tf_op jit(solution)/shard_map/ppermute | solution.py:34
  23.0 1.8 %collective-permute-start.3 = (bf16[64,3328]{1,0:T(8,128)(2,1)S(1)}, bf16[64,3328]{1,0:T(8,128)(2,1)S(1)}, u32[]{:S(2)}, u32[]{:S(2)}) collective-permute-start(bf16[64,3328]{1,0:T(8,128)(2,1)S(1)} %get-tuple-element.69), channel_id=1, source_target_pairs={{8,24},{9,25},{10,26},{11,27},{12,28},{13,29},{14,30},{15,31},{16,... | collective-permute-start | bytes 1277960 | tf_op jit(solution)/shard_map/ppermute | solution.py:34
  23.1 2.4 %collective-permute-start.4 = (bf16[64,3328]{1,0:T(8,128)(2,1)S(1)}, bf16[64,3328]{1,0:T(8,128)(2,1)S(1)}, u32[]{:S(2)}, u32[]{:S(2)}) collective-permute-start(bf16[64,3328]{1,0:T(8,128)(2,1)S(1)} %get-tuple-element.70), channel_id=1, source_target_pairs={{9,25},{10,26},{11,27},{12,28},{13,29},{14,30},{15,31},{16,0},{17,... | collective-permute-start | bytes 1277960 | tf_op jit(solution)/shard_map/ppermute | solution.py:34
  25.6 15.6 %collective-permute-start.10 = (bf16[128,3328]{1,0:T(8,128)(2,1)S(1)}, bf16[128,3328]{1,0:T(8,128)(2,1)S(1)}, u32[]{:S(2)}, u32[]{:S(2)}) collective-permute-start(bf16[128,3328]{1,0:T(8,128)(2,1)S(1)} %add_first.1), channel_id=1, source_target_pairs={{0,32},{1,33},{2,34},{3,35},{4,36},{5,37},{6,38},{7,39},{8,40},{9,... | collective-permute-start | bytes 2555912 | tf_op jit(solution)/shard_map/ppermute | solution.py:34
  30.0 11.6 %collective-permute-start.9 = (bf16[128,3328]{1,0:T(8,128)(2,1)S(1)}, bf16[128,3328]{1,0:T(8,128)(2,1)S(1)}, u32[]{:S(2)}, u32[]{:S(2)}) collective-permute-start(bf16[128,3328]{1,0:T(8,128)(2,1)S(1)} %get-tuple-element.78), channel_id=1, source_target_pairs={{1,17},{2,18},{3,19},{4,20},{5,21},{6,22},{7,23},{8,24},{9,25},{10... | collective-permute-start | bytes 2555912 | tf_op jit(solution)/shard_map/ppermute | solution.py:34
  32.2 3.9 %collective-permute-start.8 = (bf16[128,1024]{1,0:T(8,128)(2,1)S(1)}, bf16[128,1024]{1,0:T(8,128)(2,1)S(1)}, u32[]{:S(2)}, u32[]{:S(2)}) collective-permute-start(bf16[128,1024]{1,0:T(8,128)(2,1)S(1)} %get-tuple-element.116), channel_id=1, source_target_pairs={{3,19},{4,20},{5,21},{6,22},{7,23},{8,24},{9,25},{10,26},{11,27},{... | collective-permute-start | bytes 786440 | tf_op jit(solution)/shard_map/ppermute | solution.py:34
  32.6 3.5 %collective-permute-start.7 = (bf16[128,1024]{1,0:T(8,128)(2,1)S(1)}, bf16[128,1024]{1,0:T(8,128)(2,1)S(1)}, u32[]{:S(2)}, u32[]{:S(2)}) collective-permute-start(bf16[128,1024]{1,0:T(8,128)(2,1)S(1)} %get-tuple-element.117), channel_id=1, source_target_pairs={{2,18},{3,19},{4,20},{5,21},{6,22},{7,23},{8,24},{9,25},{10,26},{1... | collective-permute-start | bytes 786440 | tf_op jit(solution)/shard_map/ppermute | solution.py:34
  32.8 14.2 %collective-permute-start.16 = (bf16[128,3328]{1,0:T(8,128)(2,1)S(1)}, bf16[128,3328]{1,0:T(8,128)(2,1)S(1)}, u32[]{:S(2)}, u32[]{:S(2)}) collective-permute-start(bf16[128,3328]{1,0:T(8,128)(2,1)S(1)} %mix.4.value_ref), channel_id=1, source_target_pairs={{0,2},{1,3},{2,0},{3,1},{4,6},{5,7},{6,4},{7,5},{8,10},{9,11},{10,... | collective-permute-start | bytes 2555912 | tf_op jit(solution)/shard_map/ppermute | solution.py:34
  39.8 2.2 %collective-permute-start.11 = (bf16[64,3328]{1,0:T(8,128)(2,1)S(1)}, bf16[64,3328]{1,0:T(8,128)(2,1)S(1)}, u32[]{:S(2)}, u32[]{:S(2)}) collective-permute-start(bf16[64,3328]{1,0:T(8,128)(2,1)S(1)} %get-tuple-element.82), channel_id=1, source_target_pairs={{6,22},{7,23},{8,24},{9,25},{10,26},{11,27},{12,28},{13,29},{14,30... | collective-permute-start | bytes 1277960 | tf_op jit(solution)/shard_map/ppermute | solution.py:34
  40.5 2.0 %collective-permute-start.12 = (bf16[64,3328]{1,0:T(8,128)(2,1)S(1)}, bf16[64,3328]{1,0:T(8,128)(2,1)S(1)}, u32[]{:S(2)}, u32[]{:S(2)}) collective-permute-start(bf16[64,3328]{1,0:T(8,128)(2,1)S(1)} %get-tuple-element.83), channel_id=1, source_target_pairs={{7,23},{8,24},{9,25},{10,26},{11,27},{12,28},{13,29},{14,30},{15,3... | collective-permute-start | bytes 1277960 | tf_op jit(solution)/shard_map/ppermute | solution.py:34
  41.3 1.9 %collective-permute-start.13 = (bf16[64,3328]{1,0:T(8,128)(2,1)S(1)}, bf16[64,3328]{1,0:T(8,128)(2,1)S(1)}, u32[]{:S(2)}, u32[]{:S(2)}) collective-permute-start(bf16[64,3328]{1,0:T(8,128)(2,1)S(1)} %get-tuple-element.85), channel_id=1, source_target_pairs={{4,20},{5,21},{6,22},{7,23},{8,24},{9,25},{10,26},{11,27},{12,28},... | collective-permute-start | bytes 1277960 | tf_op jit(solution)/shard_map/ppermute | solution.py:34
  41.6 2.1 %collective-permute-start.14 = (bf16[64,3328]{1,0:T(8,128)(2,1)S(1)}, bf16[64,3328]{1,0:T(8,128)(2,1)S(1)}, u32[]{:S(2)}, u32[]{:S(2)}) collective-permute-start(bf16[64,3328]{1,0:T(8,128)(2,1)S(1)} %get-tuple-element.86), channel_id=1, source_target_pairs={{5,21},{6,22},{7,23},{8,24},{9,25},{10,26},{11,27},{12,28},{13,29}... | collective-permute-start | bytes 1277960 | tf_op jit(solution)/shard_map/ppermute | solution.py:34
  43.9 20.9 %collective-permute-start.15 = (bf16[128,3328]{1,0:T(8,128)(2,1)S(1)}, bf16[128,3328]{1,0:T(8,128)(2,1)S(1)}, u32[]{:S(2)}, u32[]{:S(2)}) collective-permute-start(bf16[128,3328]{1,0:T(8,128)(2,1)S(1)} %add_second.1), channel_id=1, source_target_pairs={{0,48},{1,49},{2,50},{3,51},{4,52},{5,53},{6,54},{7,55},{8,56},{9,... | collective-permute-start | bytes 2555912 | tf_op jit(solution)/shard_map/ppermute | solution.py:34
  45.4 23.0 %collective-permute-start.19 = (bf16[128,3328]{1,0:T(8,128)(2,1)S(1)}, bf16[128,3328]{1,0:T(8,128)(2,1)S(1)}, u32[]{:S(2)}, u32[]{:S(2)}) collective-permute-start(bf16[128,3328]{1,0:T(8,128)(2,1)S(1)} %add_third.1), channel_id=1, source_target_pairs={{0,32},{1,33},{2,34},{3,35},{4,36},{5,37},{6,38},{7,39},{8,40},{9,... | collective-permute-start | bytes 2555912 | tf_op jit(solution)/shard_map/ppermute | solution.py:34
  47.2 10.1 %collective-permute-start.17 = (bf16[64,3328]{1,0:T(8,128)(2,1)S(1)}, bf16[64,3328]{1,0:T(8,128)(2,1)S(1)}, u32[]{:S(2)}, u32[]{:S(2)}) collective-permute-start(bf16[64,3328]{1,0:T(8,128)(2,1)S(1)} %get-tuple-element.88.refs_0_), channel_id=1, source_target_pairs={{0,8},{1,9},{2,10},{3,11},{4,12},{5,13},{6,14},{7,15},{8,0},{9,1},... | collective-permute-start | bytes 1277960 | tf_op jit(solution)/shard_map/ppermute | solution.py:34
  51.3 10.7 %collective-permute-start.18 = (bf16[64,3328]{1,0:T(8,128)(2,1)S(1)}, bf16[64,3328]{1,0:T(8,128)(2,1)S(1)}, u32[]{:S(2)}, u32[]{:S(2)}) collective-permute-start(bf16[64,3328]{1,0:T(8,128)(2,1)S(1)} %get-tuple-element.89.refs_1_), channel_id=1, source_target_pairs={{0,8},{1,9},{2,10},{3,11},{4,12},{5,13},{6,14},{7,15},{8,0},{9,1},... | collective-permute-start | bytes 1277960 | tf_op jit(solution)/shard_map/ppermute | solution.py:34
  62.6 22.2 %collective-permute-start.24 = (bf16[3328,128]{1,0:T(8,128)(2,1)S(1)}, bf16[3328,128]{1,0:T(8,128)(2,1)S(1)}, u32[]{:S(2)}, u32[]{:S(2)}) collective-permute-start(bf16[3328,128]{1,0:T(8,128)(2,1)S(1)} %rotate.1.refs_0_), channel_id=1, source_target_pairs={{0,96},{1,97},{2,98},{3,99},{4,100},{5,101},{6,102},{7,103},{8,104... | collective-permute-start | bytes 2555912 | tf_op jit(solution)/shard_map/ppermute | solution.py:34
  64.8 20.5 %collective-permute-start.23 = (bf16[3328,128]{1,0:T(8,128)(2,1)S(1)}, bf16[3328,128]{1,0:T(8,128)(2,1)S(1)}, u32[]{:S(2)}, u32[]{:S(2)}) collective-permute-start(bf16[3328,128]{1,0:T(8,128)(2,1)S(1)} %rotate.1.refs_0_), channel_id=1, source_target_pairs={{0,32},{1,33},{2,34},{3,35},{4,36},{5,37},{6,38},{7,39},{8,40},{9,... | collective-permute-start | bytes 2555912 | tf_op jit(solution)/shard_map/ppermute | solution.py:34
  68.7 7.4 %collective-permute-start.20 = (bf16[32,3328]{1,0:T(8,128)(2,1)S(1)}, bf16[32,3328]{1,0:T(8,128)(2,1)S(1)}, u32[]{:S(2)}, u32[]{:S(2)}) collective-permute-start(bf16[32,3328]{1,0:T(8,128)(2,1)S(1)} %get-tuple-element.94), channel_id=1, source_target_pairs={{0,2},{1,3},{2,0},{3,1},{4,6},{5,7},{6,4},{7,5},{8,10},{9,11},{10,... | collective-permute-start | bytes 638984 | tf_op jit(solution)/shard_map/ppermute | solution.py:34
  72.0 7.1 %collective-permute-start.21 = (bf16[32,3328]{1,0:T(8,128)(2,1)S(1)}, bf16[32,3328]{1,0:T(8,128)(2,1)S(1)}, u32[]{:S(2)}, u32[]{:S(2)}) collective-permute-start(bf16[32,3328]{1,0:T(8,128)(2,1)S(1)} %get-tuple-element.95), channel_id=1, source_target_pairs={{0,1},{1,2},{2,3},{3,0},{4,5},{5,6},{6,7},{7,4},{8,9},{9,10},{10,1... | collective-permute-start | bytes 638984 | tf_op jit(solution)/shard_map/ppermute | solution.py:34
  72.7 6.4 %collective-permute-start.22 = (bf16[32,3328]{1,0:T(8,128)(2,1)S(1)}, bf16[32,3328]{1,0:T(8,128)(2,1)S(1)}, u32[]{:S(2)}, u32[]{:S(2)}) collective-permute-start(bf16[32,3328]{1,0:T(8,128)(2,1)S(1)} %get-tuple-element.96), channel_id=1, source_target_pairs={{0,3},{1,0},{2,1},{3,2},{4,7},{5,4},{6,5},{7,6},{8,11},{9,8},{10,9... | collective-permute-start | bytes 638984 | tf_op jit(solution)/shard_map/ppermute | solution.py:34
  79.7 7.5 %collective-permute-start.25 = (bf16[32,3328]{1,0:T(8,128)(2,1)S(1)}, bf16[32,3328]{1,0:T(8,128)(2,1)S(1)}, u32[]{:S(2)}, u32[]{:S(2)}) collective-permute-start(bf16[32,3328]{1,0:T(8,128)(2,1)S(1)} %get-tuple-element.99), channel_id=1, source_target_pairs={{0,2},{1,3},{2,0},{3,1},{4,6},{5,7},{6,4},{7,5},{8,10},{9,11},{10,... | collective-permute-start | bytes 638984 | tf_op jit(solution)/shard_map/ppermute | solution.py:34
  81.6 7.8 %collective-permute-start.26 = (bf16[32,3328]{1,0:T(8,128)(2,1)S(1)}, bf16[32,3328]{1,0:T(8,128)(2,1)S(1)}, u32[]{:S(2)}, u32[]{:S(2)}) collective-permute-start(bf16[32,3328]{1,0:T(8,128)(2,1)S(1)} %get-tuple-element.100), channel_id=1, source_target_pairs={{0,1},{1,2},{2,3},{3,0},{4,5},{5,6},{6,7},{7,4},{8,9},{9,10},{10,1... | collective-permute-start | bytes 638984 | tf_op jit(solution)/shard_map/ppermute | solution.py:34
  83.9 6.1 %collective-permute-start.27 = (bf16[32,3328]{1,0:T(8,128)(2,1)S(1)}, bf16[32,3328]{1,0:T(8,128)(2,1)S(1)}, u32[]{:S(2)}, u32[]{:S(2)}) collective-permute-start(bf16[32,3328]{1,0:T(8,128)(2,1)S(1)} %get-tuple-element.101), channel_id=1, source_target_pairs={{0,3},{1,0},{2,1},{3,2},{4,7},{5,4},{6,5},{7,6},{8,11},{9,8},{10,9... | collective-permute-start | bytes 638984 | tf_op jit(solution)/shard_map/ppermute | solution.py:34
  84.8 10.4 %collective-permute-start.28 = (bf16[3328,128]{1,0:T(8,128)(2,1)S(1)}, bf16[3328,128]{1,0:T(8,128)(2,1)S(1)}, u32[]{:S(2)}, u32[]{:S(2)}) collective-permute-start(bf16[3328,128]{1,0:T(8,128)(2,1)S(1)} %rotate.1.refs_0_), channel_id=1, source_target_pairs={{11,27},{12,28},{13,29},{14,30},{15,31},{16,0},{17,1},{18,2},{19,3... | collective-permute-start | bytes 2555912 | tf_op jit(solution)/shard_map/ppermute | solution.py:34
  90.1 6.1 %collective-permute-start.29 = (bf16[3328,128]{1,0:T(8,128)(2,1)S(1)}, bf16[3328,128]{1,0:T(8,128)(2,1)S(1)}, u32[]{:S(2)}, u32[]{:S(2)}) collective-permute-start(bf16[3328,128]{1,0:T(8,128)(2,1)S(1)} %collective-permute-done.24.refs_5_), channel_id=1, source_target_pairs={{13,29},{14,30},{15,31},{16,0},{17,1},{18,2},{19,3},{20,4},{21,5},... | collective-permute-start | bytes 2555912 | tf_op jit(solution)/shard_map/ppermute | solution.py:34
  90.2 8.2 %collective-permute-start.30 = (bf16[3328,128]{1,0:T(8,128)(2,1)S(1)}, bf16[3328,128]{1,0:T(8,128)(2,1)S(1)}, u32[]{:S(2)}, u32[]{:S(2)}) collective-permute-start(bf16[3328,128]{1,0:T(8,128)(2,1)S(1)} %collective-permute-done.23.refs_2_), channel_id=1, source_target_pairs={{12,28},{13,29},{14,30},{15,31},{16,0},{17,1},{18,2},{19,3},{20,4}... | collective-permute-start | bytes 2555912 | tf_op jit(solution)/shard_map/ppermute | solution.py:34
  90.7 13.9 %collective-permute-start.34 = (bf16[3328,128]{1,0:T(8,128)(2,1)S(1)}, bf16[3328,128]{1,0:T(8,128)(2,1)S(1)}, u32[]{:S(2)}, u32[]{:S(2)}) collective-permute-start(bf16[3328,128]{1,0:T(8,128)(2,1)S(1)} %collective-permute-done.23.refs_2_), channel_id=1, source_target_pairs={{0,32},{1,33},{2,34},{3,35},{4,36},{5,37},{6,38},{7,39},{8,40},{9,... | collective-permute-start | bytes 2555912 | tf_op jit(solution)/shard_map/ppermute | solution.py:34
  91.5 12.4 %collective-permute-start.31 = (bf16[32,3328]{1,0:T(8,128)(2,1)S(1)}, bf16[32,3328]{1,0:T(8,128)(2,1)S(1)}, u32[]{:S(2)}, u32[]{:S(2)}) collective-permute-start(bf16[32,3328]{1,0:T(8,128)(2,1)S(1)} %get-tuple-element.106), channel_id=1, source_target_pairs={{0,8},{1,9},{2,10},{3,11},{4,12},{5,13},{6,14},{7,15},{8,0},{9,1},... | collective-permute-start | bytes 638984 | tf_op jit(solution)/shard_map/ppermute | solution.py:34
  95.2 8.7 %collective-permute-start.32 = (bf16[32,3328]{1,0:T(8,128)(2,1)S(1)}, bf16[32,3328]{1,0:T(8,128)(2,1)S(1)}, u32[]{:S(2)}, u32[]{:S(2)}) collective-permute-start(bf16[32,3328]{1,0:T(8,128)(2,1)S(1)} %get-tuple-element.107), channel_id=1, source_target_pairs={{0,4},{1,5},{2,6},{3,7},{4,8},{5,9},{6,10},{7,11},{8,12},{9,13},{1... | collective-permute-start | bytes 638984 | tf_op jit(solution)/shard_map/ppermute | solution.py:34
  96.2 7.7 %collective-permute-start.33 = (bf16[32,3328]{1,0:T(8,128)(2,1)S(1)}, bf16[32,3328]{1,0:T(8,128)(2,1)S(1)}, u32[]{:S(2)}, u32[]{:S(2)}) collective-permute-start(bf16[32,3328]{1,0:T(8,128)(2,1)S(1)} %get-tuple-element.108), channel_id=1, source_target_pairs={{0,12},{1,13},{2,14},{3,15},{4,0},{5,1},{6,2},{7,3},{8,4},{9,5},{1... | collective-permute-start | bytes 638984 | tf_op jit(solution)/shard_map/ppermute | solution.py:34
  104.6 6.8 %collective-permute-start.35 = (bf16[3328,128]{1,0:T(8,128)(2,1)S(1)}, bf16[3328,128]{1,0:T(8,128)(2,1)S(1)}, u32[]{:S(2)}, u32[]{:S(2)}) collective-permute-start(bf16[3328,128]{1,0:T(8,128)(2,1)S(1)} %collective-permute-done.34.refs_0_), channel_id=1, source_target_pairs={{14,30},{15,31},{16,0},{17,1},{18,2},{19,3},{20,4},{21,5},{22,6},{... | collective-permute-start | bytes 2555912 | tf_op jit(solution)/shard_map/ppermute | solution.py:34
  104.7 10.0 %collective-permute-start.36 = (bf16[32,3328]{1,0:T(8,128)(2,1)S(1)}, bf16[32,3328]{1,0:T(8,128)(2,1)S(1)}, u32[]{:S(2)}, u32[]{:S(2)}) collective-permute-start(bf16[32,3328]{1,0:T(8,128)(2,1)S(1)} %get-tuple-element.113), channel_id=1, source_target_pairs={{0,8},{1,9},{2,10},{3,11},{4,12},{5,13},{6,14},{7,15},{8,0},{9,1},... | collective-permute-start | bytes 638984 | tf_op jit(solution)/shard_map/ppermute | solution.py:34
  108.2 7.1 %collective-permute-start.37 = (bf16[32,3328]{1,0:T(8,128)(2,1)S(1)}, bf16[32,3328]{1,0:T(8,128)(2,1)S(1)}, u32[]{:S(2)}, u32[]{:S(2)}) collective-permute-start(bf16[32,3328]{1,0:T(8,128)(2,1)S(1)} %get-tuple-element.114), channel_id=1, source_target_pairs={{0,4},{1,5},{2,6},{3,7},{4,8},{5,9},{6,10},{7,11},{8,12},{9,13},{1... | collective-permute-start | bytes 638984 | tf_op jit(solution)/shard_map/ppermute | solution.py:34
  109.2 6.1 %collective-permute-start.38 = (bf16[32,3328]{1,0:T(8,128)(2,1)S(1)}, bf16[32,3328]{1,0:T(8,128)(2,1)S(1)}, u32[]{:S(2)}, u32[]{:S(2)}) collective-permute-start(bf16[32,3328]{1,0:T(8,128)(2,1)S(1)} %get-tuple-element.115), channel_id=1, source_target_pairs={{0,12},{1,13},{2,14},{3,15},{4,0},{5,1},{6,2},{7,3},{8,4},{9,5},{1... | collective-permute-start | bytes 638984 | tf_op jit(solution)/shard_map/ppermute | solution.py:34

commit v5 on v4

--- a/solution.py
+++ b/solution.py
@@ -404,16 +404,19 @@
 def mix_quarters_kernel(stage, *refs):
     values, outs = refs[:4], refs[4:]
     mine = place(stage)
-    for k, out in enumerate(outs):
-        signs = []
+    signs = []
+    for k in range(4):
+        row = []
         for m in BEHIND:
             both = jnp.bitwise_and(jnp.bitwise_and(mine + k, mine - m), 3)
             odd = jnp.bitwise_and(both + (both >> 1), 1)
-            signs.append((1 - 2 * odd).astype(F32))
-        for i in range(out.shape[1] // HB):
-            part = pl.ds(i * HB, HB)
-            total = sum(ref[:, part].astype(F32) * sign for ref, sign in zip(values, signs))
-            out[:, part] = total.astype(BF16)
+            row.append((1 - 2 * odd).astype(F32))
+        signs.append(row)
+    for i in range(outs[0].shape[1] // HB):
+        part = pl.ds(i * HB, HB)
+        blocks = [ref[:, part].astype(F32) for ref in values]
+        for out, row in zip(outs, signs):
+            out[:, part] = sum(block * sign for block, sign in zip(blocks, row)).astype(BF16)
 
 
 def mix_quarters(stage, values):

time: 116 us -> 116 us (level)
  transfers between devices with their start and end apart: 39 -> 39, of which waited for: 21 -> 22; matrix products, arithmetic and copies ran while one was open for 0% -> 0% of each run, Pallas kernels for 24% -> 24%
where the time goes in v5:
time: 116 us
  starting transfers between devices  53.1 us (46%)
  waiting for transfers between devices  30.7 us (26%)
  Pallas kernels  30.6 us (26%)
    ppermute x39, starting transfers between devices, move(): return lax.ppermute(value, AXES, pairs[turn:] + pairs[:turn])  53.1 us
    ppermute x39, waiting for transfers between devices, move(): return lax.ppermute(value, AXES, pairs[turn:] + pairs[:turn])  30.7 us
    pallas_call x1, Pallas kernels, quantize(): call(quantize_kernel, 'quantize', 14, [VMEM, ANY, VMEM], [VMEM] * 2, [plt...  7.73 us
    pallas_call x3, Pallas kernels, product(): call(functools.partial(product_kernel, takes), 'product', 10, [VMEM] * (l...  7.68 us
    pallas_call x1, Pallas kernels, early_product(): call(functools.partial(early_kernel, blocks), 'early_product', 10, [VMEM]...  5.46 us
    pallas_call x1, Pallas kernels, late_product(): call(functools.partial(late_kernel, blocks), 'late_product', 14, [VMEM] *...  3.24 us
  transfers between devices with their start and end apart: 39, of which 22 were waited for; matrix products, arithmetic and copies ran while one was open for 0% of the time, Pallas kernels for 24%

profile of v5, /device:TPU:0, one launch (start us, length us, event | category | flops | bytes accessed | tf_op | source)
XLA Modules:
  0.0 116.1 jit_solution(18100349238867694285)
XLA Ops:
  0.8 1.7 %split.1 = (bf16[4,128,1024]{2,1,0:T(8,128)(2,1)S(1)}, bf16[4,128,1024]{2,1,0:T(8,128)(2,1)S(1)}) custom-call(bf16[128,8192]{1,0:T(8,128)(2,1)} %grad_ref), custom_call_target="tpu_custom_call" | custom-call | flops 1 | bytes 1 | tf_op jit(solution)/shard_map/split/pallas_call | solution.py:106
  2.6 1.7 %collective-permute-start.2 = (bf16[128,3328]{1,0:T(8,128)(2,1)}, bf16[128,3328]{1,0:T(8,128)(2,1)S(1)}, u32[]{:S(2)}, u32[]{:S(2)}) collective-permute-start(bf16[128,3328]{1,0:T(8,128)(2,1)} %value_ref), channel_id=1, source_target_pairs={{0,1},{1,0},{2,3},{3,2},{4,5},{5,4},{6,7},{7,6},{8,9},{9,8},{10,11... | collective-permute-start | bytes 2555912 | tf_op jit(solution)/shard_map/ppermute | solution.py:34
  4.3 0.9 collective-permute-done.got_ref
  5.4 3.2 %collective-permute-start.1 = (bf16[256,1024]{1,0:T(8,128)(2,1)S(1)}, bf16[256,1024]{1,0:T(8,128)(2,1)S(1)}, u32[]{:S(2)}, u32[]{:S(2)}) collective-permute-start(bf16[256,1024]{1,0:T(8,128)(2,1)S(1)} %get-tuple-element.63), channel_id=1, source_target_pairs={{0,64},{1,65},{2,66},{3,67},{4,68},{5,69},{6,70},{7,71},{8,72},{9,... | collective-permute-start | bytes 1572872 | tf_op jit(solution)/shard_map/ppermute | solution.py:34
  8.5 0.6 collective-permute-start.5
  9.1 0.7 copy-done.1
  9.8 7.7 %quantize.1 = (bf16[3328,1024]{1,0:T(8,128)(2,1)S(1)}, bf16[3328,1024]{1,0:T(8,128)(2,1)S(1)}) custom-call(bf16[256,256]{1,0:T(8,128)(2,1)S(1)} %fusion.3.table_ref, bf16[3328,1024]{1,0:T(8,128)(2,1)} %weight_ref, f32[1,1024]{1,0:T(1,128)S(1)} %bitcast.1), custom_call_target="tpu_custom_call" | custom-call | flops 1 | bytes 1 | tf_op jit(solution)/shard_map/quantize/pallas_call | solution.py:168
  17.6 0.3 mix.3.value_ref
  17.8 2.0 %collective-permute-start.6 = (bf16[128,3328]{1,0:T(8,128)(2,1)S(1)}, bf16[128,3328]{1,0:T(8,128)(2,1)S(1)}, u32[]{:S(2)}, u32[]{:S(2)}) collective-permute-start(bf16[128,3328]{1,0:T(8,128)(2,1)S(1)} %mix.3.value_ref), channel_id=1, source_target_pairs={{0,4},{1,5},{2,6},{3,7},{4,0},{5,1},{6,2},{7,3},{8,12},{9,13},{10,... | collective-permute-start | bytes 2555912 | tf_op jit(solution)/shard_map/ppermute | solution.py:34
  19.8 1.2 %collective-permute-done.1.refs_0_.refs_2_ = bf16[256,1024]{1,0:T(8,128)(2,1)S(1)} collective-permute-done((bf16[256,1024]{1,0:T(8,128)(2,1)S(1)}, bf16[256,1024]{1,0:T(8,128)(2,1)S(1)}, u32[]{:S(2)}, u32[]{:S(2)}) %collective-permute-start.1) | collective-permute-done | bytes 524320 | tf_op jit(solution)/shard_map/ppermute | solution.py:34
  21.0 2.0 %product.3 = (bf16[128,3328]{1,0:T(8,128)(2,1)S(1)}, bf16[64,3328]{1,0:T(8,128)(2,1)S(1)}, bf16[64,3328]{1,0:T(8,128)(2,1)S(1)}) custom-call(bf16[256,1024]{1,0:T(8,128)(2,1)S(1)} %collective-permute-done.1.refs_0_.refs_2_, bf16[3328,1024]{1,0:T(8,128)(2,1)S(1)} %get-tuple-element.65.refs_1_.refs_3_), custom_call_target="tpu_custom_call" | custom-call | flops 1 | bytes 1 | tf_op jit(solution)/shard_map/product/pallas_call | solution.py:193
  23.1 0.5 collective-permute-start.4
  23.6 1.3 %collective-permute-done.3.refs_1_ = bf16[64,3328]{1,0:T(8,128)(2,1)S(1)} collective-permute-done((bf16[64,3328]{1,0:T(8,128)(2,1)S(1)}, bf16[64,3328]{1,0:T(8,128)(2,1)S(1)}, u32[]{:S(2)}, u32[]{:S(2)}) %collective-permute-start.3) | collective-permute-done | bytes 426016 | tf_op jit(solution)/shard_map/ppermute | solution.py:34
  24.8 0.6 collective-permute-done.4.refs_2_
  25.6 2.4 %collective-permute-start.10 = (bf16[128,3328]{1,0:T(8,128)(2,1)S(1)}, bf16[128,3328]{1,0:T(8,128)(2,1)S(1)}, u32[]{:S(2)}, u32[]{:S(2)}) collective-permute-start(bf16[128,3328]{1,0:T(8,128)(2,1)S(1)} %add_first.1), channel_id=1, source_target_pairs={{0,32},{1,33},{2,34},{3,35},{4,36},{5,37},{6,38},{7,39},{8,40},{9,... | collective-permute-start | bytes 2555912 | tf_op jit(solution)/shard_map/ppermute | solution.py:34
  28.0 2.0 %product.4 = (bf16[128,3328]{1,0:T(8,128)(2,1)S(1)}, bf16[128,3328]{1,0:T(8,128)(2,1)S(1)}) custom-call(bf16[256,1024]{1,0:T(8,128)(2,1)S(1)} %get-tuple-element.71.refs_0_.refs_6_, bf16[3328,1024]{1,0:T(8,128)(2,1)S(1)} %get-tuple-element.65.refs_1_.refs_3_), custom_call_target="tpu_custom_call" | custom-call | flops 1 | bytes 1 | tf_op jit(solution)/shard_map/product/pallas_call | solution.py:193
  30.0 1.4 %collective-permute-start.9 = (bf16[128,3328]{1,0:T(8,128)(2,1)S(1)}, bf16[128,3328]{1,0:T(8,128)(2,1)S(1)}, u32[]{:S(2)}, u32[]{:S(2)}) collective-permute-start(bf16[128,3328]{1,0:T(8,128)(2,1)S(1)} %get-tuple-element.78), channel_id=1, source_target_pairs={{1,17},{2,18},{3,19},{4,20},{5,21},{6,22},{7,23},{8,24},{9,25},{10... | collective-permute-start | bytes 2555912 | tf_op jit(solution)/shard_map/ppermute | solution.py:34
  31.4 0.3 mix.4.value_ref
  31.7 0.5 collective-permute-done.5.refs_0_.refs_7_
  32.2 0.4 collective-permute-start.8
  32.8 3.3 %collective-permute-start.16 = (bf16[128,3328]{1,0:T(8,128)(2,1)S(1)}, bf16[128,3328]{1,0:T(8,128)(2,1)S(1)}, u32[]{:S(2)}, u32[]{:S(2)}) collective-permute-start(bf16[128,3328]{1,0:T(8,128)(2,1)S(1)} %mix.4.value_ref), channel_id=1, source_target_pairs={{0,2},{1,3},{2,0},{3,1},{4,6},{5,7},{6,4},{7,5},{8,10},{9,11},{10,... | collective-permute-start | bytes 2555912 | tf_op jit(solution)/shard_map/ppermute | solution.py:34
  36.0 3.7 %product.5 = (bf16[64,3328]{1,0:T(8,128)(2,1)S(1)}, bf16[64,3328]{1,0:T(8,128)(2,1)S(1)}, bf16[64,3328]{1,0:T(8,128)(2,1)S(1)}, bf16[64,3328]{1,0:T(8,128)(2,1)S...) custom-call(bf16[512,1024]{1,0:T(8,128)(2,1)S(1)} %collective-permute-done.5.refs_0_., ...), custom_call_target="tpu_custom_call" | custom-call | flops 1 | bytes 1 | tf_op jit(solution)/shard_map/product/pallas_call | solution.py:193
  39.8 0.7 collective-permute-start.11
  40.6 0.7 collective-permute-done.10.refs_0_
  41.3 0.3 collective-permute-start.13
  42.0 0.5 collective-permute-done.12.refs_4_
  42.5 0.3 add_third.1
  42.8 0.3 collective-permute-done.13.refs_1_
  43.1 0.6 collective-permute-done.14.refs_2_
  43.9 1.5 %collective-permute-start.15 = (bf16[128,3328]{1,0:T(8,128)(2,1)S(1)}, bf16[128,3328]{1,0:T(8,128)(2,1)S(1)}, u32[]{:S(2)}, u32[]{:S(2)}) collective-permute-start(bf16[128,3328]{1,0:T(8,128)(2,1)S(1)} %add_second.1), channel_id=1, source_target_pairs={{0,48},{1,49},{2,50},{3,51},{4,52},{5,53},{6,54},{7,55},{8,56},{9,... | collective-permute-start | bytes 2555912 | tf_op jit(solution)/shard_map/ppermute | solution.py:34
  45.4 1.4 %collective-permute-start.19 = (bf16[128,3328]{1,0:T(8,128)(2,1)S(1)}, bf16[128,3328]{1,0:T(8,128)(2,1)S(1)}, u32[]{:S(2)}, u32[]{:S(2)}) collective-permute-start(bf16[128,3328]{1,0:T(8,128)(2,1)S(1)} %add_third.1), channel_id=1, source_target_pairs={{0,32},{1,33},{2,34},{3,35},{4,36},{5,37},{6,38},{7,39},{8,40},{9,... | collective-permute-start | bytes 2555912 | tf_op jit(solution)/shard_map/ppermute | solution.py:34
  47.2 4.0 %collective-permute-start.17 = (bf16[64,3328]{1,0:T(8,128)(2,1)S(1)}, bf16[64,3328]{1,0:T(8,128)(2,1)S(1)}, u32[]{:S(2)}, u32[]{:S(2)}) collective-permute-start(bf16[64,3328]{1,0:T(8,128)(2,1)S(1)} %get-tuple-element.88.refs_0_), channel_id=1, source_target_pairs={{0,8},{1,9},{2,10},{3,11},{4,12},{5,13},{6,14},{7,15},{8,0},{9,1},... | collective-permute-start | bytes 1277960 | tf_op jit(solution)/shard_map/ppermute | solution.py:34
  51.4 6.0 %collective-permute-done.17.refs_2_ = bf16[64,3328]{1,0:T(8,128)(2,1)S(1)} collective-permute-done((bf16[64,3328]{1,0:T(8,128)(2,1)S(1)}, bf16[64,3328]{1,0:T(8,128)(2,1)S(1)}, u32[]{:S(2)}, u32[]{:S(2)}) %collective-permute-start.17) | collective-permute-done | bytes 426016 | tf_op jit(solution)/shard_map/ppermute | solution.py:34
  57.4 4.6 %collective-permute-done.18.refs_3_ = bf16[64,3328]{1,0:T(8,128)(2,1)S(1)} collective-permute-done((bf16[64,3328]{1,0:T(8,128)(2,1)S(1)}, bf16[64,3328]{1,0:T(8,128)(2,1)S(1)}, u32[]{:S(2)}, u32[]{:S(2)}) %collective-permute-start.18) | collective-permute-done | bytes 426016 | tf_op jit(solution)/shard_map/ppermute | solution.py:34
  61.9 0.6 rotate.1.refs_0_
  62.6 2.2 %collective-permute-start.24 = (bf16[3328,128]{1,0:T(8,128)(2,1)S(1)}, bf16[3328,128]{1,0:T(8,128)(2,1)S(1)}, u32[]{:S(2)}, u32[]{:S(2)}) collective-permute-start(bf16[3328,128]{1,0:T(8,128)(2,1)S(1)} %rotate.1.refs_0_), channel_id=1, source_target_pairs={{0,96},{1,97},{2,98},{3,99},{4,100},{5,101},{6,102},{7,103},{8,104... | collective-permute-start | bytes 2555912 | tf_op jit(solution)/shard_map/ppermute | solution.py:34
  64.8 3.6 %collective-permute-done.19.refs_2_ = bf16[128,3328]{1,0:T(8,128)(2,1)S(1)} collective-permute-done((bf16[128,3328]{1,0:T(8,128)(2,1)S(1)}, bf16[128,3328]{1,0:T(8,128)(2,1)S(1)}, u32[]{:S(2)}, u32[]{:S(2)}) %collective-permute-start.19) | collective-permute-done | bytes 852000 | tf_op jit(solution)/shard_map/ppermute | solution.py:34
  68.4 0.3 deal_grad.1
  68.7 3.3 %collective-permute-start.20 = (bf16[32,3328]{1,0:T(8,128)(2,1)S(1)}, bf16[32,3328]{1,0:T(8,128)(2,1)S(1)}, u32[]{:S(2)}, u32[]{:S(2)}) collective-permute-start(bf16[32,3328]{1,0:T(8,128)(2,1)S(1)} %get-tuple-element.94), channel_id=1, source_target_pairs={{0,2},{1,3},{2,0},{3,1},{4,6},{5,7},{6,4},{7,5},{8,10},{9,11},{10,... | collective-permute-start | bytes 638984 | tf_op jit(solution)/shard_map/ppermute | solution.py:34
  72.0 0.7 collective-permute-start.21
  72.7 2.6 %collective-permute-start.22 = (bf16[32,3328]{1,0:T(8,128)(2,1)S(1)}, bf16[32,3328]{1,0:T(8,128)(2,1)S(1)}, u32[]{:S(2)}, u32[]{:S(2)}) collective-permute-start(bf16[32,3328]{1,0:T(8,128)(2,1)S(1)} %get-tuple-element.96), channel_id=1, source_target_pairs={{0,3},{1,0},{2,1},{3,2},{4,7},{5,4},{6,5},{7,6},{8,11},{9,8},{10,9... | collective-permute-start | bytes 638984 | tf_op jit(solution)/shard_map/ppermute | solution.py:34
  75.2 0.9 collective-permute-done.20.refs_1_
  76.1 2.9 %collective-permute-done.21.refs_2_ = bf16[32,3328]{1,0:T(8,128)(2,1)S(1)} collective-permute-done((bf16[32,3328]{1,0:T(8,128)(2,1)S(1)}, bf16[32,3328]{1,0:T(8,128)(2,1)S(1)}, u32[]{:S(2)}, u32[]{:S(2)}) %collective-permute-start.21) | collective-permute-done | bytes 213024 | tf_op jit(solution)/shard_map/ppermute | solution.py:34
  79.0 0.5 mix_quarters.2
  79.5 1.9 %collective-permute-start.25 = (bf16[32,3328]{1,0:T(8,128)(2,1)S(1)}, bf16[32,3328]{1,0:T(8,128)(2,1)S(1)}, u32[]{:S(2)}, u32[]{:S(2)}) collective-permute-start(bf16[32,3328]{1,0:T(8,128)(2,1)S(1)} %get-tuple-element.99), channel_id=1, source_target_pairs={{0,2},{1,3},{2,0},{3,1},{4,6},{5,7},{6,4},{7,5},{8,10},{9,11},{10,... | collective-permute-start | bytes 638984 | tf_op jit(solution)/shard_map/ppermute | solution.py:34
  81.4 2.3 %collective-permute-start.26 = (bf16[32,3328]{1,0:T(8,128)(2,1)S(1)}, bf16[32,3328]{1,0:T(8,128)(2,1)S(1)}, u32[]{:S(2)}, u32[]{:S(2)}) collective-permute-start(bf16[32,3328]{1,0:T(8,128)(2,1)S(1)} %get-tuple-element.100), channel_id=1, source_target_pairs={{0,1},{1,2},{2,3},{3,0},{4,5},{5,6},{6,7},{7,4},{8,9},{9,10},{10,1... | collective-permute-start | bytes 638984 | tf_op jit(solution)/shard_map/ppermute | solution.py:34
  83.7 0.9 collective-permute-start.27
  84.6 0.6 collective-permute-done.23.refs_2_
  85.3 1.7 %collective-permute-done.25.refs_1_ = bf16[32,3328]{1,0:T(8,128)(2,1)S(1)} collective-permute-done((bf16[32,3328]{1,0:T(8,128)(2,1)S(1)}, bf16[32,3328]{1,0:T(8,128)(2,1)S(1)}, u32[]{:S(2)}, u32[]{:S(2)}) %collective-permute-start.25) | collective-permute-done | bytes 213024 | tf_op jit(solution)/shard_map/ppermute | solution.py:34
  87.0 2.2 %collective-permute-done.26.refs_2_ = bf16[32,3328]{1,0:T(8,128)(2,1)S(1)} collective-permute-done((bf16[32,3328]{1,0:T(8,128)(2,1)S(1)}, bf16[32,3328]{1,0:T(8,128)(2,1)S(1)}, u32[]{:S(2)}, u32[]{:S(2)}) %collective-permute-start.26) | collective-permute-done | bytes 213024 | tf_op jit(solution)/shard_map/ppermute | solution.py:34
  89.2 0.6 collective-permute-done.27.refs_3_
  90.0 0.5 collective-permute-start.30
  90.5 0.8 collective-permute-start.34
  91.3 3.7 %collective-permute-start.31 = (bf16[32,3328]{1,0:T(8,128)(2,1)S(1)}, bf16[32,3328]{1,0:T(8,128)(2,1)S(1)}, u32[]{:S(2)}, u32[]{:S(2)}) collective-permute-start(bf16[32,3328]{1,0:T(8,128)(2,1)S(1)} %get-tuple-element.106), channel_id=1, source_target_pairs={{0,8},{1,9},{2,10},{3,11},{4,12},{5,13},{6,14},{7,15},{8,0},{9,1},... | collective-permute-start | bytes 638984 | tf_op jit(solution)/shard_map/ppermute | solution.py:34
  95.0 1.0 collective-permute-start.32
  96.0 2.2 %collective-permute-start.33 = (bf16[32,3328]{1,0:T(8,128)(2,1)S(1)}, bf16[32,3328]{1,0:T(8,128)(2,1)S(1)}, u32[]{:S(2)}, u32[]{:S(2)}) collective-permute-start(bf16[32,3328]{1,0:T(8,128)(2,1)S(1)} %get-tuple-element.108), channel_id=1, source_target_pairs={{0,12},{1,13},{2,14},{3,15},{4,0},{5,1},{6,2},{7,3},{8,4},{9,5},{1... | collective-permute-start | bytes 638984 | tf_op jit(solution)/shard_map/ppermute | solution.py:34
  98.2 5.5 %early_product.1.refs_4_ = f32[3328,1024]{1,0:T(8,128)S(1)} custom-call(bf16[3328,128]{1,0:T(8,128)(2,1)S(1)} %rotate.1.refs_0_, bf16[3328,128]{1,0:T(8,128)(2,1)S(1)} %collective-permute-done.28.refs_1_, bf16[3328,128]{1,0:T(8,128)(2,1)S(1)} %collective-permute-done.23.refs_2_, bf16[3328,128]{1,0:T(8,128)(2,1)S(1)} %collective-permute-done.29.refs_3_, ...), custom_call_target="tpu_custom_call" | custom-call | flops 1 | bytes 1 | tf_op jit(solution)/shard_map/early_product/pallas_call | solution.py:320
  103.7 0.5 mix_quarters.3
  104.4 3.6 %collective-permute-start.36 = (bf16[32,3328]{1,0:T(8,128)(2,1)S(1)}, bf16[32,3328]{1,0:T(8,128)(2,1)S(1)}, u32[]{:S(2)}, u32[]{:S(2)}) collective-permute-start(bf16[32,3328]{1,0:T(8,128)(2,1)S(1)} %get-tuple-element.113), channel_id=1, source_target_pairs={{0,8},{1,9},{2,10},{3,11},{4,12},{5,13},{6,14},{7,15},{8,0},{9,1},... | collective-permute-start | bytes 638984 | tf_op jit(solution)/shard_map/ppermute | solution.py:34
  108.0 1.0 collective-permute-start.37
  109.0 2.2 %collective-permute-start.38 = (bf16[32,3328]{1,0:T(8,128)(2,1)S(1)}, bf16[32,3328]{1,0:T(8,128)(2,1)S(1)}, u32[]{:S(2)}, u32[]{:S(2)}) collective-permute-start(bf16[32,3328]{1,0:T(8,128)(2,1)S(1)} %get-tuple-element.115), channel_id=1, source_target_pairs={{0,12},{1,13},{2,14},{3,15},{4,0},{5,1},{6,2},{7,3},{8,4},{9,5},{1... | collective-permute-start | bytes 638984 | tf_op jit(solution)/shard_map/ppermute | solution.py:34
  111.3 3.2 %late_product.1 = bf16[3328,1024]{1,0:T(8,128)(2,1)} custom-call(bf16[3328,128]{1,0:T(8,128)(2,1)S(1)} %collective-permute-done.34.refs_0_, bf16[3328,128]{1,0:T(8,128)(2,1)S(1)} %collective-permute-done.35.refs_1_, bf16[256,1024]{1,0:T(8,128)(2,1)S(1)} %collective-permute-done.1.refs_0_.refs_2_, bf16[3328,1024]{1,0:T(8,128)(2,1)S(1)} %get-tuple-element.111.refs_3_, ...), custom_call_target="tpu_custom_call" | custom-call | flops 1 | bytes 1 | tf_op jit(solution)/shard_map/late_product/pallas_call | solution.py:349
  114.5 0.6 collective-permute-done.37.refs_2_
  115.1 1.0 collect.3
  (41 shorter events, 2.6 us)
Async XLA Ops:
  0.6 16.9 %copy-start = (bf16[128,3328]{1,0:T(8,128)(2,1)S(1)}, bf16[128,3328]{1,0:T(8,128)(2,1)}, u32[]{:S(2)}) copy-start(bf16[128,3328]{1,0:T(8,128)(2,1)} %value_ref) | copy-start | bytes 2555908
  2.5 2.7 %collective-permute-start = (bf16[4,128,1024]{2,1,0:T(8,128)(2,1)S(1)}, bf16[4,128,1024]{2,1,0:T(8,128)(2,1)S(1)}, u32[]{:S(2)}, u32[]{:S(2)}) collective-permute-start(bf16[4,128,1024]{2,1,0:T(8,128)(2,1)S(1)} %get-tuple-element.61), channel_id=1, source_target_pairs={{0,16},{1,17},{2,18},{3,19},{4,20},{5,21},{6,22},{7,23},{8,24},{9,... | collective-permute-start | bytes 3145736 | tf_op jit(solution)/shard_map/ppermute | solution.py:34
  2.6 15.0 %collective-permute-start.2 = (bf16[128,3328]{1,0:T(8,128)(2,1)}, bf16[128,3328]{1,0:T(8,128)(2,1)S(1)}, u32[]{:S(2)}, u32[]{:S(2)}) collective-permute-start(bf16[128,3328]{1,0:T(8,128)(2,1)} %value_ref), channel_id=1, source_target_pairs={{0,1},{1,0},{2,3},{3,2},{4,5},{5,4},{6,7},{7,6},{8,9},{9,8},{10,11... | collective-permute-start | bytes 2555912 | tf_op jit(solution)/shard_map/ppermute | solution.py:34
  5.4 15.7 %collective-permute-start.1 = (bf16[256,1024]{1,0:T(8,128)(2,1)S(1)}, bf16[256,1024]{1,0:T(8,128)(2,1)S(1)}, u32[]{:S(2)}, u32[]{:S(2)}) collective-permute-start(bf16[256,1024]{1,0:T(8,128)(2,1)S(1)} %get-tuple-element.63), channel_id=1, source_target_pairs={{0,64},{1,65},{2,66},{3,67},{4,68},{5,69},{6,70},{7,71},{8,72},{9,... | collective-permute-start | bytes 1572872 | tf_op jit(solution)/shard_map/ppermute | solution.py:34
  8.5 23.6 %collective-permute-start.5 = (bf16[512,1024]{1,0:T(8,128)(2,1)S(1)}, bf16[512,1024]{1,0:T(8,128)(2,1)S(1)}, u32[]{:S(2)}, u32[]{:S(2)}) collective-permute-start(bf16[512,1024]{1,0:T(8,128)(2,1)S(1)} %get-tuple-element.73), channel_id=1, source_target_pairs={{0,32},{1,33},{2,34},{3,35},{4,36},{5,37},{6,38},{7,39},{8,40},{9,... | collective-permute-start | bytes 3145736 | tf_op jit(solution)/shard_map/ppermute | solution.py:34
  9.1 0.7 copy-start.1
  17.8 13.5 %collective-permute-start.6 = (bf16[128,3328]{1,0:T(8,128)(2,1)S(1)}, bf16[128,3328]{1,0:T(8,128)(2,1)S(1)}, u32[]{:S(2)}, u32[]{:S(2)}) collective-permute-start(bf16[128,3328]{1,0:T(8,128)(2,1)S(1)} %mix.3.value_ref), channel_id=1, source_target_pairs={{0,4},{1,5},{2,6},{3,7},{4,0},{5,1},{6,2},{7,3},{8,12},{9,13},{10,... | collective-permute-start | bytes 2555912 | tf_op jit(solution)/shard_map/ppermute | solution.py:34
  23.0 1.8 %collective-permute-start.3 = (bf16[64,3328]{1,0:T(8,128)(2,1)S(1)}, bf16[64,3328]{1,0:T(8,128)(2,1)S(1)}, u32[]{:S(2)}, u32[]{:S(2)}) collective-permute-start(bf16[64,3328]{1,0:T(8,128)(2,1)S(1)} %get-tuple-element.69), channel_id=1, source_target_pairs={{8,24},{9,25},{10,26},{11,27},{12,28},{13,29},{14,30},{15,31},{16,... | collective-permute-start | bytes 1277960 | tf_op jit(solution)/shard_map/ppermute | solution.py:34
  23.1 2.4 %collective-permute-start.4 = (bf16[64,3328]{1,0:T(8,128)(2,1)S(1)}, bf16[64,3328]{1,0:T(8,128)(2,1)S(1)}, u32[]{:S(2)}, u32[]{:S(2)}) collective-permute-start(bf16[64,3328]{1,0:T(8,128)(2,1)S(1)} %get-tuple-element.70), channel_id=1, source_target_pairs={{9,25},{10,26},{11,27},{12,28},{13,29},{14,30},{15,31},{16,0},{17,... | collective-permute-start | bytes 1277960 | tf_op jit(solution)/shard_map/ppermute | solution.py:34
  25.6 15.6 %collective-permute-start.10 = (bf16[128,3328]{1,0:T(8,128)(2,1)S(1)}, bf16[128,3328]{1,0:T(8,128)(2,1)S(1)}, u32[]{:S(2)}, u32[]{:S(2)}) collective-permute-start(bf16[128,3328]{1,0:T(8,128)(2,1)S(1)} %add_first.1), channel_id=1, source_target_pairs={{0,32},{1,33},{2,34},{3,35},{4,36},{5,37},{6,38},{7,39},{8,40},{9,... | collective-permute-start | bytes 2555912 | tf_op jit(solution)/shard_map/ppermute | solution.py:34
  30.0 11.6 %collective-permute-start.9 = (bf16[128,3328]{1,0:T(8,128)(2,1)S(1)}, bf16[128,3328]{1,0:T(8,128)(2,1)S(1)}, u32[]{:S(2)}, u32[]{:S(2)}) collective-permute-start(bf16[128,3328]{1,0:T(8,128)(2,1)S(1)} %get-tuple-element.78), channel_id=1, source_target_pairs={{1,17},{2,18},{3,19},{4,20},{5,21},{6,22},{7,23},{8,24},{9,25},{10... | collective-permute-start | bytes 2555912 | tf_op jit(solution)/shard_map/ppermute | solution.py:34
  32.2 3.9 %collective-permute-start.8 = (bf16[128,1024]{1,0:T(8,128)(2,1)S(1)}, bf16[128,1024]{1,0:T(8,128)(2,1)S(1)}, u32[]{:S(2)}, u32[]{:S(2)}) collective-permute-start(bf16[128,1024]{1,0:T(8,128)(2,1)S(1)} %get-tuple-element.116), channel_id=1, source_target_pairs={{3,19},{4,20},{5,21},{6,22},{7,23},{8,24},{9,25},{10,26},{11,27},{... | collective-permute-start | bytes 786440 | tf_op jit(solution)/shard_map/ppermute | solution.py:34
  32.6 3.5 %collective-permute-start.7 = (bf16[128,1024]{1,0:T(8,128)(2,1)S(1)}, bf16[128,1024]{1,0:T(8,128)(2,1)S(1)}, u32[]{:S(2)}, u32[]{:S(2)}) collective-permute-start(bf16[128,1024]{1,0:T(8,128)(2,1)S(1)} %get-tuple-element.117), channel_id=1, source_target_pairs={{2,18},{3,19},{4,20},{5,21},{6,22},{7,23},{8,24},{9,25},{10,26},{1... | collective-permute-start | bytes 786440 | tf_op jit(solution)/shard_map/ppermute | solution.py:34
  32.8 14.2 %collective-permute-start.16 = (bf16[128,3328]{1,0:T(8,128)(2,1)S(1)}, bf16[128,3328]{1,0:T(8,128)(2,1)S(1)}, u32[]{:S(2)}, u32[]{:S(2)}) collective-permute-start(bf16[128,3328]{1,0:T(8,128)(2,1)S(1)} %mix.4.value_ref), channel_id=1, source_target_pairs={{0,2},{1,3},{2,0},{3,1},{4,6},{5,7},{6,4},{7,5},{8,10},{9,11},{10,... | collective-permute-start | bytes 2555912 | tf_op jit(solution)/shard_map/ppermute | solution.py:34
  39.8 2.2 %collective-permute-start.11 = (bf16[64,3328]{1,0:T(8,128)(2,1)S(1)}, bf16[64,3328]{1,0:T(8,128)(2,1)S(1)}, u32[]{:S(2)}, u32[]{:S(2)}) collective-permute-start(bf16[64,3328]{1,0:T(8,128)(2,1)S(1)} %get-tuple-element.82), channel_id=1, source_target_pairs={{6,22},{7,23},{8,24},{9,25},{10,26},{11,27},{12,28},{13,29},{14,30... | collective-permute-start | bytes 1277960 | tf_op jit(solution)/shard_map/ppermute | solution.py:34
  40.5 2.0 %collective-permute-start.12 = (bf16[64,3328]{1,0:T(8,128)(2,1)S(1)}, bf16[64,3328]{1,0:T(8,128)(2,1)S(1)}, u32[]{:S(2)}, u32[]{:S(2)}) collective-permute-start(bf16[64,3328]{1,0:T(8,128)(2,1)S(1)} %get-tuple-element.83), channel_id=1, source_target_pairs={{7,23},{8,24},{9,25},{10,26},{11,27},{12,28},{13,29},{14,30},{15,3... | collective-permute-start | bytes 1277960 | tf_op jit(solution)/shard_map/ppermute | solution.py:34
  41.3 1.9 %collective-permute-start.13 = (bf16[64,3328]{1,0:T(8,128)(2,1)S(1)}, bf16[64,3328]{1,0:T(8,128)(2,1)S(1)}, u32[]{:S(2)}, u32[]{:S(2)}) collective-permute-start(bf16[64,3328]{1,0:T(8,128)(2,1)S(1)} %get-tuple-element.85), channel_id=1, source_target_pairs={{4,20},{5,21},{6,22},{7,23},{8,24},{9,25},{10,26},{11,27},{12,28},... | collective-permute-start | bytes 1277960 | tf_op jit(solution)/shard_map/ppermute | solution.py:34
  41.6 2.1 %collective-permute-start.14 = (bf16[64,3328]{1,0:T(8,128)(2,1)S(1)}, bf16[64,3328]{1,0:T(8,128)(2,1)S(1)}, u32[]{:S(2)}, u32[]{:S(2)}) collective-permute-start(bf16[64,3328]{1,0:T(8,128)(2,1)S(1)} %get-tuple-element.86), channel_id=1, source_target_pairs={{5,21},{6,22},{7,23},{8,24},{9,25},{10,26},{11,27},{12,28},{13,29}... | collective-permute-start | bytes 1277960 | tf_op jit(solution)/shard_map/ppermute | solution.py:34
  43.9 20.9 %collective-permute-start.15 = (bf16[128,3328]{1,0:T(8,128)(2,1)S(1)}, bf16[128,3328]{1,0:T(8,128)(2,1)S(1)}, u32[]{:S(2)}, u32[]{:S(2)}) collective-permute-start(bf16[128,3328]{1,0:T(8,128)(2,1)S(1)} %add_second.1), channel_id=1, source_target_pairs={{0,48},{1,49},{2,50},{3,51},{4,52},{5,53},{6,54},{7,55},{8,56},{9,... | collective-permute-start | bytes 2555912 | tf_op jit(solution)/shard_map/ppermute | solution.py:34
  45.4 23.0 %collective-permute-start.19 = (bf16[128,3328]{1,0:T(8,128)(2,1)S(1)}, bf16[128,3328]{1,0:T(8,128)(2,1)S(1)}, u32[]{:S(2)}, u32[]{:S(2)}) collective-permute-start(bf16[128,3328]{1,0:T(8,128)(2,1)S(1)} %add_third.1), channel_id=1, source_target_pairs={{0,32},{1,33},{2,34},{3,35},{4,36},{5,37},{6,38},{7,39},{8,40},{9,... | collective-permute-start | bytes 2555912 | tf_op jit(solution)/shard_map/ppermute | solution.py:34
  47.2 10.1 %collective-permute-start.17 = (bf16[64,3328]{1,0:T(8,128)(2,1)S(1)}, bf16[64,3328]{1,0:T(8,128)(2,1)S(1)}, u32[]{:S(2)}, u32[]{:S(2)}) collective-permute-start(bf16[64,3328]{1,0:T(8,128)(2,1)S(1)} %get-tuple-element.88.refs_0_), channel_id=1, source_target_pairs={{0,8},{1,9},{2,10},{3,11},{4,12},{5,13},{6,14},{7,15},{8,0},{9,1},... | collective-permute-start | bytes 1277960 | tf_op jit(solution)/shard_map/ppermute | solution.py:34
  51.3 10.7 %collective-permute-start.18 = (bf16[64,3328]{1,0:T(8,128)(2,1)S(1)}, bf16[64,3328]{1,0:T(8,128)(2,1)S(1)}, u32[]{:S(2)}, u32[]{:S(2)}) collective-permute-start(bf16[64,3328]{1,0:T(8,128)(2,1)S(1)} %get-tuple-element.89.refs_1_), channel_id=1, source_target_pairs={{0,8},{1,9},{2,10},{3,11},{4,12},{5,13},{6,14},{7,15},{8,0},{9,1},... | collective-permute-start | bytes 1277960 | tf_op jit(solution)/shard_map/ppermute | solution.py:34
  62.6 22.0 %collective-permute-start.24 = (bf16[3328,128]{1,0:T(8,128)(2,1)S(1)}, bf16[3328,128]{1,0:T(8,128)(2,1)S(1)}, u32[]{:S(2)}, u32[]{:S(2)}) collective-permute-start(bf16[3328,128]{1,0:T(8,128)(2,1)S(1)} %rotate.1.refs_0_), channel_id=1, source_target_pairs={{0,96},{1,97},{2,98},{3,99},{4,100},{5,101},{6,102},{7,103},{8,104... | collective-permute-start | bytes 2555912 | tf_op jit(solution)/shard_map/ppermute | solution.py:34
  64.8 20.5 %collective-permute-start.23 = (bf16[3328,128]{1,0:T(8,128)(2,1)S(1)}, bf16[3328,128]{1,0:T(8,128)(2,1)S(1)}, u32[]{:S(2)}, u32[]{:S(2)}) collective-permute-start(bf16[3328,128]{1,0:T(8,128)(2,1)S(1)} %rotate.1.refs_0_), channel_id=1, source_target_pairs={{0,32},{1,33},{2,34},{3,35},{4,36},{5,37},{6,38},{7,39},{8,40},{9,... | collective-permute-start | bytes 2555912 | tf_op jit(solution)/shard_map/ppermute | solution.py:34
  68.7 7.4 %collective-permute-start.20 = (bf16[32,3328]{1,0:T(8,128)(2,1)S(1)}, bf16[32,3328]{1,0:T(8,128)(2,1)S(1)}, u32[]{:S(2)}, u32[]{:S(2)}) collective-permute-start(bf16[32,3328]{1,0:T(8,128)(2,1)S(1)} %get-tuple-element.94), channel_id=1, source_target_pairs={{0,2},{1,3},{2,0},{3,1},{4,6},{5,7},{6,4},{7,5},{8,10},{9,11},{10,... | collective-permute-start | bytes 638984 | tf_op jit(solution)/shard_map/ppermute | solution.py:34
  72.0 7.1 %collective-permute-start.21 = (bf16[32,3328]{1,0:T(8,128)(2,1)S(1)}, bf16[32,3328]{1,0:T(8,128)(2,1)S(1)}, u32[]{:S(2)}, u32[]{:S(2)}) collective-permute-start(bf16[32,3328]{1,0:T(8,128)(2,1)S(1)} %get-tuple-element.95), channel_id=1, source_target_pairs={{0,1},{1,2},{2,3},{3,0},{4,5},{5,6},{6,7},{7,4},{8,9},{9,10},{10,1... | collective-permute-start | bytes 638984 | tf_op jit(solution)/shard_map/ppermute | solution.py:34
  72.7 6.4 %collective-permute-start.22 = (bf16[32,3328]{1,0:T(8,128)(2,1)S(1)}, bf16[32,3328]{1,0:T(8,128)(2,1)S(1)}, u32[]{:S(2)}, u32[]{:S(2)}) collective-permute-start(bf16[32,3328]{1,0:T(8,128)(2,1)S(1)} %get-tuple-element.96), channel_id=1, source_target_pairs={{0,3},{1,0},{2,1},{3,2},{4,7},{5,4},{6,5},{7,6},{8,11},{9,8},{10,9... | collective-permute-start | bytes 638984 | tf_op jit(solution)/shard_map/ppermute | solution.py:34
  79.5 7.5 %collective-permute-start.25 = (bf16[32,3328]{1,0:T(8,128)(2,1)S(1)}, bf16[32,3328]{1,0:T(8,128)(2,1)S(1)}, u32[]{:S(2)}, u32[]{:S(2)}) collective-permute-start(bf16[32,3328]{1,0:T(8,128)(2,1)S(1)} %get-tuple-element.99), channel_id=1, source_target_pairs={{0,2},{1,3},{2,0},{3,1},{4,6},{5,7},{6,4},{7,5},{8,10},{9,11},{10,... | collective-permute-start | bytes 638984 | tf_op jit(solution)/shard_map/ppermute | solution.py:34
  81.4 7.8 %collective-permute-start.26 = (bf16[32,3328]{1,0:T(8,128)(2,1)S(1)}, bf16[32,3328]{1,0:T(8,128)(2,1)S(1)}, u32[]{:S(2)}, u32[]{:S(2)}) collective-permute-start(bf16[32,3328]{1,0:T(8,128)(2,1)S(1)} %get-tuple-element.100), channel_id=1, source_target_pairs={{0,1},{1,2},{2,3},{3,0},{4,5},{5,6},{6,7},{7,4},{8,9},{9,10},{10,1... | collective-permute-start | bytes 638984 | tf_op jit(solution)/shard_map/ppermute | solution.py:34
  83.7 6.1 %collective-permute-start.27 = (bf16[32,3328]{1,0:T(8,128)(2,1)S(1)}, bf16[32,3328]{1,0:T(8,128)(2,1)S(1)}, u32[]{:S(2)}, u32[]{:S(2)}) collective-permute-start(bf16[32,3328]{1,0:T(8,128)(2,1)S(1)} %get-tuple-element.101), channel_id=1, source_target_pairs={{0,3},{1,0},{2,1},{3,2},{4,7},{5,4},{6,5},{7,6},{8,11},{9,8},{10,9... | collective-permute-start | bytes 638984 | tf_op jit(solution)/shard_map/ppermute | solution.py:34
  84.6 10.4 %collective-permute-start.28 = (bf16[3328,128]{1,0:T(8,128)(2,1)S(1)}, bf16[3328,128]{1,0:T(8,128)(2,1)S(1)}, u32[]{:S(2)}, u32[]{:S(2)}) collective-permute-start(bf16[3328,128]{1,0:T(8,128)(2,1)S(1)} %rotate.1.refs_0_), channel_id=1, source_target_pairs={{11,27},{12,28},{13,29},{14,30},{15,31},{16,0},{17,1},{18,2},{19,3... | collective-permute-start | bytes 2555912 | tf_op jit(solution)/shard_map/ppermute | solution.py:34
  89.9 6.1 %collective-permute-start.29 = (bf16[3328,128]{1,0:T(8,128)(2,1)S(1)}, bf16[3328,128]{1,0:T(8,128)(2,1)S(1)}, u32[]{:S(2)}, u32[]{:S(2)}) collective-permute-start(bf16[3328,128]{1,0:T(8,128)(2,1)S(1)} %collective-permute-done.24.refs_5_), channel_id=1, source_target_pairs={{13,29},{14,30},{15,31},{16,0},{17,1},{18,2},{19,3},{20,4},{21,5},... | collective-permute-start | bytes 2555912 | tf_op jit(solution)/shard_map/ppermute | solution.py:34
  90.0 8.2 %collective-permute-start.30 = (bf16[3328,128]{1,0:T(8,128)(2,1)S(1)}, bf16[3328,128]{1,0:T(8,128)(2,1)S(1)}, u32[]{:S(2)}, u32[]{:S(2)}) collective-permute-start(bf16[3328,128]{1,0:T(8,128)(2,1)S(1)} %collective-permute-done.23.refs_2_), channel_id=1, source_target_pairs={{12,28},{13,29},{14,30},{15,31},{16,0},{17,1},{18,2},{19,3},{20,4}... | collective-permute-start | bytes 2555912 | tf_op jit(solution)/shard_map/ppermute | solution.py:34
  90.5 13.9 %collective-permute-start.34 = (bf16[3328,128]{1,0:T(8,128)(2,1)S(1)}, bf16[3328,128]{1,0:T(8,128)(2,1)S(1)}, u32[]{:S(2)}, u32[]{:S(2)}) collective-permute-start(bf16[3328,128]{1,0:T(8,128)(2,1)S(1)} %collective-permute-done.23.refs_2_), channel_id=1, source_target_pairs={{0,32},{1,33},{2,34},{3,35},{4,36},{5,37},{6,38},{7,39},{8,40},{9,... | collective-permute-start | bytes 2555912 | tf_op jit(solution)/shard_map/ppermute | solution.py:34
  91.3 12.4 %collective-permute-start.31 = (bf16[32,3328]{1,0:T(8,128)(2,1)S(1)}, bf16[32,3328]{1,0:T(8,128)(2,1)S(1)}, u32[]{:S(2)}, u32[]{:S(2)}) collective-permute-start(bf16[32,3328]{1,0:T(8,128)(2,1)S(1)} %get-tuple-element.106), channel_id=1, source_target_pairs={{0,8},{1,9},{2,10},{3,11},{4,12},{5,13},{6,14},{7,15},{8,0},{9,1},... | collective-permute-start | bytes 638984 | tf_op jit(solution)/shard_map/ppermute | solution.py:34
  95.0 8.7 %collective-permute-start.32 = (bf16[32,3328]{1,0:T(8,128)(2,1)S(1)}, bf16[32,3328]{1,0:T(8,128)(2,1)S(1)}, u32[]{:S(2)}, u32[]{:S(2)}) collective-permute-start(bf16[32,3328]{1,0:T(8,128)(2,1)S(1)} %get-tuple-element.107), channel_id=1, source_target_pairs={{0,4},{1,5},{2,6},{3,7},{4,8},{5,9},{6,10},{7,11},{8,12},{9,13},{1... | collective-permute-start | bytes 638984 | tf_op jit(solution)/shard_map/ppermute | solution.py:34
  96.0 7.7 %collective-permute-start.33 = (bf16[32,3328]{1,0:T(8,128)(2,1)S(1)}, bf16[32,3328]{1,0:T(8,128)(2,1)S(1)}, u32[]{:S(2)}, u32[]{:S(2)}) collective-permute-start(bf16[32,3328]{1,0:T(8,128)(2,1)S(1)} %get-tuple-element.108), channel_id=1, source_target_pairs={{0,12},{1,13},{2,14},{3,15},{4,0},{5,1},{6,2},{7,3},{8,4},{9,5},{1... | collective-permute-start | bytes 638984 | tf_op jit(solution)/shard_map/ppermute | solution.py:34
  104.4 6.8 %collective-permute-start.35 = (bf16[3328,128]{1,0:T(8,128)(2,1)S(1)}, bf16[3328,128]{1,0:T(8,128)(2,1)S(1)}, u32[]{:S(2)}, u32[]{:S(2)}) collective-permute-start(bf16[3328,128]{1,0:T(8,128)(2,1)S(1)} %collective-permute-done.34.refs_0_), channel_id=1, source_target_pairs={{14,30},{15,31},{16,0},{17,1},{18,2},{19,3},{20,4},{21,5},{22,6},{... | collective-permute-start | bytes 2555912 | tf_op jit(solution)/shard_map/ppermute | solution.py:34
  104.4 10.1 %collective-permute-start.36 = (bf16[32,3328]{1,0:T(8,128)(2,1)S(1)}, bf16[32,3328]{1,0:T(8,128)(2,1)S(1)}, u32[]{:S(2)}, u32[]{:S(2)}) collective-permute-start(bf16[32,3328]{1,0:T(8,128)(2,1)S(1)} %get-tuple-element.113), channel_id=1, source_target_pairs={{0,8},{1,9},{2,10},{3,11},{4,12},{5,13},{6,14},{7,15},{8,0},{9,1},... | collective-permute-start | bytes 638984 | tf_op jit(solution)/shard_map/ppermute | solution.py:34
  108.0 7.1 %collective-permute-start.37 = (bf16[32,3328]{1,0:T(8,128)(2,1)S(1)}, bf16[32,3328]{1,0:T(8,128)(2,1)S(1)}, u32[]{:S(2)}, u32[]{:S(2)}) collective-permute-start(bf16[32,3328]{1,0:T(8,128)(2,1)S(1)} %get-tuple-element.114), channel_id=1, source_target_pairs={{0,4},{1,5},{2,6},{3,7},{4,8},{5,9},{6,10},{7,11},{8,12},{9,13},{1... | collective-permute-start | bytes 638984 | tf_op jit(solution)/shard_map/ppermute | solution.py:34
  109.0 6.1 %collective-permute-start.38 = (bf16[32,3328]{1,0:T(8,128)(2,1)S(1)}, bf16[32,3328]{1,0:T(8,128)(2,1)S(1)}, u32[]{:S(2)}, u32[]{:S(2)}) collective-permute-start(bf16[32,3328]{1,0:T(8,128)(2,1)S(1)} %get-tuple-element.115), channel_id=1, source_target_pairs={{0,12},{1,13},{2,14},{3,15},{4,0},{5,1},{6,2},{7,3},{8,4},{9,5},{1... | collective-permute-start | bytes 638984 | tf_op jit(solution)/shard_map/ppermute | solution.py:34
